TPU v7x, 256 devices: a whole 4x4x8 slice. The times are simulated.
256 devices in a mesh: leaf: 64 (over y, z, core), bond: 4 (over x).
Axes of the slice: x: 4, y: 4, z: 8, core: 2. Of those that a mesh axis runs over, the one named last changes fastest.
Arguments:
- leaf_metric: float32 [4, 256, 1024], P('bond', 'leaf'), may hold values from -257 to 257, as said below
- local_iso: float32 [192, 32, 1024], P('leaf', 'bond'), may hold values from -6 to 6
- top_iso: float32 [64, 32, 1024], P('leaf', 'bond'), may hold values from -6 to 6
Outputs:
- leaf_rho: float32 [4, 256, 1024], P('bond', 'leaf')
- inner_rho: float32 [4, 192, 1024], P('bond', 'leaf')
- top_rho: float32 [4, 64, 1024], P('bond', 'leaf')
Inputs may be any that keep to these rules, and one draw needn't show every extreme that they name: Each entry of leaf_metric, taken as a 32 x 32 matrix, is symmetric positive definite.
All inputs are finite; a program needn't handle non-finite values.
Results may differ from a plain program's by a relative error of at most 0.0003.
Values sent between devices are 32-bit elements; how exact they have to be, the bound alone decides.
No kernel may reach another device: no remote copies, remote signals or barrier semaphores. Data moves between devices by JAX's collectives and lax.ppermute only.
A program may use at most 64 MiB of HBM per device.

v0:
```python
import functools

import jax
import jax.numpy as jnp
from jax import lax
from jax.experimental import pallas as pl
from jax.experimental.pallas import tpu as pltpu
from jax.sharding import PartitionSpec as P

CHI = 32
LEAVES_DEV = 4
CHI2 = 1024
LANES = 128
CHUNKS = CHI2 // LANES
BF = jnp.bfloat16
F32 = jnp.float32


def lane_group(shape):
    return lax.broadcasted_iota(jnp.int32, shape, len(shape) - 1) // CHI


def halves(x):
    high = x.astype(BF).astype(F32)
    return high, x - high


def swap(chunks, first, second):
    for c in range(CHUNKS):
        first[c * CHI : (c + 1) * CHI, :] = chunks[c]
    group = lane_group((8, LANES))
    for c in range(CHUNKS):
        rows = [first[pl.ds(c * CHI + h, 8, stride=4), :] for h in range(4)]
        for g in range(4):
            moved = [pltpu.roll(rows[h], CHI * ((h - g) % 4), 1) if h != g else rows[h] for h in range(4)]
            low = jnp.where(group == 0, moved[0], moved[1])
            high = jnp.where(group == 2, moved[2], moved[3])
            second[(4 * c + g) * 8 : (4 * c + g) * 8 + 8, :] = jnp.where(group < 2, low, high)
    return [second[pl.ds(c, CHI, stride=8), :] for c in range(CHUNKS)]


def transposed(chunks):
    result = []
    for i in range(2):
        block = jnp.concatenate(chunks[4 * i : 4 * i + 4], axis=0).T
        result += [block[CHI * g : CHI * (g + 1)] for g in range(4)]
    return result


def swap_back(chunks, first, second):
    for c in range(CHUNKS):
        first[c * CHI : (c + 1) * CHI, :] = chunks[c]
    group = lane_group((8, LANES))
    for c in range(CHUNKS):
        rows = [first[pl.ds(c * CHI + h, 8, stride=4), :] for h in range(4)]
        for j in range(4):
            moved = [pltpu.roll(rows[h], CHI * ((h - j) % 4), 1) if h != j else rows[h] for h in range(4)]
            low = jnp.where(group == 0, moved[0], moved[1])
            high = jnp.where(group == 2, moved[2], moved[3])
            a = 16 * (c // 4) + 4 * j + c % 4
            second[a * 8 : a * 8 + 8, :] = jnp.where(group < 2, low, high)
    return [second[pl.ds(c, CHI, stride=8), :] for c in range(CHUNKS)]


def split_rows(chunks):
    pairs = [halves(c) for c in chunks]
    high = jnp.concatenate([p[0] for p in pairs], axis=1)
    low = jnp.concatenate([p[1] for p in pairs], axis=1)
    return jnp.concatenate([high, low], axis=0).astype(BF)


def split_lanes(chunks):
    high, low = halves(jnp.concatenate(chunks, axis=0))
    return jnp.concatenate([high, low], axis=1).astype(BF)


def left_multiply(matrix, split):
    high, low = halves(matrix)
    left = jnp.where(lane_group(matrix.shape) < 2, high, low).astype(BF)
    right = jnp.concatenate([split, split], axis=0)
    out = jnp.dot(left, right, preferred_element_type=F32)
    return [out[:, LANES * c : LANES * (c + 1)] for c in range(CHUNKS)]


def right_multiply(split, matrix):
    shape = (LANES, LANES)
    keep = lax.broadcasted_iota(jnp.int32, shape, 0) // CHI == lane_group(shape)
    blocks = [
        jnp.where(keep, jnp.concatenate([part] * 4, axis=0), 0.0).astype(BF) for part in halves(matrix)
    ]
    row = jnp.concatenate(blocks, axis=1)
    out = jnp.dot(split, jnp.concatenate([row, row], axis=0), preferred_element_type=F32)
    out = out[:, :LANES] + out[:, LANES:]
    return [out[CHI * c : CHI * (c + 1)] for c in range(CHUNKS)]


def contract(left, right):
    high, low = right[:CHI], right[CHI:]
    wide = jnp.concatenate([high] * 4 + [low] * 4, axis=0)
    out = lax.dot_general(left, wide, (((1,), (1,)), ((), ())), preferred_element_type=F32)
    out = out[:CHI] + out[CHI:]
    return out[:, :LANES] + out[:, LANES:]


def normalize(matrix):
    row = lax.broadcasted_iota(jnp.int32, matrix.shape, 0)
    lane = lax.broadcasted_iota(jnp.int32, matrix.shape, 1)
    diagonal = jnp.where(row == lane, matrix, 0.0)
    trace = jnp.sum(jnp.sum(diagonal, axis=1, keepdims=True), axis=0, keepdims=True)
    return matrix * (CHI / trace)


def grow(natural_split, moved_split, left_env, right_env, first, second):
    turned = swap(left_multiply(left_env, moved_split), first, second)
    both = right_multiply(split_lanes(turned), right_env)
    return normalize(contract(split_rows(both), natural_split))


def load_chunks(ref):
    return [ref[:, LANES * c : LANES * (c + 1)] for c in range(CHUNKS)]


def scratch_pair():
    return [pltpu.VMEM((CHUNKS * CHI, LANES), F32), pltpu.VMEM((CHUNKS * CHI, LANES), F32)]


def full_spec():
    return pl.BlockSpec(memory_space=pltpu.VMEM)


def scalar_spec():
    return pl.BlockSpec(memory_space=pltpu.SMEM)


def shape_of(*shape, dtype=F32):
    return jax.ShapeDtypeStruct(shape, dtype)


ENV = (CHI, LANES)
ROWS = (2 * CHI, CHI2)
WIDE = (CHUNKS * CHI, 2 * LANES)


def kernel_call(kernel, outs, in_specs, args, scratch, nanos):
    return pl.pallas_call(
        kernel,
        out_shape=outs,
        in_specs=in_specs,
        out_specs=[full_spec()] * len(outs),
        scratch_shapes=scratch,
        cost_estimate=pl.CostEstimate(flops=int(nanos * 1000), bytes_accessed=1024 * 256, transcendentals=0),
        compiler_params=pltpu.CompilerParams(vmem_limit_bytes=24 * 1024 * 1024),
    )(*args)


def prepare_kernel(upper_ref, iso_ref, natural_ref, moved_ref, own_ref, other_ref, first, second):
    natural = load_chunks(iso_ref)
    natural_ref[...] = split_rows(natural)
    moved_ref[...] = split_rows(swap(natural, first, second))
    by_left = swap_back(transposed(natural), first, second)
    by_right = swap(by_left, first, second)
    upper = upper_ref[0] == 1
    own = [jnp.where(upper, r, l) for l, r in zip(by_left, by_right)]
    other = [jnp.where(upper, l, r) for l, r in zip(by_left, by_right)]
    own_ref[...] = split_lanes(own)
    other_ref[...] = split_rows(other)


def prepare(upper, iso):
    outs = [shape_of(*ROWS, dtype=BF), shape_of(*ROWS, dtype=BF), shape_of(*WIDE, dtype=BF), shape_of(*ROWS, dtype=BF)]
    return kernel_call(prepare_kernel, outs, [scalar_spec(), full_spec()], (upper, iso), scratch_pair(), 1000)


def grow_kernel(upper_ref, natural_ref, moved_ref, env_ref, sibling_ref, out_ref, first, second):
    upper = upper_ref[0] == 1
    env, sibling = env_ref[...], sibling_ref[...]
    left_env = jnp.where(upper, sibling, env)
    right_env = jnp.where(upper, env, sibling)
    out_ref[...] = grow(natural_ref[...], moved_ref[...], left_env, right_env, first, second)


def grow_level(upper, natural, moved, env, sibling):
    specs = [scalar_spec()] + [full_spec()] * 4
    return kernel_call(
        grow_kernel, [shape_of(*ENV)], specs, (upper, natural, moved, env, sibling), scratch_pair(), 1000
    )[0]


def partner_kernel(other_ref, sibling_ref, out_ref, first, second):
    out_ref[...] = split_rows(swap(left_multiply(sibling_ref[...], other_ref[...]), first, second))


def partner_level(other, sibling):
    outs = [shape_of(*ROWS, dtype=BF)]
    return kernel_call(partner_kernel, outs, [full_spec()] * 2, (other, sibling), scratch_pair(), 500)[0]


def local_kernel(leaf_ref, iso_ref, env_ref, top_env_ref, first, second):
    envs = []
    for node in range(3):
        natural = load_chunks(iso_ref.at[node])
        natural_split = split_rows(natural)
        moved_split = split_rows(swap(natural, first, second))
        if node < 2:
            pair = leaf_ref[2 * node], leaf_ref[2 * node + 1]
        else:
            pair = envs
        env = grow(natural_split, moved_split, *pair, first, second)
        envs.append(env)
    env_ref[0] = envs[0]
    env_ref[1] = envs[1]
    top_env_ref[...] = envs[2]


def local_edges_kernel(leaf_ref, env_ref, iso_ref, own_ref, partner_ref, first, second):
    for node in range(3):
        by_left = swap_back(transposed(load_chunks(iso_ref.at[node])), first, second)
        by_right = swap(by_left, first, second)
        if node < 2:
            left_env, right_env = leaf_ref[2 * node], leaf_ref[2 * node + 1]
        else:
            left_env, right_env = env_ref[0], env_ref[1]
        own_ref[2 * node] = split_lanes(by_left)
        own_ref[2 * node + 1] = split_lanes(by_right)
        left_split, right_split = split_rows(by_left), split_rows(by_right)
        partner_ref[2 * node] = split_rows(swap(left_multiply(right_env, right_split), first, second))
        partner_ref[2 * node + 1] = split_rows(swap(left_multiply(left_env, left_split), first, second))


def flat(matrix, first):
    first[0:CHI, :] = matrix
    group = lane_group((8, LANES))
    rows = [first[pl.ds(h, 8, stride=4), :] for h in range(4)]
    return jnp.where(group < 2, jnp.where(group == 0, rows[0], rows[1]), jnp.where(group == 2, rows[2], rows[3]))


def write_flat(out_ref, index, flattened):
    for c in range(CHUNKS):
        out_ref[index : index + 1, LANES * c : LANES * (c + 1)] = flattened[c : c + 1, :]


def descend(own, partner, state):
    mixed = right_multiply(own, state)
    return normalize(contract(split_rows(mixed), partner))


def down_kernel(levels, marked_ref, root_ref, env_ref, *refs):
    own_refs, partner_refs = refs[:levels], refs[levels : 2 * levels]
    local_own, local_partner, leaf_out, inner_out, top_out, first = refs[2 * levels :]
    gram = split_rows(load_chunks(root_ref))
    state = normalize(contract(gram, gram))
    top = env_ref[...]
    for level in range(levels - 1, -1, -1):
        top = jnp.where(marked_ref[level] == 1, state, top)
        state = descend(own_refs[level][...], partner_refs[level][...], state)
    write_flat(top_out, 0, flat(top, first))
    states = [None, None, state]
    for node in (2, 1, 0):
        write_flat(inner_out, node, flat(states[node], first))
        for side in range(2):
            child = descend(local_own[2 * node + side], local_partner[2 * node + side], states[node])
            if node == 2:
                states[side] = child
            else:
                write_flat(leaf_out, 2 * node + side, flat(child, first))


def exchange(value, mask):
    pairs = [(source, source ^ mask) for source in range(lax.axis_size("leaf"))]
    return lax.ppermute(value, "leaf", pairs)


def gather_bond(value):
    size = lax.axis_size("bond")
    mine = lax.axis_index("bond")
    whole = jnp.zeros((size, *value.shape), value.dtype)
    whole = lax.dynamic_update_index_in_dim(whole, value, mine, 0)
    for mask in range(1, size):
        pairs = [(source, source ^ mask) for source in range(size)]
        whole = lax.dynamic_update_index_in_dim(whole, lax.ppermute(value, "bond", pairs), mine ^ mask, 0)
    return whole


def body(leaf_metric, local_iso, top_iso):
    devices = lax.axis_size("leaf")
    top_levels = devices.bit_length() - 1
    position = lax.axis_index("leaf")
    uppers = [(position >> level & 1).astype(jnp.int32).reshape(1) for level in range(top_levels)]
    leaves = jnp.tile(leaf_metric.reshape(LEAVES_DEV, CHI, CHI), (1, 1, 4))

    gathered = gather_bond(jnp.concatenate([local_iso, top_iso], axis=0))
    gathered = jnp.moveaxis(gathered, 0, 1).reshape(LEAVES_DEV, CHI, CHI2)
    local_whole, packed = gathered[: LEAVES_DEV - 1], gathered[LEAVES_DEV - 1]

    local_envs, env = kernel_call(
        local_kernel,
        [shape_of(2, *ENV), shape_of(*ENV)],
        [full_spec()] * 2,
        (leaves, local_whole),
        scratch_pair(),
        3000,
    )
    local_own, local_partner = kernel_call(
        local_edges_kernel,
        [shape_of(6, *WIDE, dtype=BF), shape_of(6, *ROWS, dtype=BF)],
        [full_spec()] * 3,
        (leaves, local_envs, local_whole),
        scratch_pair(),
        4000,
    )

    shares = []
    for height in range(1, top_levels + 1):
        start = CHI2 - (CHI2 >> height - 1)
        shares.append(packed[:, start : start + (CHI2 >> height)])
    shares.append(packed[:, CHI2 - (CHI2 >> top_levels) :])
    for level in range(top_levels):
        pending = shares[level:]
        incoming = exchange(jnp.concatenate(pending, axis=1), 1 << level)
        upper = uppers[level][0] == 1
        merged = []
        cursor = 0
        for mine in pending:
            breadth = mine.shape[1]
            theirs = incoming[:, cursor : cursor + breadth]
            cursor += breadth
            merged.append(
                jnp.where(
                    upper,
                    jnp.concatenate([theirs, mine], axis=1),
                    jnp.concatenate([mine, theirs], axis=1),
                )
            )
        shares = shares[:level] + merged

    masks = [1, 2, 4, 12, 16, 48]
    owns, partners = [], []
    for level in range(top_levels):
        natural, moved, own, other = prepare(uppers[level], shares[level])
        sibling = exchange(env, masks[level] if level < len(masks) else 1 << level)
        env = grow_level(uppers[level], natural, moved, env, sibling)
        owns.append(own)
        partners.append(partner_level(other, sibling))

    marked = jnp.stack(
        [((position + 1) % (2 << level) == 1 << level).astype(jnp.int32) for level in range(top_levels)]
    )
    leaf_rho, inner_rho, top_rho = kernel_call(
        functools.partial(down_kernel, top_levels),
        [shape_of(LEAVES_DEV, CHI2), shape_of(LEAVES_DEV - 1, CHI2), shape_of(1, CHI2)],
        [scalar_spec()] + [full_spec()] * (2 * top_levels + 4),
        (marked, shares[top_levels], env, *owns, *partners, local_own, local_partner),
        [pltpu.VMEM((CHI, LANES), F32)],
        8000,
    )
    return (leaf_rho[None], inner_rho[None], top_rho[None])


def solution(mesh):
    in_specs = (P("bond", "leaf", None), P("leaf", "bond", None), P("leaf", "bond", None))
    out_specs = (P("bond", "leaf", None), P("bond", "leaf", None), P("bond", "leaf", None))
    return jax.shard_map(body, mesh=mesh, in_specs=in_specs, out_specs=out_specs, check_vma=False)
```

profile of v0, /device:TPU:24, one launch (start us, length us, event | category | flops | bytes accessed | tf_op | source)
XLA Modules:
  0.0 79.7 jit_solution(5232371812724680275)
XLA Ops:
  0.6 0.9 %constant_dynamic-update-slice_fusion.1 = f32[4,8,1024]{2,1,0:T(8,128)S(1)} fusion(f32[3,8,1024]{2,1,0:T(8,128)} %param.4), kind=kLoop, calls=%fused_computation.44 | loop fusion | bytes 196608
  1.6 1.6 %collective-permute-start = (f32[4,8,1024]{2,1,0:T(8,128)S(1)}, f32[4,8,1024]{2,1,0:T(8,128)S(1)}, u32[]{:S(2)}, u32[]{:S(2)}) collective-permute-start(f32[4,8,1024]{2,1,0:T(8,128)S(1)} %constant_dynamic-update-slice_fusion), channel_id=1, source_target_pairs={{0,1},{1,0},{2,3},{3,2},{4,5},{5,4},{6,7},{7,6},{8,9},{9,8},{10,11... | collective-permute-start | bytes 393224 | tf_op jit(solution)/shard_map/ppermute | solution.py:280
  3.1 2.7 %collective-permute-start.1 = (f32[4,8,1024]{2,1,0:T(8,128)S(1)}, f32[4,8,1024]{2,1,0:T(8,128)S(1)}, u32[]{:S(2)}, u32[]{:S(2)}) collective-permute-start(f32[4,8,1024]{2,1,0:T(8,128)S(1)} %constant_dynamic-update-slice_fusion), channel_id=1, source_target_pairs={{0,2},{1,3},{2,0},{3,1},{4,6},{5,7},{6,4},{7,5},{8,10},{9,11},{10,... | collective-permute-start | bytes 393224 | tf_op jit(solution)/shard_map/ppermute | solution.py:280
  6.4 1.1 %collective-permute-done = f32[4,8,1024]{2,1,0:T(8,128)S(1)} collective-permute-done((f32[4,8,1024]{2,1,0:T(8,128)S(1)}, f32[4,8,1024]{2,1,0:T(8,128)S(1)}, u32[]{:S(2)}, u32[]{:S(2)}) %collective-permute-start) | collective-permute-done | bytes 131104 | tf_op jit(solution)/shard_map/ppermute | solution.py:280
  7.6 4.4 %collective-permute-done.1 = f32[4,8,1024]{2,1,0:T(8,128)S(1)} collective-permute-done((f32[4,8,1024]{2,1,0:T(8,128)S(1)}, f32[4,8,1024]{2,1,0:T(8,128)S(1)}, u32[]{:S(2)}, u32[]{:S(2)}) %collective-permute-start.1) | collective-permute-done | bytes 131104 | tf_op jit(solution)/shard_map/ppermute | solution.py:280
  12.0 2.0 %collective-permute-done.2 = f32[4,8,1024]{2,1,0:T(8,128)S(1)} collective-permute-done((f32[4,8,1024]{2,1,0:T(8,128)S(1)}, f32[4,8,1024]{2,1,0:T(8,128)S(1)}, u32[]{:S(2)}, u32[]{:S(2)}) %collective-permute-start.2) | collective-permute-done | bytes 131104 | tf_op jit(solution)/shard_map/ppermute | solution.py:280
  14.4 1.2 %collective-permute-done.3 = f32[32,1024]{1,0:T(8,128)S(1)} collective-permute-done((f32[32,1024]{1,0:T(8,128)S(1)}, f32[32,1024]{1,0:T(8,128)S(1)}, u32[]{:S(2)}, u32[]{:S(2)}) %collective-permute-start.3) | collective-permute-done | bytes 131104 | tf_op jit(solution)/shard_map/ppermute | solution.py:270
  16.1 1.9 %collective-permute-start.4 = (f32[32,1024]{1,0:T(8,128)S(1)}, f32[32,1024]{1,0:T(8,128)S(1)}, u32[]{:S(2)}, u32[]{:S(2)}) collective-permute-start(f32[32,1024]{1,0:T(8,128)S(1)} %concatenate.195), channel_id=1, source_target_pairs={{0,8},{4,12},{8,0},{12,4},{16,24},{20,28},{24,16},{28,20},{32,40},... | collective-permute-start | bytes 393224 | tf_op jit(solution)/shard_map/ppermute | solution.py:270
  18.0 3.8 %collective-permute-done.4 = f32[32,1024]{1,0:T(8,128)S(1)} collective-permute-done((f32[32,1024]{1,0:T(8,128)S(1)}, f32[32,1024]{1,0:T(8,128)S(1)}, u32[]{:S(2)}, u32[]{:S(2)}) %collective-permute-start.4) | collective-permute-done | bytes 131104 | tf_op jit(solution)/shard_map/ppermute | solution.py:270
  22.3 3.3 %collective-permute-start.5 = (f32[32,1024]{1,0:T(8,128)S(1)}, f32[32,1024]{1,0:T(8,128)S(1)}, u32[]{:S(2)}, u32[]{:S(2)}) collective-permute-start(f32[32,1024]{1,0:T(8,128)S(1)} %concatenate.206), channel_id=1, source_target_pairs={{0,16},{4,20},{8,24},{12,28},{16,0},{20,4},{24,8},{28,12},{32,48},... | collective-permute-start | bytes 393224 | tf_op jit(solution)/shard_map/ppermute | solution.py:270
  25.6 0.7 copy-done.3
  26.8 4.8 %collective-permute-done.5 = f32[32,1024]{1,0:T(8,128)S(1)} collective-permute-done((f32[32,1024]{1,0:T(8,128)S(1)}, f32[32,1024]{1,0:T(8,128)S(1)}, u32[]{:S(2)}, u32[]{:S(2)}) %collective-permute-start.5) | collective-permute-done | bytes 131104 | tf_op jit(solution)/shard_map/ppermute | solution.py:270
  31.9 6.3 %collective-permute-start.6 = (f32[32,1024]{1,0:T(8,128)S(1)}, f32[32,1024]{1,0:T(8,128)S(1)}, u32[]{:S(2)}, u32[]{:S(2)}) collective-permute-start(f32[32,1024]{1,0:T(8,128)S(1)} %fusion.5), channel_id=1, source_target_pairs={{0,32},{4,36},{8,40},{12,44},{16,48},{20,52},{24,56},{28,60},{32,0... | collective-permute-start | bytes 393224 | tf_op jit(solution)/shard_map/ppermute | solution.py:270
  38.2 2.2 %shard_map.64 = (f32[2,32,128]{2,1,0:T(8,128)S(1)}, f32[32,128]{1,0:T(8,128)S(1)}) custom-call(f32[4,32,128]{2,1,0:T(8,128)S(1)} %tile.12.leaf_ref, f32[3,32,1024]{2,1,0:T(8,128)S(1)} %slice_bitcast_fusion.iso_ref), custom_call_target="tpu_custom_call" | custom-call | flops 3000000 | bytes 262144 | tf_op jit(solution)/shard_map/pallas_call | solution.py:145
  40.5 2.4 %shard_map.77 = (bf16[6,256,256]{2,1,0:T(8,128)(2,1)S(1)}, bf16[6,64,1024]{2,1,0:T(8,128)(2,1)S(1)}) custom-call(f32[4,32,128]{2,1,0:T(8,128)S(1)} %tile.12.leaf_ref, f32[2,32,128]{2,1,0:T(8,128)S(1)} %get-tuple-element.59.env_ref, f32[3,32,1024]{2,1,0:T(8,128)S(1)} %slice_bitcast_fusion.iso_ref), custom_call_target="tpu_custom_call" | custom-call | flops 4000000 | bytes 262144 | tf_op jit(solution)/shard_map/pallas_call | solution.py:145
  43.6 0.8 shard_map.65.env_ref
  45.0 0.8 %collective-permute-start.7 = (f32[32,1024]{1,0:T(8,128)S(1)}, f32[32,1024]{1,0:T(8,128)S(1)}, u32[]{:S(2)}, u32[]{:S(2)}) collective-permute-start(f32[32,1024]{1,0:T(8,128)S(1)} %fusion.2), channel_id=1, source_target_pairs={{0,64},{4,68},{8,72},{12,76},{16,80},{20,84},{24,88},{28,92},{32,9... | collective-permute-start | bytes 393224 | tf_op jit(solution)/shard_map/ppermute | solution.py:270
  46.4 1.8 %collective-permute-done.10.sibling_ref = f32[32,128]{1,0:T(8,128)S(1)} collective-permute-done((f32[32,128]{1,0:T(8,128)S(1)}, f32[32,128]{1,0:T(8,128)S(1)}, u32[]{:S(2)}, u32[]{:S(2)}) %collective-permute-start.10) | collective-permute-done | bytes 16416 | tf_op jit(solution)/shard_map/ppermute | solution.py:270
  48.2 0.8 shard_map.66.env_ref
  49.0 0.9 %collective-permute-start.11 = (f32[32,128]{1,0:T(8,128)S(1)}, f32[32,128]{1,0:T(8,128)S(1)}, u32[]{:S(2)}, u32[]{:S(2)}) collective-permute-start(f32[32,128]{1,0:T(8,128)S(1)} %shard_map.66.env_ref), channel_id=1, source_target_pairs={{0,16},{4,20},{8,24},{12,28},{16,0},{20,4},{24,8},{28,12},{32,48},... | collective-permute-start | bytes 49160 | tf_op jit(solution)/shard_map/ppermute | solution.py:270
  50.9 3.0 %collective-permute-done.11.sibling_ref = f32[32,128]{1,0:T(8,128)S(1)} collective-permute-done((f32[32,128]{1,0:T(8,128)S(1)}, f32[32,128]{1,0:T(8,128)S(1)}, u32[]{:S(2)}, u32[]{:S(2)}) %collective-permute-start.11) | collective-permute-done | bytes 16416 | tf_op jit(solution)/shard_map/ppermute | solution.py:270
  53.9 0.8 shard_map.67.env_ref
  55.2 1.3 %collective-permute-start.8 = (f32[32,1024]{1,0:T(8,128)S(1)}, f32[32,1024]{1,0:T(8,128)S(1)}, u32[]{:S(2)}, u32[]{:S(2)}) collective-permute-start(f32[32,1024]{1,0:T(8,128)S(1)} %pad_maximum_fusion.5), channel_id=1, source_target_pairs={{0,128},{4,132},{8,136},{12,140},{16,144},{20,148},{24,152},{28,15... | collective-permute-start | bytes 393224 | tf_op jit(solution)/shard_map/ppermute | solution.py:270
  57.1 3.5 %collective-permute-done.12.sibling_ref = f32[32,128]{1,0:T(8,128)S(1)} collective-permute-done((f32[32,128]{1,0:T(8,128)S(1)}, f32[32,128]{1,0:T(8,128)S(1)}, u32[]{:S(2)}, u32[]{:S(2)}) %collective-permute-start.12) | collective-permute-done | bytes 16416 | tf_op jit(solution)/shard_map/ppermute | solution.py:270
  60.6 0.8 shard_map.68.env_ref
  61.4 0.8 %collective-permute-start.13 = (f32[32,128]{1,0:T(8,128)S(1)}, f32[32,128]{1,0:T(8,128)S(1)}, u32[]{:S(2)}, u32[]{:S(2)}) collective-permute-start(f32[32,128]{1,0:T(8,128)S(1)} %shard_map.68.env_ref), channel_id=1, source_target_pairs={{0,64},{4,68},{8,72},{12,76},{16,80},{20,84},{24,88},{28,92},{32,9... | collective-permute-start | bytes 49160 | tf_op jit(solution)/shard_map/ppermute | solution.py:270
  63.2 2.0 %collective-permute-done.13.sibling_ref = f32[32,128]{1,0:T(8,128)S(1)} collective-permute-done((f32[32,128]{1,0:T(8,128)S(1)}, f32[32,128]{1,0:T(8,128)S(1)}, u32[]{:S(2)}, u32[]{:S(2)}) %collective-permute-start.13) | collective-permute-done | bytes 16416 | tf_op jit(solution)/shard_map/ppermute | solution.py:270
  65.2 0.8 shard_map.69.env_ref
  67.3 3.7 %collective-permute-done.14.sibling_ref = f32[32,128]{1,0:T(8,128)S(1)} collective-permute-done((f32[32,128]{1,0:T(8,128)S(1)}, f32[32,128]{1,0:T(8,128)S(1)}, u32[]{:S(2)}, u32[]{:S(2)}) %collective-permute-start.14) | collective-permute-done | bytes 16416 | tf_op jit(solution)/shard_map/ppermute | solution.py:270
  71.4 0.8 shard_map.70.env_ref
  72.2 6.8 %shard_map.78 = (f32[4,1024]{1,0:T(4,128)}, f32[3,1024]{1,0:T(4,128)S(1)}, f32[1,1024]{1,0:T(1,128)}) custom-call(s32[6]{0:T(128)S(1)} %stack.36.marked_ref, f32[32,1024]{1,0:T(8,128)S(1)} %fusion.1.root_ref, f32[32,128]{1,0:T(8,128)S(1)} %shard_map.70.env_ref, bf16[256,256]{1,0:T(8,128)(2,1)S(1)} %get-tuple-element.47.refs_0_, ...), custom_call_target="tpu_custom_call" | custom-call | flops 8000000 | bytes 262144 | tf_op jit(solution)/shard_map/pallas_call | solution.py:145
  79.0 0.6 copy.10
  (102 shorter events, 8.7 us)
Async XLA Ops:
  0.6 0.9 %copy-start.2 = (f32[1,8,1024]{2,1,0:T(8,128)S(1)}, f32[1,8,1024]{2,1,0:T(8,128)}, u32[]{:S(2)}) copy-start(f32[1,8,1024]{2,1,0:T(8,128)} %param.5) | copy-start | bytes 98308
  1.6 6.0 %collective-permute-start = (f32[4,8,1024]{2,1,0:T(8,128)S(1)}, f32[4,8,1024]{2,1,0:T(8,128)S(1)}, u32[]{:S(2)}, u32[]{:S(2)}) collective-permute-start(f32[4,8,1024]{2,1,0:T(8,128)S(1)} %constant_dynamic-update-slice_fusion), channel_id=1, source_target_pairs={{0,1},{1,0},{2,3},{3,2},{4,5},{5,4},{6,7},{7,6},{8,9},{9,8},{10,11... | collective-permute-start | bytes 393224 | tf_op jit(solution)/shard_map/ppermute | solution.py:280
  3.1 8.9 %collective-permute-start.1 = (f32[4,8,1024]{2,1,0:T(8,128)S(1)}, f32[4,8,1024]{2,1,0:T(8,128)S(1)}, u32[]{:S(2)}, u32[]{:S(2)}) collective-permute-start(f32[4,8,1024]{2,1,0:T(8,128)S(1)} %constant_dynamic-update-slice_fusion), channel_id=1, source_target_pairs={{0,2},{1,3},{2,0},{3,1},{4,6},{5,7},{6,4},{7,5},{8,10},{9,11},{10,... | collective-permute-start | bytes 393224 | tf_op jit(solution)/shard_map/ppermute | solution.py:280
  5.9 8.2 %collective-permute-start.2 = (f32[4,8,1024]{2,1,0:T(8,128)S(1)}, f32[4,8,1024]{2,1,0:T(8,128)S(1)}, u32[]{:S(2)}, u32[]{:S(2)}) collective-permute-start(f32[4,8,1024]{2,1,0:T(8,128)S(1)} %constant_dynamic-update-slice_fusion), channel_id=1, source_target_pairs={{0,3},{1,2},{2,1},{3,0},{4,7},{5,6},{6,5},{7,4},{8,11},{9,10},{10,... | collective-permute-start | bytes 393224 | tf_op jit(solution)/shard_map/ppermute | solution.py:280
  14.1 1.4 %collective-permute-start.3 = (f32[32,1024]{1,0:T(8,128)S(1)}, f32[32,1024]{1,0:T(8,128)S(1)}, u32[]{:S(2)}, u32[]{:S(2)}) collective-permute-start(f32[32,1024]{1,0:T(8,128)S(1)} %slice_bitcast_fusion.1), channel_id=1, source_target_pairs={{0,4},{4,0},{8,12},{12,8},{16,20},{20,16},{24,28},{28,24},{32,36},... | collective-permute-start | bytes 393224 | tf_op jit(solution)/shard_map/ppermute | solution.py:270
  16.1 5.8 %collective-permute-start.4 = (f32[32,1024]{1,0:T(8,128)S(1)}, f32[32,1024]{1,0:T(8,128)S(1)}, u32[]{:S(2)}, u32[]{:S(2)}) collective-permute-start(f32[32,1024]{1,0:T(8,128)S(1)} %concatenate.195), channel_id=1, source_target_pairs={{0,8},{4,12},{8,0},{12,4},{16,24},{20,28},{24,16},{28,20},{32,40},... | collective-permute-start | bytes 393224 | tf_op jit(solution)/shard_map/ppermute | solution.py:270
  21.8 23.0 %copy-start = (f32[32,1024]{1,0:T(8,128)}, f32[32,1024]{1,0:T(8,128)S(1)}, u32[]{:S(2)}) copy-start(f32[32,1024]{1,0:T(8,128)S(1)} %collective-permute-done.4) | copy-start | bytes 393220
  22.3 9.3 %collective-permute-start.5 = (f32[32,1024]{1,0:T(8,128)S(1)}, f32[32,1024]{1,0:T(8,128)S(1)}, u32[]{:S(2)}, u32[]{:S(2)}) collective-permute-start(f32[32,1024]{1,0:T(8,128)S(1)} %concatenate.206), channel_id=1, source_target_pairs={{0,16},{4,20},{8,24},{12,28},{16,0},{20,4},{24,8},{28,12},{32,48},... | collective-permute-start | bytes 393224 | tf_op jit(solution)/shard_map/ppermute | solution.py:270
  25.6 0.7 copy-start.3
  31.9 13.0 %collective-permute-start.6 = (f32[32,1024]{1,0:T(8,128)S(1)}, f32[32,1024]{1,0:T(8,128)S(1)}, u32[]{:S(2)}, u32[]{:S(2)}) collective-permute-start(f32[32,1024]{1,0:T(8,128)S(1)} %fusion.5), channel_id=1, source_target_pairs={{0,32},{4,36},{8,40},{12,44},{16,48},{20,52},{24,56},{28,60},{32,0... | collective-permute-start | bytes 393224 | tf_op jit(solution)/shard_map/ppermute | solution.py:270
  40.4 3.1 %collective-permute-start.9 = (f32[32,128]{1,0:T(8,128)S(1)}, f32[32,128]{1,0:T(8,128)S(1)}, u32[]{:S(2)}, u32[]{:S(2)}) collective-permute-start(f32[32,128]{1,0:T(8,128)S(1)} %get-tuple-element.46.env_ref), channel_id=1, source_target_pairs={{0,4},{4,0},{8,12},{12,8},{16,20},{20,16},{24,28},{28,24},{32,36},... | collective-permute-start | bytes 49160 | tf_op jit(solution)/shard_map/ppermute | solution.py:270
  44.4 3.8 %collective-permute-start.10 = (f32[32,128]{1,0:T(8,128)S(1)}, f32[32,128]{1,0:T(8,128)S(1)}, u32[]{:S(2)}, u32[]{:S(2)}) collective-permute-start(f32[32,128]{1,0:T(8,128)S(1)} %shard_map.65.env_ref), channel_id=1, source_target_pairs={{0,8},{4,12},{8,0},{12,4},{16,24},{20,28},{24,16},{28,20},{32,40},... | collective-permute-start | bytes 49160 | tf_op jit(solution)/shard_map/ppermute | solution.py:270
  44.8 10.3 %copy-start.1 = (f32[32,1024]{1,0:T(8,128)}, f32[32,1024]{1,0:T(8,128)S(1)}, u32[]{:S(2)}) copy-start(f32[32,1024]{1,0:T(8,128)S(1)} %collective-permute-done.6) | copy-start | bytes 393220
  44.9 0.9 %slice-start = ((f32[32,1024]{1,0:T(8,128)}), f32[32,512]{1,0:T(8,128)S(1)}, s32[]{:S(2)}) async-start(f32[32,1024]{1,0:T(8,128)} %copy-done), calls=%async_computation | async-start | bytes 131072 | tf_op jit(solution)/shard_map/slice | solution.py:325
  45.0 10.2 %collective-permute-start.7 = (f32[32,1024]{1,0:T(8,128)S(1)}, f32[32,1024]{1,0:T(8,128)S(1)}, u32[]{:S(2)}, u32[]{:S(2)}) collective-permute-start(f32[32,1024]{1,0:T(8,128)S(1)} %fusion.2), channel_id=1, source_target_pairs={{0,64},{4,68},{8,72},{12,76},{16,80},{20,84},{24,88},{28,92},{32,9... | collective-permute-start | bytes 393224 | tf_op jit(solution)/shard_map/ppermute | solution.py:270
  49.0 4.9 %collective-permute-start.11 = (f32[32,128]{1,0:T(8,128)S(1)}, f32[32,128]{1,0:T(8,128)S(1)}, u32[]{:S(2)}, u32[]{:S(2)}) collective-permute-start(f32[32,128]{1,0:T(8,128)S(1)} %shard_map.66.env_ref), channel_id=1, source_target_pairs={{0,16},{4,20},{8,24},{12,28},{16,0},{20,4},{24,8},{28,12},{32,48},... | collective-permute-start | bytes 49160 | tf_op jit(solution)/shard_map/ppermute | solution.py:270
  54.7 5.9 %collective-permute-start.12 = (f32[32,128]{1,0:T(8,128)S(1)}, f32[32,128]{1,0:T(8,128)S(1)}, u32[]{:S(2)}, u32[]{:S(2)}) collective-permute-start(f32[32,128]{1,0:T(8,128)S(1)} %shard_map.67.env_ref), channel_id=1, source_target_pairs={{0,48},{4,52},{8,56},{12,60},{16,32},{20,36},{24,40},{28,44},{32,1... | collective-permute-start | bytes 49160 | tf_op jit(solution)/shard_map/ppermute | solution.py:270
  55.2 1.4 %slice-start.1 = ((f32[32,1024]{1,0:T(8,128)}), f32[32,512]{1,0:T(8,128)S(1)}, s32[]{:S(2)}) async-start(f32[32,1024]{1,0:T(8,128)} %copy-done.1), calls=%async_computation.1 | async-start | bytes 131072 | tf_op jit(solution)/shard_map/slice | solution.py:325
  55.2 11.5 %collective-permute-start.8 = (f32[32,1024]{1,0:T(8,128)S(1)}, f32[32,1024]{1,0:T(8,128)S(1)}, u32[]{:S(2)}, u32[]{:S(2)}) collective-permute-start(f32[32,1024]{1,0:T(8,128)S(1)} %pad_maximum_fusion.5), channel_id=1, source_target_pairs={{0,128},{4,132},{8,136},{12,140},{16,144},{20,148},{24,152},{28,15... | collective-permute-start | bytes 393224 | tf_op jit(solution)/shard_map/ppermute | solution.py:270
  61.4 3.8 %collective-permute-start.13 = (f32[32,128]{1,0:T(8,128)S(1)}, f32[32,128]{1,0:T(8,128)S(1)}, u32[]{:S(2)}, u32[]{:S(2)}) collective-permute-start(f32[32,128]{1,0:T(8,128)S(1)} %shard_map.68.env_ref), channel_id=1, source_target_pairs={{0,64},{4,68},{8,72},{12,76},{16,80},{20,84},{24,88},{28,92},{32,9... | collective-permute-start | bytes 49160 | tf_op jit(solution)/shard_map/ppermute | solution.py:270
  66.0 5.0 %collective-permute-start.14 = (f32[32,128]{1,0:T(8,128)S(1)}, f32[32,128]{1,0:T(8,128)S(1)}, u32[]{:S(2)}, u32[]{:S(2)}) collective-permute-start(f32[32,128]{1,0:T(8,128)S(1)} %shard_map.69.env_ref), channel_id=1, source_target_pairs={{0,192},{4,196},{8,200},{12,204},{16,208},{20,212},{24,216},{28,22... | collective-permute-start | bytes 49160 | tf_op jit(solution)/shard_map/ppermute | solution.py:270
where the time goes:
time: 79.9 us; the launch traced here: 79.7 us
  waiting for transfers between devices  31.5 us (39%)
  Pallas kernels  21.6 us (27%)
  starting transfers between devices  20.9 us (26%)
  local copies, waits for them, and re-layouts  3.49 us (4%)
  between operations  1.33 us (2%)
  other arithmetic  0.86 us (1%)
    ppermute x12, waiting for transfers between devices, exchange(): return lax.ppermute(value, 'leaf', pairs)  23.9 us
    pallas_call x21, Pallas kernels, kernel_call(): pl.pallas_call(kernel, out_shape=outs, in_specs=in_specs, out_specs=[full...  21.6 us
    ppermute x12, starting transfers between devices, exchange(): return lax.ppermute(value, 'leaf', pairs)  16.1 us
    ppermute x3, waiting for transfers between devices, gather_bond(): lax.ppermute(value, 'bond', pairs)  7.6 us
    ppermute x3, starting transfers between devices, gather_bond(): lax.ppermute(value, 'bond', pairs)  4.79 us
    unnamed x10, local copies, waits for them, and re-layouts  2.25 us
  transfers between devices with their start and end apart: 15, of which 11 were waited for; matrix products, arithmetic and copies ran while one was open for 1% of the time, Pallas kernels for 17%

commit v1 on v0

v1 whole, which is shorter than its diff:
```python
import functools

import jax
import jax.numpy as jnp
from jax import lax
from jax.experimental import pallas as pl
from jax.experimental.pallas import tpu as pltpu
from jax.sharding import PartitionSpec as P

CHI = 32
LEAVES_DEV = 4
CHI2 = 1024
LANES = 128
CHUNKS = CHI2 // LANES
BF = jnp.bfloat16
F32 = jnp.float32


def lane_group(shape):
    return lax.broadcasted_iota(jnp.int32, shape, len(shape) - 1) // CHI


def halves(x):
    high = x.astype(BF).astype(F32)
    return high, x - high


def swap(chunks, first, second):
    for c in range(CHUNKS):
        first[c * CHI : (c + 1) * CHI, :] = chunks[c]
    group = lane_group((8, LANES))
    for c in range(CHUNKS):
        rows = [first[pl.ds(c * CHI + h, 8, stride=4), :] for h in range(4)]
        for g in range(4):
            moved = [pltpu.roll(rows[h], CHI * ((h - g) % 4), 1) if h != g else rows[h] for h in range(4)]
            low = jnp.where(group == 0, moved[0], moved[1])
            high = jnp.where(group == 2, moved[2], moved[3])
            second[(4 * c + g) * 8 : (4 * c + g) * 8 + 8, :] = jnp.where(group < 2, low, high)
    return [second[pl.ds(c, CHI, stride=8), :] for c in range(CHUNKS)]


def transposed(chunks):
    result = []
    for i in range(2):
        block = jnp.concatenate(chunks[4 * i : 4 * i + 4], axis=0).T
        result += [block[CHI * g : CHI * (g + 1)] for g in range(4)]
    return result


def swap_back(chunks, first, second):
    for c in range(CHUNKS):
        first[c * CHI : (c + 1) * CHI, :] = chunks[c]
    group = lane_group((8, LANES))
    for c in range(CHUNKS):
        rows = [first[pl.ds(c * CHI + h, 8, stride=4), :] for h in range(4)]
        for j in range(4):
            moved = [pltpu.roll(rows[h], CHI * ((h - j) % 4), 1) if h != j else rows[h] for h in range(4)]
            low = jnp.where(group == 0, moved[0], moved[1])
            high = jnp.where(group == 2, moved[2], moved[3])
            a = 16 * (c // 4) + 4 * j + c % 4
            second[a * 8 : a * 8 + 8, :] = jnp.where(group < 2, low, high)
    return [second[pl.ds(c, CHI, stride=8), :] for c in range(CHUNKS)]


def split_rows(chunks):
    pairs = [halves(c) for c in chunks]
    high = jnp.concatenate([p[0] for p in pairs], axis=1)
    low = jnp.concatenate([p[1] for p in pairs], axis=1)
    return jnp.concatenate([high, low], axis=0).astype(BF)


def split_lanes(chunks):
    high, low = halves(jnp.concatenate(chunks, axis=0))
    return jnp.concatenate([high, low], axis=1).astype(BF)


def left_multiply(matrix, split):
    high, low = halves(matrix)
    left = jnp.where(lane_group(matrix.shape) < 2, high, low).astype(BF)
    right = jnp.concatenate([split, split], axis=0)
    out = jnp.dot(left, right, preferred_element_type=F32)
    return [out[:, LANES * c : LANES * (c + 1)] for c in range(CHUNKS)]


def right_multiply(split, matrix):
    shape = (LANES, LANES)
    keep = lax.broadcasted_iota(jnp.int32, shape, 0) // CHI == lane_group(shape)
    blocks = [
        jnp.where(keep, jnp.concatenate([part] * 4, axis=0), 0.0).astype(BF) for part in halves(matrix)
    ]
    row = jnp.concatenate(blocks, axis=1)
    out = jnp.dot(split, jnp.concatenate([row, row], axis=0), preferred_element_type=F32)
    out = out[:, :LANES] + out[:, LANES:]
    return [out[CHI * c : CHI * (c + 1)] for c in range(CHUNKS)]


def contract(left, right):
    high, low = right[:CHI], right[CHI:]
    wide = jnp.concatenate([high, high, low, low], axis=0)
    out = lax.dot_general(left, wide, (((1,), (1,)), ((), ())), preferred_element_type=F32)
    out = out[:CHI] + out[CHI:]
    return out + pltpu.roll(out, LANES // 2, 1)


def normalize(matrix):
    row = lax.broadcasted_iota(jnp.int32, matrix.shape, 0)
    lane = lax.broadcasted_iota(jnp.int32, matrix.shape, 1)
    diagonal = jnp.where(row == lane, matrix, 0.0)
    trace = jnp.sum(jnp.sum(diagonal, axis=0, keepdims=True), axis=1, keepdims=True)
    return matrix * (CHI / trace)


def grow(natural_split, moved_split, left_env, right_env, first, second):
    turned = swap(left_multiply(left_env, moved_split), first, second)
    both = right_multiply(split_lanes(turned), right_env)
    return normalize(contract(split_rows(both), natural_split))


def load_chunks(ref):
    return [ref[:, LANES * c : LANES * (c + 1)] for c in range(CHUNKS)]


def scratch_pair():
    return [pltpu.VMEM((CHUNKS * CHI, LANES), F32), pltpu.VMEM((CHUNKS * CHI, LANES), F32)]


def full_spec():
    return pl.BlockSpec(memory_space=pltpu.VMEM)


def scalar_spec():
    return pl.BlockSpec(memory_space=pltpu.SMEM)


def shape_of(*shape, dtype=F32):
    return jax.ShapeDtypeStruct(shape, dtype)


ENV = (CHI, LANES)
MESSAGE = (CHI + 8, LANES)
ROWS = (2 * CHI, CHI2)
WIDE = (CHUNKS * CHI, 2 * LANES)
HALF = (CHI, CHI2 // 2)


def kernel_call(kernel, outs, scalars, args, scratch, nanos):
    return pl.pallas_call(
        kernel,
        out_shape=outs,
        in_specs=[scalar_spec()] * len(scalars) + [full_spec()] * len(args),
        out_specs=[full_spec()] * len(outs),
        scratch_shapes=scratch,
        cost_estimate=pl.CostEstimate(flops=int(nanos * 1150000), bytes_accessed=1024, transcendentals=0),
        compiler_params=pltpu.CompilerParams(vmem_limit_bytes=24 * 1024 * 1024),
    )(*scalars, *args)


def bond_rows(bond_ref, mask):
    return pl.ds(pl.multiple_of(8 * (bond_ref[0] ^ mask), 8), 8)


def assemble_kernel(bond_ref, *refs):
    *pieces, now_ref, later_ref = refs
    for mask, piece in enumerate(pieces):
        rows = bond_rows(bond_ref, mask)
        now_ref[rows, :] = piece[LEAVES_DEV - 1, :, : CHI2 // 2]
        later_ref[rows, :] = piece[LEAVES_DEV - 1, :, CHI2 // 2 :]


def interleave(low, high, width):
    chunks = []
    lane = lax.broadcasted_iota(jnp.int32, (CHI, LANES), 1)
    for c in range(CHUNKS):
        if width >= LANES:
            block, rest = LANES * c // width, LANES * c % width
            part = high if block % 2 else low
            chunks.append(part[(block // 2 * width + rest) // LANES])
            continue
        base = LANES // 2 * (c % 2)
        out = None
        for block in range(LANES // width):
            part = (high if block % 2 else low)[c // 2]
            shift = (block * width - base - block // 2 * width) % LANES
            moved = pltpu.roll(part, shift, 1) if shift else part
            out = moved if out is None else jnp.where(lane < block * width, out, moved)
        chunks.append(out)
    return chunks


def every_other(chunks, width, parity):
    half = len(chunks) // 2
    if width >= LANES:
        step = width // LANES
        return [c for i, c in enumerate(chunks) if i // step % 2 == parity]
    lane = lax.broadcasted_iota(jnp.int32, (CHI, LANES), 1)
    groups = LANES // width
    result = []
    for i in range(half):
        out = None
        for j in range(groups):
            source = 2 * j + parity
            shift = (j - source) * width % LANES
            part = chunks[2 * i + source // groups]
            moved = pltpu.roll(part, shift, 1) if shift else part
            out = moved if out is None else jnp.where(lane < j * width, out, moved)
        result.append(out)
    return result


def merge_kernel(width, upper_ref, mine_ref, theirs_ref, after_ref, now_ref, *later_refs):
    upper = upper_ref[0] == 1
    mine = [mine_ref[:, LANES * c : LANES * (c + 1)] for c in range(CHUNKS // 2)]
    theirs = [theirs_ref[:, LANES * c : LANES * (c + 1)] for c in range(CHUNKS // 2)]
    low = [jnp.where(upper, t, m) for m, t in zip(mine, theirs)]
    high = [jnp.where(upper, m, t) for m, t in zip(mine, theirs)]
    for parity, out_ref in enumerate((now_ref, *later_refs)):
        out = every_other(low, width, parity) + every_other(high, width, parity)
        for c, chunk in enumerate(out):
            out_ref[:, LANES * c : LANES * (c + 1)] = chunk


def merge(width, upper, mine, theirs, after, last):
    outs = [shape_of(*HALF)] * (1 if last else 2)
    return kernel_call(
        functools.partial(merge_kernel, width), outs, (upper,), (mine, theirs, after), [], 300
    )


def prepare_kernel(
    width, core_ref, upper_ref, mine_ref, theirs_ref, natural_ref, moved_ref, own_ref, other_ref, first, second
):
    core = core_ref[0] == 1
    mine = [mine_ref[:, LANES * c : LANES * (c + 1)] for c in range(CHUNKS // 2)]
    theirs = [theirs_ref[:, LANES * c : LANES * (c + 1)] for c in range(CHUNKS // 2)]
    low = [jnp.where(core, t, m) for m, t in zip(mine, theirs)]
    high = [jnp.where(core, m, t) for m, t in zip(mine, theirs)]
    natural = interleave(low, high, width)
    natural_ref[...] = split_rows(natural)
    moved_ref[...] = split_rows(swap(natural, first, second))
    by_left = swap_back(transposed(natural), first, second)
    by_right = swap(by_left, first, second)
    upper = upper_ref[0] == 1
    own = [jnp.where(upper, r, l) for l, r in zip(by_left, by_right)]
    other = [jnp.where(upper, l, r) for l, r in zip(by_left, by_right)]
    own_ref[...] = split_lanes(own)
    other_ref[...] = split_rows(other)


def prepare(width, core, upper, mine, theirs):
    outs = [shape_of(*ROWS, dtype=BF), shape_of(*ROWS, dtype=BF), shape_of(*WIDE, dtype=BF), shape_of(*ROWS, dtype=BF)]
    return kernel_call(
        functools.partial(prepare_kernel, width), outs, (core, upper), (mine, theirs), scratch_pair(), 600
    )


def grow_kernel(upper_ref, natural_ref, moved_ref, mine_ref, theirs_ref, out_ref, first, second):
    upper = upper_ref[0] == 1
    mine, theirs = mine_ref[:CHI, :], theirs_ref[:CHI, :]
    left_env = jnp.where(upper, theirs, mine)
    right_env = jnp.where(upper, mine, theirs)
    out_ref[:CHI, :] = grow(natural_ref[...], moved_ref[...], left_env, right_env, first, second)
    out_ref[CHI:, :] = mine_ref[CHI:, :] + theirs_ref[CHI:, :]


def grow_level(upper, natural, moved, mine, theirs):
    return kernel_call(
        grow_kernel, [shape_of(*MESSAGE)], (upper,), (natural, moved, mine, theirs), scratch_pair(), 800
    )[0]


def partner_kernel(other_ref, theirs_ref, out_ref, first, second):
    out_ref[...] = split_rows(swap(left_multiply(theirs_ref[:CHI, :], other_ref[...]), first, second))


def partner_level(other, theirs):
    return kernel_call(partner_kernel, [shape_of(*ROWS, dtype=BF)], (), (other, theirs), scratch_pair(), 350)[0]


def local_kernel(root_width, bond_ref, leaf_ref, *refs):
    pieces = refs[:-5]
    iso_ref, env_ref, message_ref, first, second = refs[-5:]
    nodes = LEAVES_DEV - 1
    for mask, piece in enumerate(pieces):
        rows = bond_rows(bond_ref, mask)
        for node in range(nodes):
            iso_ref[node, rows, :] = piece[node]
        first[rows, :] = piece[nodes, :, CHI2 - LANES :]
    lane = lax.broadcasted_iota(jnp.int32, (CHI, LANES), 1)
    root = split_rows([jnp.where(lane >= LANES - root_width, first[:CHI, :], 0.0)])
    gram = contract(root, root)
    envs = []
    for node in range(nodes):
        natural = load_chunks(iso_ref.at[node])
        natural_split = split_rows(natural)
        moved_split = split_rows(swap(natural, first, second))
        if node < 2:
            pair = leaf_ref[2 * node], leaf_ref[2 * node + 1]
        else:
            pair = envs
        envs.append(grow(natural_split, moved_split, *pair, first, second))
    env_ref[0] = envs[0]
    env_ref[1] = envs[1]
    message_ref[:CHI, :] = envs[2]
    message_ref[CHI:, :] = flat(gram, first)


def local_edges_kernel(leaf_ref, env_ref, iso_ref, after_ref, own_ref, partner_ref, first, second):
    for node in range(LEAVES_DEV - 1):
        by_left = swap_back(transposed(load_chunks(iso_ref.at[node])), first, second)
        by_right = swap(by_left, first, second)
        if node < 2:
            left_env, right_env = leaf_ref[2 * node], leaf_ref[2 * node + 1]
        else:
            left_env, right_env = env_ref[0], env_ref[1]
        own_ref[2 * node] = split_lanes(by_left)
        own_ref[2 * node + 1] = split_lanes(by_right)
        left_split, right_split = split_rows(by_left), split_rows(by_right)
        partner_ref[2 * node] = split_rows(swap(left_multiply(right_env, right_split), first, second))
        partner_ref[2 * node + 1] = split_rows(swap(left_multiply(left_env, left_split), first, second))


def flat(matrix, first):
    first[0:CHI, :] = matrix
    group = lane_group((8, LANES))
    rows = [first[pl.ds(h, 8, stride=4), :] for h in range(4)]
    return jnp.where(group < 2, jnp.where(group == 0, rows[0], rows[1]), jnp.where(group == 2, rows[2], rows[3]))


def unflat(flattened, first):
    group = lane_group((8, LANES))
    for h in range(4):
        part = jnp.where(group == h, flattened, 0.0)
        part = part + pltpu.roll(part, CHI, 1)
        first[pl.ds(h, 8, stride=4), :] = part + pltpu.roll(part, 2 * CHI, 1)
    return first[0:CHI, :]


def write_flat(out_ref, index, flattened):
    for c in range(CHUNKS):
        out_ref[index, 0:1, LANES * c : LANES * (c + 1)] = flattened[c : c + 1, :]


def descend(own, partner, state):
    mixed = right_multiply(own, state)
    return normalize(contract(split_rows(mixed), partner))


def down_kernel(levels, marked_ref, message_ref, *refs):
    own_refs, partner_refs = refs[:levels], refs[levels : 2 * levels]
    local_own, local_partner, leaf_out, inner_out, top_out, first = refs[2 * levels :]
    state = normalize(unflat(message_ref[CHI:, :], first))
    top = message_ref[:CHI, :]
    for level in range(levels - 1, -1, -1):
        top = jnp.where(marked_ref[level] == 1, state, top)
        state = descend(own_refs[level][...], partner_refs[level][...], state)
    states = [None, None, state]
    children = []
    for node in (2, 1, 0):
        for side in range(2):
            child = descend(local_own[2 * node + side], local_partner[2 * node + side], states[node])
            if node == 2:
                states[side] = child
            else:
                children.append((2 * node + side, child))
    write_flat(top_out, 0, flat(top, first))
    for node in range(3):
        write_flat(inner_out, node, flat(states[node], first))
    for leaf, child in children:
        flattened = flat(child, first)
        for c in range(CHUNKS):
            leaf_out[leaf : leaf + 1, LANES * c : LANES * (c + 1)] = flattened[c : c + 1, :]


def exchange(value, mask):
    pairs = [(source, source ^ mask) for source in range(lax.axis_size("leaf"))]
    return lax.ppermute(value, "leaf", pairs)


def bond_pieces(value):
    size = lax.axis_size("bond")
    return [value] + [
        lax.ppermute(value, "bond", [(source, source ^ mask) for source in range(size)]) for mask in range(1, size)
    ]


def body(leaf_metric, local_iso, top_iso):
    devices = lax.axis_size("leaf")
    top_levels = devices.bit_length() - 1
    masks = [1, 2, 4, 12, 16, 48]
    position = lax.axis_index("leaf")
    bits = [(position >> level & 1).astype(jnp.int32).reshape(1) for level in range(top_levels)]
    bond = lax.axis_index("bond").astype(jnp.int32).reshape(1)
    leaves = jnp.tile(leaf_metric.reshape(LEAVES_DEV, CHI, CHI), (1, 1, 4))

    pieces = bond_pieces(jnp.concatenate([local_iso, top_iso], axis=0))
    now, later = kernel_call(assemble_kernel, [shape_of(*HALF)] * 2, (bond,), pieces, [], 200)
    local_whole, local_envs, message = kernel_call(
        functools.partial(local_kernel, CHI2 // devices),
        [shape_of(LEAVES_DEV - 1, CHI, CHI2), shape_of(2, *ENV), shape_of(*MESSAGE)],
        (bond,),
        (leaves, *pieces),
        scratch_pair(),
        2500,
    )

    owns, partners = [], []
    for level in range(top_levels):
        if level + 1 < top_levels:
            incoming = exchange(later, masks[level + 1])
        other_half = exchange(now, 1)
        natural, moved, own, other = prepare(CHI2 >> level + 1, bits[0], bits[level], now, other_half)
        theirs = exchange(message, masks[level])
        before = message
        message = grow_level(bits[level], natural, moved, message, theirs)
        if level + 1 < top_levels:
            last = level + 2 == top_levels
            now, *rest = merge(CHI2 >> level + 2, bits[level + 1], later, incoming, before, last)
            later = None if last else rest[0]
        if level == top_levels - 2:
            after = message
        owns.append(own)
        partners.append(partner_level(other, theirs))
    local_own, local_partner = kernel_call(
        local_edges_kernel,
        [shape_of(6, *WIDE, dtype=BF), shape_of(6, *ROWS, dtype=BF)],
        (),
        (leaves, local_envs, local_whole, after),
        scratch_pair(),
        2500,
    )

    marked = jnp.stack(
        [((position + 1) % (2 << level) == 1 << level).astype(jnp.int32) for level in range(top_levels)]
    )
    leaf_rho, inner_rho, top_rho = kernel_call(
        functools.partial(down_kernel, top_levels),
        [shape_of(LEAVES_DEV, CHI2), shape_of(LEAVES_DEV - 1, 1, CHI2), shape_of(1, 1, CHI2)],
        (marked,),
        (message, *owns, *partners, local_own, local_partner),
        [pltpu.VMEM((CHI, LANES), F32)],
        7000,
    )
    return (leaf_rho[None], jnp.swapaxes(inner_rho, 0, 1), top_rho)


def solution(mesh):
    in_specs = (P("bond", "leaf", None), P("leaf", "bond", None), P("leaf", "bond", None))
    out_specs = (P("bond", "leaf", None), P("bond", "leaf", None), P("bond", "leaf", None))
    return jax.shard_map(body, mesh=mesh, in_specs=in_specs, out_specs=out_specs, check_vma=False)
```

time: 79.9 us -> 63 us (0.79)
  the two profiles are of different devices: /device:TPU:24 before, /device:TPU:1 now
where the time goes in v1:
time: 63 us; the launch traced here: 62.8 us
  starting transfers between devices  32.7 us (52%)
  Pallas kernels  22.4 us (36%)
  waiting for transfers between devices  4.85 us (8%)
  local copies, waits for them, and re-layouts  1.92 us (3%)
  between operations  0.92 us (1%)
    ppermute x17, starting transfers between devices, exchange(): return lax.ppermute(value, 'leaf', pairs)  28.6 us
    pallas_call x27, Pallas kernels, kernel_call(): pl.pallas_call(kernel, out_shape=outs, in_specs=[scalar_spec()] * len(sca...  22.4 us
    ppermute x3, starting transfers between devices, bond_pieces(): lax.ppermute(value, 'bond', [(source, source ^ mask) for source in range(...  4.07 us
    ppermute x3, waiting for transfers between devices, bond_pieces(): lax.ppermute(value, 'bond', [(source, source ^ mask) for source in range(...  3.73 us
    unnamed x5, local copies, waits for them, and re-layouts  1.52 us
  transfers between devices with their start and end apart: 20, of which 3 were waited for; matrix products, arithmetic and copies ran while one was open for 1% of the time, Pallas kernels for 24%

profile of v1, /device:TPU:1, one launch (start us, length us, event | category | flops | bytes accessed | tf_op | source)
XLA Modules:
  0.0 62.8 jit_solution(15693860037072076445)
XLA Ops:
  0.6 0.9 %constant_dynamic-update-slice_fusion.1 = f32[4,8,1024]{2,1,0:T(8,128)S(1)} fusion(f32[3,8,1024]{2,1,0:T(8,128)} %param.4), kind=kLoop, calls=%fused_computation.1 | loop fusion | bytes 196608
  1.6 3.4 %collective-permute-start.2 = (f32[4,8,1024]{2,1,0:T(8,128)S(1)}, f32[4,8,1024]{2,1,0:T(8,128)S(1)}, u32[]{:S(2)}, u32[]{:S(2)}) collective-permute-start(f32[4,8,1024]{2,1,0:T(8,128)S(1)} %constant_dynamic-update-slice_fusion.refs_0_), channel_id=1, source_target_pairs={{0,3},{1,2},{2,1},{3,0},{4,7},{5,6},{6,5},{7,4},{8,11},{9,10},{10,... | collective-permute-start | bytes 393224 | tf_op jit(solution)/shard_map/ppermute | solution.py:382
  5.8 0.6 copy-done.1
  6.7 2.5 %collective-permute-done.2.refs_3_ = f32[4,8,1024]{2,1,0:T(8,128)S(1)} collective-permute-done((f32[4,8,1024]{2,1,0:T(8,128)S(1)}, f32[4,8,1024]{2,1,0:T(8,128)S(1)}, u32[]{:S(2)}, u32[]{:S(2)}) %collective-permute-start.2) | collective-permute-done | bytes 131104 | tf_op jit(solution)/shard_map/ppermute | solution.py:382
  9.2 1.2 %collective-permute-done.1.refs_2_ = f32[4,8,1024]{2,1,0:T(8,128)S(1)} collective-permute-done((f32[4,8,1024]{2,1,0:T(8,128)S(1)}, f32[4,8,1024]{2,1,0:T(8,128)S(1)}, u32[]{:S(2)}, u32[]{:S(2)}) %collective-permute-start.1) | collective-permute-done | bytes 131104 | tf_op jit(solution)/shard_map/ppermute | solution.py:382
  10.4 2.5 %collective-permute-start.3 = (f32[32,512]{1,0:T(8,128)S(1)}, f32[32,512]{1,0:T(8,128)S(1)}, u32[]{:S(2)}, u32[]{:S(2)}) collective-permute-start(f32[32,512]{1,0:T(8,128)S(1)} %get-tuple-element.45.mine_ref), channel_id=1, source_target_pairs={{0,8},{4,12},{8,0},{12,4},{16,24},{20,28},{24,16},{28,20},{32,40},... | collective-permute-start | bytes 196616 | tf_op jit(solution)/shard_map/ppermute | solution.py:376
  13.0 2.9 %collective-permute-start.5 = (f32[32,512]{1,0:T(8,128)S(1)}, f32[32,512]{1,0:T(8,128)S(1)}, u32[]{:S(2)}, u32[]{:S(2)}) collective-permute-start(f32[32,512]{1,0:T(8,128)S(1)} %get-tuple-element.48.mine_ref), channel_id=1, source_target_pairs={{0,4},{4,0},{8,12},{12,8},{16,20},{20,16},{24,28},{28,24},{32,36},... | collective-permute-start | bytes 196616 | tf_op jit(solution)/shard_map/ppermute | solution.py:376
  15.8 2.1 %shard_map.59 = (f32[3,32,1024]{2,1,0:T(8,128)S(1)}, f32[2,32,128]{2,1,0:T(8,128)S(1)}, f32[40,128]{1,0:T(8,128)S(1)}) custom-call(s32[1]{0:T(128)} %bitcast.12.bond_ref, f32[4,32,128]{2,1,0:T(8,128)S(1)} %tile.12.leaf_ref, f32[4,8,1024]{2,1,0:T(8,128)S(1)} %constant_dynamic-update-slice_fusion.refs_0_, f32[4,8,1024]{2,1,0:T(8,128)S(1)} %collective-permute-done.refs_1_, ...), custom_call_target="tpu_custom_call" | custom-call | flops 2875000064 | bytes 1024 | tf_op jit(solution)/shard_map/pallas_call | solution.py:147
  18.0 3.1 %collective-permute-start.4 = (f32[32,512]{1,0:T(8,128)S(1)}, f32[32,512]{1,0:T(8,128)S(1)}, u32[]{:S(2)}, u32[]{:S(2)}) collective-permute-start(f32[32,512]{1,0:T(8,128)S(1)} %get-tuple-element.47.mine_ref), channel_id=1, source_target_pairs={{0,16},{4,20},{8,24},{12,28},{16,0},{20,4},{24,8},{28,12},{32,48},... | collective-permute-start | bytes 196616 | tf_op jit(solution)/shard_map/ppermute | solution.py:376
  21.1 0.8 %collective-permute-start.8 = (f32[32,512]{1,0:T(8,128)S(1)}, f32[32,512]{1,0:T(8,128)S(1)}, u32[]{:S(2)}, u32[]{:S(2)}) collective-permute-start(f32[32,512]{1,0:T(8,128)S(1)} %get-tuple-element.52.mine_ref), channel_id=1, source_target_pairs={{0,4},{4,0},{8,12},{12,8},{16,20},{20,16},{24,28},{28,24},{32,36},... | collective-permute-start | bytes 196616 | tf_op jit(solution)/shard_map/ppermute | solution.py:376
  22.4 0.8 %shard_map.62.after_ref.mine_ref = f32[40,128]{1,0:T(8,128)S(1)} custom-call(s32[1]{0:T(128)} %bitcast.7.core_ref.upper_ref, bf16[64,1024]{1,0:T(8,128)(2,1)S(1)} %get-tuple-element.49.natural_ref, bf16[64,1024]{1,0:T(8,128)(2,1)S(1)} %get-tuple-element.50.moved_ref, f32[40,128]{1,0:T(8,128)S(1)} %get-tuple-element.46.after_ref.mine_ref, ...), custom_call_target="tpu_custom_call" | custom-call | flops 920000000 | bytes 1024 | tf_op jit(solution)/shard_map/pallas_call | solution.py:147
  23.2 1.4 %collective-permute-start.9 = (f32[40,128]{1,0:T(8,128)S(1)}, f32[40,128]{1,0:T(8,128)S(1)}, u32[]{:S(2)}, u32[]{:S(2)}) collective-permute-start(f32[40,128]{1,0:T(8,128)S(1)} %shard_map.62.after_ref.mine_ref), channel_id=1, source_target_pairs={{0,8},{4,12},{8,0},{12,4},{16,24},{20,28},{24,16},{28,20},{32,40},... | collective-permute-start | bytes 61448 | tf_op jit(solution)/shard_map/ppermute | solution.py:376
  25.0 3.4 %collective-permute-start.7 = (f32[32,512]{1,0:T(8,128)S(1)}, f32[32,512]{1,0:T(8,128)S(1)}, u32[]{:S(2)}, u32[]{:S(2)}) collective-permute-start(f32[32,512]{1,0:T(8,128)S(1)} %get-tuple-element.51.mine_ref), channel_id=1, source_target_pairs={{0,48},{4,52},{8,56},{12,60},{16,32},{20,36},{24,40},{28,44},{32,1... | collective-permute-start | bytes 196616 | tf_op jit(solution)/shard_map/ppermute | solution.py:376
  29.0 0.8 %shard_map.65.after_ref.mine_ref = f32[40,128]{1,0:T(8,128)S(1)} custom-call(s32[1]{0:T(128)} %bitcast.11.upper_ref, bf16[64,1024]{1,0:T(8,128)(2,1)S(1)} %get-tuple-element.53.natural_ref, bf16[64,1024]{1,0:T(8,128)(2,1)S(1)} %get-tuple-element.54.moved_ref, f32[40,128]{1,0:T(8,128)S(1)} %shard_map.62.after_ref.mine_ref, ...), custom_call_target="tpu_custom_call" | custom-call | flops 920000000 | bytes 1024 | tf_op jit(solution)/shard_map/pallas_call | solution.py:147
  29.8 1.2 %collective-permute-start.12 = (f32[40,128]{1,0:T(8,128)S(1)}, f32[40,128]{1,0:T(8,128)S(1)}, u32[]{:S(2)}, u32[]{:S(2)}) collective-permute-start(f32[40,128]{1,0:T(8,128)S(1)} %shard_map.65.after_ref.mine_ref), channel_id=1, source_target_pairs={{0,16},{4,20},{8,24},{12,28},{16,0},{20,4},{24,8},{28,12},{32,48},... | collective-permute-start | bytes 61448 | tf_op jit(solution)/shard_map/ppermute | solution.py:376
  31.0 2.4 %collective-permute-start.11 = (f32[32,512]{1,0:T(8,128)S(1)}, f32[32,512]{1,0:T(8,128)S(1)}, u32[]{:S(2)}, u32[]{:S(2)}) collective-permute-start(f32[32,512]{1,0:T(8,128)S(1)} %get-tuple-element.56.mine_ref), channel_id=1, source_target_pairs={{0,4},{4,0},{8,12},{12,8},{16,20},{20,16},{24,28},{28,24},{32,36},... | collective-permute-start | bytes 196616 | tf_op jit(solution)/shard_map/ppermute | solution.py:376
  33.9 1.4 %collective-permute-start.10 = (f32[32,512]{1,0:T(8,128)S(1)}, f32[32,512]{1,0:T(8,128)S(1)}, u32[]{:S(2)}, u32[]{:S(2)}) collective-permute-start(f32[32,512]{1,0:T(8,128)S(1)} %get-tuple-element.55.mine_ref), channel_id=1, source_target_pairs={{0,64},{4,68},{8,72},{12,76},{16,80},{20,84},{24,88},{28,92},{32,9... | collective-permute-start | bytes 196616 | tf_op jit(solution)/shard_map/ppermute | solution.py:376
  36.1 0.8 %shard_map.68.after_ref.mine_ref = f32[40,128]{1,0:T(8,128)S(1)} custom-call(s32[1]{0:T(128)} %bitcast.10.upper_ref, bf16[64,1024]{1,0:T(8,128)(2,1)S(1)} %get-tuple-element.57.natural_ref, bf16[64,1024]{1,0:T(8,128)(2,1)S(1)} %get-tuple-element.58.moved_ref, f32[40,128]{1,0:T(8,128)S(1)} %shard_map.65.after_ref.mine_ref, ...), custom_call_target="tpu_custom_call" | custom-call | flops 920000000 | bytes 1024 | tf_op jit(solution)/shard_map/pallas_call | solution.py:147
  37.0 2.3 %collective-permute-start.15 = (f32[40,128]{1,0:T(8,128)S(1)}, f32[40,128]{1,0:T(8,128)S(1)}, u32[]{:S(2)}, u32[]{:S(2)}) collective-permute-start(f32[40,128]{1,0:T(8,128)S(1)} %shard_map.68.after_ref.mine_ref), channel_id=1, source_target_pairs={{0,48},{4,52},{8,56},{12,60},{16,32},{20,36},{24,40},{28,44},{32,1... | collective-permute-start | bytes 61448 | tf_op jit(solution)/shard_map/ppermute | solution.py:376
  39.7 2.0 %collective-permute-start.13 = (f32[32,512]{1,0:T(8,128)S(1)}, f32[32,512]{1,0:T(8,128)S(1)}, u32[]{:S(2)}, u32[]{:S(2)}) collective-permute-start(f32[32,512]{1,0:T(8,128)S(1)} %get-tuple-element.59.mine_ref), channel_id=1, source_target_pairs={{0,192},{4,196},{8,200},{12,204},{16,208},{20,212},{24,216},{28,22... | collective-permute-start | bytes 196616 | tf_op jit(solution)/shard_map/ppermute | solution.py:376
  41.7 0.6 collective-permute-start.17
  42.3 0.6 %shard_map.70 = (bf16[64,1024]{1,0:T(8,128)(2,1)S(1)}, bf16[64,1024]{1,0:T(8,128)(2,1)S(1)}, bf16[256,256]{1,0:T(8,128)(2,1)S(1)}, bf16[64,1024]{1,0:T(8,128)(2,1)S(1)}) custom-call(s32[1]{0:T(128)} %bitcast.7.core_ref.upper_ref, s32[1]{0:T(128)} %bitcast.9.upper_ref, f32[32,512]{1,0:T(8,128)S(1)} %get-tuple-element.60.mine_ref, ...), custom_call_target="tpu_custom_call" | custom-call | flops 690000000 | bytes 1024 | tf_op jit(solution)/shard_map/pallas_call | solution.py:147
  43.0 0.8 %shard_map.71.after_ref.mine_ref = f32[40,128]{1,0:T(8,128)S(1)} custom-call(s32[1]{0:T(128)} %bitcast.9.upper_ref, bf16[64,1024]{1,0:T(8,128)(2,1)S(1)} %get-tuple-element.61.natural_ref, bf16[64,1024]{1,0:T(8,128)(2,1)S(1)} %get-tuple-element.62.moved_ref, f32[40,128]{1,0:T(8,128)S(1)} %shard_map.68.after_ref.mine_ref, ...), custom_call_target="tpu_custom_call" | custom-call | flops 920000000 | bytes 1024 | tf_op jit(solution)/shard_map/pallas_call | solution.py:147
  44.6 0.8 %shard_map.74 = (bf16[64,1024]{1,0:T(8,128)(2,1)S(1)}, bf16[64,1024]{1,0:T(8,128)(2,1)S(1)}, bf16[256,256]{1,0:T(8,128)(2,1)S(1)}, bf16[64,1024]{1,0:T(8,128)(2,1)S(1)}) custom-call(s32[1]{0:T(128)} %bitcast.7.core_ref.upper_ref, s32[1]{0:T(128)} %bitcast.8.upper_ref, f32[32,512]{1,0:T(8,128)S(1)} %get-tuple-element.65.mine_ref, ...), custom_call_target="tpu_custom_call" | custom-call | flops 690000000 | bytes 1024 | tf_op jit(solution)/shard_map/pallas_call | solution.py:147
  45.4 1.1 %collective-permute-done.18.theirs_ref = f32[40,128]{1,0:T(8,128)S(1)} collective-permute-done((f32[40,128]{1,0:T(8,128)S(1)}, f32[40,128]{1,0:T(8,128)S(1)}, u32[]{:S(2)}, u32[]{:S(2)}) %collective-permute-start.18) | collective-permute-done | bytes 20512 | tf_op jit(solution)/shard_map/ppermute | solution.py:376
  46.4 0.8 %shard_map.75.mine_ref.after_ref = f32[40,128]{1,0:T(8,128)S(1)} custom-call(s32[1]{0:T(128)} %bitcast.8.upper_ref, bf16[64,1024]{1,0:T(8,128)(2,1)S(1)} %get-tuple-element.66.natural_ref, bf16[64,1024]{1,0:T(8,128)(2,1)S(1)} %get-tuple-element.67.moved_ref, f32[40,128]{1,0:T(8,128)S(1)} %shard_map.71.after_ref.mine_ref, ...), custom_call_target="tpu_custom_call" | custom-call | flops 920000000 | bytes 1024 | tf_op jit(solution)/shard_map/pallas_call | solution.py:147
  47.3 0.8 %collective-permute-start.19 = (f32[40,128]{1,0:T(8,128)S(1)}, f32[40,128]{1,0:T(8,128)S(1)}, u32[]{:S(2)}, u32[]{:S(2)}) collective-permute-start(f32[40,128]{1,0:T(8,128)S(1)} %shard_map.75.mine_ref.after_ref), channel_id=1, source_target_pairs={{0,192},{4,196},{8,200},{12,204},{16,208},{20,212},{24,216},{28,22... | collective-permute-start | bytes 61448 | tf_op jit(solution)/shard_map/ppermute | solution.py:376
  48.3 3.3 %collective-permute-start.16 = (f32[32,512]{1,0:T(8,128)S(1)}, f32[32,512]{1,0:T(8,128)S(1)}, u32[]{:S(2)}, u32[]{:S(2)}) collective-permute-start(f32[32,512]{1,0:T(8,128)S(1)} %shard_map.72.mine_ref), channel_id=1, source_target_pairs={{0,4},{4,0},{8,12},{12,8},{16,20},{20,16},{24,28},{28,24},{32,36},... | collective-permute-start | bytes 196616 | tf_op jit(solution)/shard_map/ppermute | solution.py:376
  51.6 2.4 %shard_map.83 = (bf16[6,256,256]{2,1,0:T(8,128)(2,1)S(1)}, bf16[6,64,1024]{2,1,0:T(8,128)(2,1)S(1)}) custom-call(f32[4,32,128]{2,1,0:T(8,128)S(1)} %tile.12.leaf_ref, f32[2,32,128]{2,1,0:T(8,128)S(1)} %get-tuple-element.80.env_ref, f32[3,32,1024]{2,1,0:T(8,128)S(1)} %get-tuple-element.81.iso_ref, f32[40,128]{1,0:T(8,128)S(1)} %shard_map.75.mine_ref.after_ref), custom_call_target="tpu_custom_call" | custom-call | flops 2875000064 | bytes 1024 | tf_op jit(solution)/shard_map/pallas_call | solution.py:147
  54.4 0.9 %shard_map.73 = (bf16[64,1024]{1,0:T(8,128)(2,1)S(1)}, bf16[64,1024]{1,0:T(8,128)(2,1)S(1)}, bf16[256,256]{1,0:T(8,128)(2,1)S(1)}, bf16[64,1024]{1,0:T(8,128)(2,1)S(1)}) custom-call(s32[1]{0:T(128)} %bitcast.7.core_ref.upper_ref, s32[1]{0:T(128)} %bitcast.6.upper_ref, f32[32,512]{1,0:T(8,128)S(1)} %shard_map.72.mine_ref, ...), custom_call_target="tpu_custom_call" | custom-call | flops 690000000 | bytes 1024 | tf_op jit(solution)/shard_map/pallas_call | solution.py:147
  55.7 0.8 %shard_map.76.message_ref = f32[40,128]{1,0:T(8,128)S(1)} custom-call(s32[1]{0:T(128)} %bitcast.6.upper_ref, bf16[64,1024]{1,0:T(8,128)(2,1)S(1)} %get-tuple-element.63.natural_ref, bf16[64,1024]{1,0:T(8,128)(2,1)S(1)} %get-tuple-element.64.moved_ref, f32[40,128]{1,0:T(8,128)S(1)} %shard_map.75.mine_ref.after_ref, ...), custom_call_target="tpu_custom_call" | custom-call | flops 920000000 | bytes 1024 | tf_op jit(solution)/shard_map/pallas_call | solution.py:147
  56.5 6.3 %shard_map.84 = (f32[4,1024]{1,0:T(4,128)}, f32[3,1,1024]{2,1,0:T(1,128)}, f32[1,1,1024]{2,1,0:T(1,128)}) custom-call(s32[6]{0:T(128)S(1)} %stack.36.marked_ref, f32[40,128]{1,0:T(8,128)S(1)} %shard_map.76.message_ref, bf16[256,256]{1,0:T(8,128)(2,1)S(1)} %get-tuple-element.68.refs_0_, bf16[256,256]{1,0:T(8,128)(2,1)S(1)} %get-tuple-element.69.refs_1_, ...), custom_call_target="tpu_custom_call" | custom-call | flops 8049999872 | bytes 1024 | tf_op jit(solution)/shard_map/pallas_call | solution.py:147
  (46 shorter events, 6.1 us)
Async XLA Ops:
  0.6 0.9 %copy-start = (f32[1,8,1024]{2,1,0:T(8,128)S(1)}, f32[1,8,1024]{2,1,0:T(8,128)}, u32[]{:S(2)}) copy-start(f32[1,8,1024]{2,1,0:T(8,128)} %param.5) | copy-start | bytes 98308
  1.6 7.6 %collective-permute-start.2 = (f32[4,8,1024]{2,1,0:T(8,128)S(1)}, f32[4,8,1024]{2,1,0:T(8,128)S(1)}, u32[]{:S(2)}, u32[]{:S(2)}) collective-permute-start(f32[4,8,1024]{2,1,0:T(8,128)S(1)} %constant_dynamic-update-slice_fusion.refs_0_), channel_id=1, source_target_pairs={{0,3},{1,2},{2,1},{3,0},{4,7},{5,6},{6,5},{7,4},{8,11},{9,10},{10,... | collective-permute-start | bytes 393224 | tf_op jit(solution)/shard_map/ppermute | solution.py:382
  5.0 5.4 %collective-permute-start.1 = (f32[4,8,1024]{2,1,0:T(8,128)S(1)}, f32[4,8,1024]{2,1,0:T(8,128)S(1)}, u32[]{:S(2)}, u32[]{:S(2)}) collective-permute-start(f32[4,8,1024]{2,1,0:T(8,128)S(1)} %constant_dynamic-update-slice_fusion.refs_0_), channel_id=1, source_target_pairs={{0,2},{1,3},{2,0},{3,1},{4,6},{5,7},{6,4},{7,5},{8,10},{9,11},{10,... | collective-permute-start | bytes 393224 | tf_op jit(solution)/shard_map/ppermute | solution.py:382
  5.5 4.9 %collective-permute-start = (f32[4,8,1024]{2,1,0:T(8,128)S(1)}, f32[4,8,1024]{2,1,0:T(8,128)S(1)}, u32[]{:S(2)}, u32[]{:S(2)}) collective-permute-start(f32[4,8,1024]{2,1,0:T(8,128)S(1)} %constant_dynamic-update-slice_fusion.refs_0_), channel_id=1, source_target_pairs={{0,1},{1,0},{2,3},{3,2},{4,5},{5,4},{6,7},{7,6},{8,9},{9,8},{10,11... | collective-permute-start | bytes 393224 | tf_op jit(solution)/shard_map/ppermute | solution.py:382
  5.6 0.7 %copy-start.1 = (f32[1,4,1024]{2,1,0:T(4,128)S(1)}, f32[1,4,1024]{2,1,0:T(4,128)}, u32[]{:S(2)}) copy-start(f32[1,4,1024]{2,1,0:T(4,128)} %param.3) | copy-start | bytes 49156
  10.4 7.5 %collective-permute-start.3 = (f32[32,512]{1,0:T(8,128)S(1)}, f32[32,512]{1,0:T(8,128)S(1)}, u32[]{:S(2)}, u32[]{:S(2)}) collective-permute-start(f32[32,512]{1,0:T(8,128)S(1)} %get-tuple-element.45.mine_ref), channel_id=1, source_target_pairs={{0,8},{4,12},{8,0},{12,4},{16,24},{20,28},{24,16},{28,20},{32,40},... | collective-permute-start | bytes 196616 | tf_op jit(solution)/shard_map/ppermute | solution.py:376
  13.0 8.9 %collective-permute-start.5 = (f32[32,512]{1,0:T(8,128)S(1)}, f32[32,512]{1,0:T(8,128)S(1)}, u32[]{:S(2)}, u32[]{:S(2)}) collective-permute-start(f32[32,512]{1,0:T(8,128)S(1)} %get-tuple-element.48.mine_ref), channel_id=1, source_target_pairs={{0,4},{4,0},{8,12},{12,8},{16,20},{20,16},{24,28},{28,24},{32,36},... | collective-permute-start | bytes 196616 | tf_op jit(solution)/shard_map/ppermute | solution.py:376
  17.9 4.5 %collective-permute-start.6 = (f32[40,128]{1,0:T(8,128)S(1)}, f32[40,128]{1,0:T(8,128)S(1)}, u32[]{:S(2)}, u32[]{:S(2)}) collective-permute-start(f32[40,128]{1,0:T(8,128)S(1)} %get-tuple-element.46.after_ref.mine_ref), channel_id=1, source_target_pairs={{0,4},{4,0},{8,12},{12,8},{16,20},{20,16},{24,28},{28,24},{32,36},... | collective-permute-start | bytes 61448 | tf_op jit(solution)/shard_map/ppermute | solution.py:376
  18.0 7.0 %collective-permute-start.4 = (f32[32,512]{1,0:T(8,128)S(1)}, f32[32,512]{1,0:T(8,128)S(1)}, u32[]{:S(2)}, u32[]{:S(2)}) collective-permute-start(f32[32,512]{1,0:T(8,128)S(1)} %get-tuple-element.47.mine_ref), channel_id=1, source_target_pairs={{0,16},{4,20},{8,24},{12,28},{16,0},{20,4},{24,8},{28,12},{32,48},... | collective-permute-start | bytes 196616 | tf_op jit(solution)/shard_map/ppermute | solution.py:376
  21.1 7.3 %collective-permute-start.8 = (f32[32,512]{1,0:T(8,128)S(1)}, f32[32,512]{1,0:T(8,128)S(1)}, u32[]{:S(2)}, u32[]{:S(2)}) collective-permute-start(f32[32,512]{1,0:T(8,128)S(1)} %get-tuple-element.52.mine_ref), channel_id=1, source_target_pairs={{0,4},{4,0},{8,12},{12,8},{16,20},{20,16},{24,28},{28,24},{32,36},... | collective-permute-start | bytes 196616 | tf_op jit(solution)/shard_map/ppermute | solution.py:376
  23.2 5.7 %collective-permute-start.9 = (f32[40,128]{1,0:T(8,128)S(1)}, f32[40,128]{1,0:T(8,128)S(1)}, u32[]{:S(2)}, u32[]{:S(2)}) collective-permute-start(f32[40,128]{1,0:T(8,128)S(1)} %shard_map.62.after_ref.mine_ref), channel_id=1, source_target_pairs={{0,8},{4,12},{8,0},{12,4},{16,24},{20,28},{24,16},{28,20},{32,40},... | collective-permute-start | bytes 61448 | tf_op jit(solution)/shard_map/ppermute | solution.py:376
  25.0 8.8 %collective-permute-start.7 = (f32[32,512]{1,0:T(8,128)S(1)}, f32[32,512]{1,0:T(8,128)S(1)}, u32[]{:S(2)}, u32[]{:S(2)}) collective-permute-start(f32[32,512]{1,0:T(8,128)S(1)} %get-tuple-element.51.mine_ref), channel_id=1, source_target_pairs={{0,48},{4,52},{8,56},{12,60},{16,32},{20,36},{24,40},{28,44},{32,1... | collective-permute-start | bytes 196616 | tf_op jit(solution)/shard_map/ppermute | solution.py:376
  29.8 6.3 %collective-permute-start.12 = (f32[40,128]{1,0:T(8,128)S(1)}, f32[40,128]{1,0:T(8,128)S(1)}, u32[]{:S(2)}, u32[]{:S(2)}) collective-permute-start(f32[40,128]{1,0:T(8,128)S(1)} %shard_map.65.after_ref.mine_ref), channel_id=1, source_target_pairs={{0,16},{4,20},{8,24},{12,28},{16,0},{20,4},{24,8},{28,12},{32,48},... | collective-permute-start | bytes 61448 | tf_op jit(solution)/shard_map/ppermute | solution.py:376
  31.0 4.5 %collective-permute-start.11 = (f32[32,512]{1,0:T(8,128)S(1)}, f32[32,512]{1,0:T(8,128)S(1)}, u32[]{:S(2)}, u32[]{:S(2)}) collective-permute-start(f32[32,512]{1,0:T(8,128)S(1)} %get-tuple-element.56.mine_ref), channel_id=1, source_target_pairs={{0,4},{4,0},{8,12},{12,8},{16,20},{20,16},{24,28},{28,24},{32,36},... | collective-permute-start | bytes 196616 | tf_op jit(solution)/shard_map/ppermute | solution.py:376
  33.9 5.7 %collective-permute-start.10 = (f32[32,512]{1,0:T(8,128)S(1)}, f32[32,512]{1,0:T(8,128)S(1)}, u32[]{:S(2)}, u32[]{:S(2)}) collective-permute-start(f32[32,512]{1,0:T(8,128)S(1)} %get-tuple-element.55.mine_ref), channel_id=1, source_target_pairs={{0,64},{4,68},{8,72},{12,76},{16,80},{20,84},{24,88},{28,92},{32,9... | collective-permute-start | bytes 196616 | tf_op jit(solution)/shard_map/ppermute | solution.py:376
  35.3 7.0 %collective-permute-start.14 = (f32[32,512]{1,0:T(8,128)S(1)}, f32[32,512]{1,0:T(8,128)S(1)}, u32[]{:S(2)}, u32[]{:S(2)}) collective-permute-start(f32[32,512]{1,0:T(8,128)S(1)} %get-tuple-element.60.mine_ref), channel_id=1, source_target_pairs={{0,4},{4,0},{8,12},{12,8},{16,20},{20,16},{24,28},{28,24},{32,36},... | collective-permute-start | bytes 196616 | tf_op jit(solution)/shard_map/ppermute | solution.py:376
  37.0 6.0 %collective-permute-start.15 = (f32[40,128]{1,0:T(8,128)S(1)}, f32[40,128]{1,0:T(8,128)S(1)}, u32[]{:S(2)}, u32[]{:S(2)}) collective-permute-start(f32[40,128]{1,0:T(8,128)S(1)} %shard_map.68.after_ref.mine_ref), channel_id=1, source_target_pairs={{0,48},{4,52},{8,56},{12,60},{16,32},{20,36},{24,40},{28,44},{32,1... | collective-permute-start | bytes 61448 | tf_op jit(solution)/shard_map/ppermute | solution.py:376
  39.7 8.3 %collective-permute-start.13 = (f32[32,512]{1,0:T(8,128)S(1)}, f32[32,512]{1,0:T(8,128)S(1)}, u32[]{:S(2)}, u32[]{:S(2)}) collective-permute-start(f32[32,512]{1,0:T(8,128)S(1)} %get-tuple-element.59.mine_ref), channel_id=1, source_target_pairs={{0,192},{4,196},{8,200},{12,204},{16,208},{20,212},{24,216},{28,22... | collective-permute-start | bytes 196616 | tf_op jit(solution)/shard_map/ppermute | solution.py:376
  41.7 2.8 %collective-permute-start.17 = (f32[32,512]{1,0:T(8,128)S(1)}, f32[32,512]{1,0:T(8,128)S(1)}, u32[]{:S(2)}, u32[]{:S(2)}) collective-permute-start(f32[32,512]{1,0:T(8,128)S(1)} %get-tuple-element.65.mine_ref), channel_id=1, source_target_pairs={{0,4},{4,0},{8,12},{12,8},{16,20},{20,16},{24,28},{28,24},{32,36},... | collective-permute-start | bytes 196616 | tf_op jit(solution)/shard_map/ppermute | solution.py:376
  43.8 2.7 %collective-permute-start.18 = (f32[40,128]{1,0:T(8,128)S(1)}, f32[40,128]{1,0:T(8,128)S(1)}, u32[]{:S(2)}, u32[]{:S(2)}) collective-permute-start(f32[40,128]{1,0:T(8,128)S(1)} %shard_map.71.after_ref.mine_ref), channel_id=1, source_target_pairs={{0,64},{4,68},{8,72},{12,76},{16,80},{20,84},{24,88},{28,92},{32,9... | collective-permute-start | bytes 61448 | tf_op jit(solution)/shard_map/ppermute | solution.py:376
  47.3 8.0 %collective-permute-start.19 = (f32[40,128]{1,0:T(8,128)S(1)}, f32[40,128]{1,0:T(8,128)S(1)}, u32[]{:S(2)}, u32[]{:S(2)}) collective-permute-start(f32[40,128]{1,0:T(8,128)S(1)} %shard_map.75.mine_ref.after_ref), channel_id=1, source_target_pairs={{0,192},{4,196},{8,200},{12,204},{16,208},{20,212},{24,216},{28,22... | collective-permute-start | bytes 61448 | tf_op jit(solution)/shard_map/ppermute | solution.py:376
  48.3 6.1 %collective-permute-start.16 = (f32[32,512]{1,0:T(8,128)S(1)}, f32[32,512]{1,0:T(8,128)S(1)}, u32[]{:S(2)}, u32[]{:S(2)}) collective-permute-start(f32[32,512]{1,0:T(8,128)S(1)} %shard_map.72.mine_ref), channel_id=1, source_target_pairs={{0,4},{4,0},{8,12},{12,8},{16,20},{20,16},{24,28},{28,24},{32,36},... | collective-permute-start | bytes 196616 | tf_op jit(solution)/shard_map/ppermute | solution.py:376

commit v2 on v1

--- a/solution.py
+++ b/solution.py
@@ -12,6 +12,7 @@
 CHI2 = 1024
 LANES = 128
 CHUNKS = CHI2 // LANES
+BOND_MASKS = (0, 2, 3, 1)
 BF = jnp.bfloat16
 F32 = jnp.float32
 
@@ -110,18 +111,24 @@
     return matrix * (CHI / trace)
 
 
-def grow(natural_split, moved_split, left_env, right_env, first, second):
-    turned = swap(left_multiply(left_env, moved_split), first, second)
-    both = right_multiply(split_lanes(turned), right_env)
-    return normalize(contract(split_rows(both), natural_split))
+def grow_all(natural_splits, moved_splits, envs, pairs):
+    turned = [left_multiply(env[0], moved) for env, moved in zip(envs, moved_splits)]
+    turned = [swap(chunks, *pair) for chunks, pair in zip(turned, pairs)]
+    both = [right_multiply(split_lanes(chunks), env[1]) for chunks, env in zip(turned, envs)]
+    raw = [contract(split_rows(chunks), natural) for chunks, natural in zip(both, natural_splits)]
+    return [normalize(matrix) for matrix in raw]
 
 
 def load_chunks(ref):
     return [ref[:, LANES * c : LANES * (c + 1)] for c in range(CHUNKS)]
 
 
-def scratch_pair():
-    return [pltpu.VMEM((CHUNKS * CHI, LANES), F32), pltpu.VMEM((CHUNKS * CHI, LANES), F32)]
+def scratch_pairs(count):
+    return [pltpu.VMEM((CHUNKS * CHI, LANES), F32)] * (2 * count)
+
+
+def in_pairs(refs):
+    return [tuple(refs[2 * i : 2 * i + 2]) for i in range(len(refs) // 2)]
 
 
 def full_spec():
@@ -137,7 +144,8 @@
 
 
 ENV = (CHI, LANES)
-MESSAGE = (CHI + 8, LANES)
+MESSAGE = (72, LANES)
+GRAM = slice(CHI, CHI + 8)
 ROWS = (2 * CHI, CHI2)
 WIDE = (CHUNKS * CHI, 2 * LANES)
 HALF = (CHI, CHI2 // 2)
@@ -161,7 +169,7 @@
 
 def assemble_kernel(bond_ref, *refs):
     *pieces, now_ref, later_ref = refs
-    for mask, piece in enumerate(pieces):
+    for mask, piece in zip(BOND_MASKS, pieces):
         rows = bond_rows(bond_ref, mask)
         now_ref[rows, :] = piece[LEAVES_DEV - 1, :, : CHI2 // 2]
         later_ref[rows, :] = piece[LEAVES_DEV - 1, :, CHI2 // 2 :]
@@ -226,19 +234,22 @@
     )
 
 
-def prepare_kernel(
-    width, core_ref, upper_ref, mine_ref, theirs_ref, natural_ref, moved_ref, own_ref, other_ref, first, second
-):
+def prepare_kernel(width, core_ref, upper_ref, mine_ref, *refs):
+    *their_refs, natural_ref, moved_ref, own_ref, other_ref = refs[:-6]
+    pairs = in_pairs(refs[-6:])
     core = core_ref[0] == 1
-    mine = [mine_ref[:, LANES * c : LANES * (c + 1)] for c in range(CHUNKS // 2)]
-    theirs = [theirs_ref[:, LANES * c : LANES * (c + 1)] for c in range(CHUNKS // 2)]
+    half = CHUNKS // 2
+    mine = [mine_ref[:, LANES * c : LANES * (c + 1)] for c in range(half)]
+    theirs = [
+        jnp.concatenate([ref[:, LANES * c : LANES * (c + 1)] for ref in their_refs], axis=0) for c in range(half)
+    ]
     low = [jnp.where(core, t, m) for m, t in zip(mine, theirs)]
     high = [jnp.where(core, m, t) for m, t in zip(mine, theirs)]
     natural = interleave(low, high, width)
     natural_ref[...] = split_rows(natural)
-    moved_ref[...] = split_rows(swap(natural, first, second))
-    by_left = swap_back(transposed(natural), first, second)
-    by_right = swap(by_left, first, second)
+    by_left = swap_back(transposed(natural), *pairs[0])
+    moved_ref[...] = split_rows(swap(natural, *pairs[1]))
+    by_right = swap(by_left, *pairs[2])
     upper = upper_ref[0] == 1
     own = [jnp.where(upper, r, l) for l, r in zip(by_left, by_right)]
     other = [jnp.where(upper, l, r) for l, r in zip(by_left, by_right)]
@@ -249,38 +260,50 @@
 def prepare(width, core, upper, mine, theirs):
     outs = [shape_of(*ROWS, dtype=BF), shape_of(*ROWS, dtype=BF), shape_of(*WIDE, dtype=BF), shape_of(*ROWS, dtype=BF)]
     return kernel_call(
-        functools.partial(prepare_kernel, width), outs, (core, upper), (mine, theirs), scratch_pair(), 600
-    )
-
-
-def grow_kernel(upper_ref, natural_ref, moved_ref, mine_ref, theirs_ref, out_ref, first, second):
-    upper = upper_ref[0] == 1
+        functools.partial(prepare_kernel, width), outs, (core, upper), (mine, *theirs), scratch_pairs(3), 1
+    )
+
+
+def grow_and_partner(upper, natural, moved, other, mine_ref, theirs_ref, pairs):
     mine, theirs = mine_ref[:CHI, :], theirs_ref[:CHI, :]
     left_env = jnp.where(upper, theirs, mine)
     right_env = jnp.where(upper, mine, theirs)
-    out_ref[:CHI, :] = grow(natural_ref[...], moved_ref[...], left_env, right_env, first, second)
-    out_ref[CHI:, :] = mine_ref[CHI:, :] + theirs_ref[CHI:, :]
-
-
-def grow_level(upper, natural, moved, mine, theirs):
+    turned = left_multiply(left_env, moved)
+    partner = left_multiply(theirs, other)
+    turned = swap(turned, *pairs[0])
+    partner = swap(partner, *pairs[1])
+    both = right_multiply(split_lanes(turned), right_env)
+    return normalize(contract(split_rows(both), natural)), split_rows(partner)
+
+
+def grow_kernel(upper_ref, natural_ref, moved_ref, other_ref, mine_ref, theirs_ref, *refs):
+    (out_ref, partner_ref), scratch = refs[-6:-4], refs[-4:]
+    env, partner = grow_and_partner(
+        upper_ref[0] == 1, natural_ref[...], moved_ref[...], other_ref[...], mine_ref, theirs_ref, in_pairs(scratch)
+    )
+    out_ref[:CHI, :] = env
+    out_ref[GRAM, :] = mine_ref[GRAM, :] + theirs_ref[GRAM, :]
+    out_ref[GRAM.stop :, :] = jnp.zeros((MESSAGE[0] - GRAM.stop, LANES), F32)
+    partner_ref[...] = partner
+
+
+def grow_level(upper, natural, moved, other, mine, theirs, *after):
     return kernel_call(
-        grow_kernel, [shape_of(*MESSAGE)], (upper,), (natural, moved, mine, theirs), scratch_pair(), 800
-    )[0]
-
-
-def partner_kernel(other_ref, theirs_ref, out_ref, first, second):
-    out_ref[...] = split_rows(swap(left_multiply(theirs_ref[:CHI, :], other_ref[...]), first, second))
-
-
-def partner_level(other, theirs):
-    return kernel_call(partner_kernel, [shape_of(*ROWS, dtype=BF)], (), (other, theirs), scratch_pair(), 350)[0]
+        grow_kernel,
+        [shape_of(*MESSAGE), shape_of(*ROWS, dtype=BF)],
+        (upper,),
+        (natural, moved, other, mine, theirs, *after),
+        scratch_pairs(2),
+        900,
+    )
 
 
 def local_kernel(root_width, bond_ref, leaf_ref, *refs):
-    pieces = refs[:-5]
-    iso_ref, env_ref, message_ref, first, second = refs[-5:]
+    *pieces, iso_ref, env_ref, message_ref = refs[:-6]
+    pairs = in_pairs(refs[-6:])
+    first = pairs[0][0]
     nodes = LEAVES_DEV - 1
-    for mask, piece in enumerate(pieces):
+    for mask, piece in zip(BOND_MASKS, pieces):
         rows = bond_rows(bond_ref, mask)
         for node in range(nodes):
             iso_ref[node, rows, :] = piece[node]
@@ -288,35 +311,42 @@
     lane = lax.broadcasted_iota(jnp.int32, (CHI, LANES), 1)
     root = split_rows([jnp.where(lane >= LANES - root_width, first[:CHI, :], 0.0)])
     gram = contract(root, root)
-    envs = []
-    for node in range(nodes):
-        natural = load_chunks(iso_ref.at[node])
-        natural_split = split_rows(natural)
-        moved_split = split_rows(swap(natural, first, second))
-        if node < 2:
-            pair = leaf_ref[2 * node], leaf_ref[2 * node + 1]
-        else:
-            pair = envs
-        envs.append(grow(natural_split, moved_split, *pair, first, second))
+    naturals = [load_chunks(iso_ref.at[node]) for node in range(nodes)]
+    moved = [split_rows(swap(natural, *pair)) for natural, pair in zip(naturals, pairs)]
+    splits = [split_rows(natural) for natural in naturals]
+    envs = grow_all(splits[:2], moved[:2], [(leaf_ref[2 * node], leaf_ref[2 * node + 1]) for node in range(2)], pairs)
     env_ref[0] = envs[0]
     env_ref[1] = envs[1]
-    message_ref[:CHI, :] = envs[2]
-    message_ref[CHI:, :] = flat(gram, first)
-
-
-def local_edges_kernel(leaf_ref, env_ref, iso_ref, after_ref, own_ref, partner_ref, first, second):
-    for node in range(LEAVES_DEV - 1):
-        by_left = swap_back(transposed(load_chunks(iso_ref.at[node])), first, second)
-        by_right = swap(by_left, first, second)
-        if node < 2:
-            left_env, right_env = leaf_ref[2 * node], leaf_ref[2 * node + 1]
-        else:
-            left_env, right_env = env_ref[0], env_ref[1]
-        own_ref[2 * node] = split_lanes(by_left)
-        own_ref[2 * node + 1] = split_lanes(by_right)
-        left_split, right_split = split_rows(by_left), split_rows(by_right)
-        partner_ref[2 * node] = split_rows(swap(left_multiply(right_env, right_split), first, second))
-        partner_ref[2 * node + 1] = split_rows(swap(left_multiply(left_env, left_split), first, second))
+    message_ref[:CHI, :] = grow_all(splits[2:], moved[2:], [envs], pairs)[0]
+    message_ref[GRAM, :] = flat(gram, first)
+    message_ref[GRAM.stop :, :] = jnp.zeros((MESSAGE[0] - GRAM.stop, LANES), F32)
+
+
+def local_edges_kernel(node, leaf_ref, env_ref, iso_ref, after_ref, own_ref, partner_ref, *scratch):
+    pairs = in_pairs(scratch)
+    by_left = swap_back(transposed(load_chunks(iso_ref.at[node])), *pairs[0])
+    if node < 2:
+        left_env, right_env = leaf_ref[2 * node], leaf_ref[2 * node + 1]
+    else:
+        left_env, right_env = env_ref[0], env_ref[1]
+    for_right = left_multiply(left_env, split_rows(by_left))
+    by_right = swap(by_left, *pairs[1])
+    partner_ref[1] = split_rows(swap(for_right, *pairs[2]))
+    for_left = left_multiply(right_env, split_rows(by_right))
+    own_ref[0] = split_lanes(by_left)
+    own_ref[1] = split_lanes(by_right)
+    partner_ref[0] = split_rows(swap(for_left, *pairs[3]))
+
+
+def local_edges(node, *args):
+    return kernel_call(
+        functools.partial(local_edges_kernel, node),
+        [shape_of(2, *WIDE, dtype=BF), shape_of(2, *ROWS, dtype=BF)],
+        (),
+        args,
+        scratch_pairs(4),
+        800,
+    )
 
 
 def flat(matrix, first):
@@ -340,35 +370,37 @@
         out_ref[index, 0:1, LANES * c : LANES * (c + 1)] = flattened[c : c + 1, :]
 
 
-def descend(own, partner, state):
-    mixed = right_multiply(own, state)
-    return normalize(contract(split_rows(mixed), partner))
-
-
-def down_kernel(levels, marked_ref, message_ref, *refs):
-    own_refs, partner_refs = refs[:levels], refs[levels : 2 * levels]
-    local_own, local_partner, leaf_out, inner_out, top_out, first = refs[2 * levels :]
-    state = normalize(unflat(message_ref[CHI:, :], first))
-    top = message_ref[:CHI, :]
+def descend(edges):
+    mixed = [split_rows(right_multiply(own, state)) for own, _, state in edges]
+    raw = [contract(left, partner) for left, (_, partner, _) in zip(mixed, edges)]
+    return [normalize(matrix) for matrix in raw]
+
+
+def down_kernel(levels, marked_ref, upper_ref, natural_ref, moved_ref, other_ref, mine_ref, theirs_ref, *refs):
+    own_refs, partner_refs, refs = refs[:levels], refs[levels : 2 * levels - 1], refs[2 * levels - 1 :]
+    local_own, local_partner, (leaf_out, inner_out, top_out) = refs[:3], refs[3:6], refs[6:9]
+    first, *rooms = refs[9:-4]
+    root_env, partner = grow_and_partner(
+        upper_ref[0] == 1, natural_ref[...], moved_ref[...], other_ref[...], mine_ref, theirs_ref, in_pairs(refs[-4:])
+    )
+    state = normalize(unflat(mine_ref[GRAM, :] + theirs_ref[GRAM, :], first))
+    top = root_env
     for level in range(levels - 1, -1, -1):
         top = jnp.where(marked_ref[level] == 1, state, top)
-        state = descend(own_refs[level][...], partner_refs[level][...], state)
-    states = [None, None, state]
-    children = []
-    for node in (2, 1, 0):
-        for side in range(2):
-            child = descend(local_own[2 * node + side], local_partner[2 * node + side], states[node])
-            if node == 2:
-                states[side] = child
-            else:
-                children.append((2 * node + side, child))
-    write_flat(top_out, 0, flat(top, first))
+        split = partner if level == levels - 1 else partner_refs[level][...]
+        state = descend([(own_refs[level][...], split, state)])[0]
+    inner = descend([(local_own[2][side], local_partner[2][side], state) for side in range(2)])
+    leaves = descend(
+        [(local_own[leaf // 2][leaf % 2], local_partner[leaf // 2][leaf % 2], inner[leaf // 2]) for leaf in range(LEAVES_DEV)]
+    )
+    matrices = [top, *inner, state, *leaves]
+    rows = [flat(matrix, room) for matrix, room in zip(matrices, rooms)]
+    write_flat(top_out, 0, rows[0])
     for node in range(3):
-        write_flat(inner_out, node, flat(states[node], first))
-    for leaf, child in children:
-        flattened = flat(child, first)
+        write_flat(inner_out, node, rows[1 + node])
+    for leaf in range(LEAVES_DEV):
         for c in range(CHUNKS):
-            leaf_out[leaf : leaf + 1, LANES * c : LANES * (c + 1)] = flattened[c : c + 1, :]
+            leaf_out[leaf : leaf + 1, LANES * c : LANES * (c + 1)] = rows[4 + leaf][c : c + 1, :]
 
 
 def exchange(value, mask):
@@ -376,10 +408,15 @@
     return lax.ppermute(value, "leaf", pairs)
 
 
+def core_exchange(value):
+    return [exchange(part, 1) for part in (value[: CHI // 2], value[CHI // 2 :])]
+
+
 def bond_pieces(value):
     size = lax.axis_size("bond")
     return [value] + [
-        lax.ppermute(value, "bond", [(source, source ^ mask) for source in range(size)]) for mask in range(1, size)
+        lax.ppermute(value, "bond", [(source, source ^ mask) for source in range(size)])
+        for mask in BOND_MASKS[1:]
     ]
 
 
@@ -394,40 +431,47 @@
 
     pieces = bond_pieces(jnp.concatenate([local_iso, top_iso], axis=0))
     now, later = kernel_call(assemble_kernel, [shape_of(*HALF)] * 2, (bond,), pieces, [], 200)
+    other_half = core_exchange(now)
     local_whole, local_envs, message = kernel_call(
         functools.partial(local_kernel, CHI2 // devices),
         [shape_of(LEAVES_DEV - 1, CHI, CHI2), shape_of(2, *ENV), shape_of(*MESSAGE)],
         (bond,),
         (leaves, *pieces),
-        scratch_pair(),
-        2500,
+        scratch_pairs(3),
+        1800,
     )
 
     owns, partners = [], []
     for level in range(top_levels):
         if level + 1 < top_levels:
             incoming = exchange(later, masks[level + 1])
-        other_half = exchange(now, 1)
+        if level:
+            other_half = core_exchange(now)
         natural, moved, own, other = prepare(CHI2 >> level + 1, bits[0], bits[level], now, other_half)
         theirs = exchange(message, masks[level])
-        before = message
-        message = grow_level(bits[level], natural, moved, message, theirs)
+        if level == top_levels - 1:
+            owns.append(own)
+            break
+        if level == 0:
+            early = merge(CHI2 >> 2, bits[1], later, incoming, message, False)
+            before = early[:1]
+        elif level == 3:
+            local_edges_2 = local_edges(2, leaves, local_envs, local_whole, message)
+            before = local_edges_2[:1]
+        else:
+            before = ()
+        message, partner = grow_level(bits[level], natural, moved, other, message, theirs, *before)
         if level + 1 < top_levels:
             last = level + 2 == top_levels
-            now, *rest = merge(CHI2 >> level + 2, bits[level + 1], later, incoming, before, last)
+            if level == 0:
+                now, *rest = early
+            else:
+                now, *rest = merge(CHI2 >> level + 2, bits[level + 1], later, incoming, message, last)
             later = None if last else rest[0]
-        if level == top_levels - 2:
-            after = message
         owns.append(own)
-        partners.append(partner_level(other, theirs))
-    local_own, local_partner = kernel_call(
-        local_edges_kernel,
-        [shape_of(6, *WIDE, dtype=BF), shape_of(6, *ROWS, dtype=BF)],
-        (),
-        (leaves, local_envs, local_whole, after),
-        scratch_pair(),
-        2500,
-    )
+        partners.append(partner)
+    edges = [local_edges(node, leaves, local_envs, local_whole, message) for node in range(2)]
+    local_own, local_partner = zip(*edges, local_edges_2)
 
     marked = jnp.stack(
         [((position + 1) % (2 << level) == 1 << level).astype(jnp.int32) for level in range(top_levels)]
@@ -435,9 +479,9 @@
     leaf_rho, inner_rho, top_rho = kernel_call(
         functools.partial(down_kernel, top_levels),
         [shape_of(LEAVES_DEV, CHI2), shape_of(LEAVES_DEV - 1, 1, CHI2), shape_of(1, 1, CHI2)],
-        (marked,),
-        (message, *owns, *partners, local_own, local_partner),
-        [pltpu.VMEM((CHI, LANES), F32)],
+        (marked, bits[-1]),
+        (natural, moved, other, message, theirs, *owns, *partners, *local_own, *local_partner),
+        [pltpu.VMEM((CHI, LANES), F32)] * 9 + scratch_pairs(2),
         7000,
     )
     return (leaf_rho[None], jnp.swapaxes(inner_rho, 0, 1), top_rho)

time: 63 us -> 58.6 us (0.930)
  starting transfers between devices: 32.7 us -> 29 us
  Pallas kernels: 22.4 us -> 19.3 us
  waiting for transfers between devices: 4.85 us -> 7.79 us
    ppermute x17 -> x23, starting transfers between devices: 28.6 us -> 24.5 us  [exchange(): return lax.ppermute(value, 'leaf', pairs)]
    pallas_call x27 -> x22, Pallas kernels: 22.4 us -> 19.3 us  [kernel_call(): pl.pallas_call(kernel, out_shape=outs, in_specs=[scalar_spec()] * len(sca...]
    ppermute x3, waiting for transfers between devices: 3.73 us -> 6.36 us  [bond_pieces(): lax.ppermute(value, 'bond', [(source, source ^ mask) for source in range(...]
    ppermute x17 -> x23, waiting for transfers between devices: 1.12 us -> 1.43 us  [exchange(): return lax.ppermute(value, 'leaf', pairs)]
  transfers between devices with their start and end apart: 20 -> 26, of which waited for: 3 -> 4; matrix products, arithmetic and copies ran while one was open for 1% -> 1% of each run, Pallas kernels for 24% -> 21%
where the time goes in v2:
time: 58.6 us; the launch traced here: 58.5 us
  starting transfers between devices  29 us (49%)
  Pallas kernels  19.3 us (33%)
  waiting for transfers between devices  7.79 us (13%)
  local copies, waits for them, and re-layouts  1.36 us (2%)
  between operations  0.94 us (2%)
    ppermute x23, starting transfers between devices, exchange(): return lax.ppermute(value, 'leaf', pairs)  24.5 us
    pallas_call x22, Pallas kernels, kernel_call(): pl.pallas_call(kernel, out_shape=outs, in_specs=[scalar_spec()] * len(sca...  19.3 us
    ppermute x3, waiting for transfers between devices, bond_pieces(): lax.ppermute(value, 'bond', [(source, source ^ mask) for source in range(...  6.36 us
    ppermute x3, starting transfers between devices, bond_pieces(): lax.ppermute(value, 'bond', [(source, source ^ mask) for source in range(...  4.52 us
    ppermute x23, waiting for transfers between devices, exchange(): return lax.ppermute(value, 'leaf', pairs)  1.43 us
  transfers between devices with their start and end apart: 26, of which 4 were waited for; matrix products, arithmetic and copies ran while one was open for 1% of the time, Pallas kernels for 21%

profile of v2, /device:TPU:1, one launch (start us, length us, event | category | flops | bytes accessed | tf_op | source)
XLA Modules:
  0.0 58.5 jit_solution(14576578195235754361)
XLA Ops:
  0.6 0.9 %constant_dynamic-update-slice_fusion.1 = f32[4,8,1024]{2,1,0:T(8,128)S(1)} fusion(f32[3,8,1024]{2,1,0:T(8,128)} %param.4), kind=kLoop, calls=%fused_computation.1 | loop fusion | bytes 196608
  1.6 3.7 %collective-permute-start = (f32[4,8,1024]{2,1,0:T(8,128)S(1)}, f32[4,8,1024]{2,1,0:T(8,128)S(1)}, u32[]{:S(2)}, u32[]{:S(2)}) collective-permute-start(f32[4,8,1024]{2,1,0:T(8,128)S(1)} %constant_dynamic-update-slice_fusion.refs_0_), channel_id=1, source_target_pairs={{0,2},{1,3},{2,0},{3,1},{4,6},{5,7},{6,4},{7,5},{8,10},{9,11},{10,... | collective-permute-start | bytes 393224 | tf_op jit(solution)/shard_map/ppermute | solution.py:418
  5.2 0.9 %collective-permute-start.1 = (f32[4,8,1024]{2,1,0:T(8,128)S(1)}, f32[4,8,1024]{2,1,0:T(8,128)S(1)}, u32[]{:S(2)}, u32[]{:S(2)}) collective-permute-start(f32[4,8,1024]{2,1,0:T(8,128)S(1)} %constant_dynamic-update-slice_fusion.refs_0_), channel_id=1, source_target_pairs={{0,3},{1,2},{2,1},{3,0},{4,7},{5,6},{6,5},{7,4},{8,11},{9,10},{10,... | collective-permute-start | bytes 393224 | tf_op jit(solution)/shard_map/ppermute | solution.py:418
  6.4 1.2 %collective-permute-done.refs_1_ = f32[4,8,1024]{2,1,0:T(8,128)S(1)} collective-permute-done((f32[4,8,1024]{2,1,0:T(8,128)S(1)}, f32[4,8,1024]{2,1,0:T(8,128)S(1)}, u32[]{:S(2)}, u32[]{:S(2)}) %collective-permute-start) | collective-permute-done | bytes 131104 | tf_op jit(solution)/shard_map/ppermute | solution.py:418
  7.6 5.2 %collective-permute-done.1.refs_2_ = f32[4,8,1024]{2,1,0:T(8,128)S(1)} collective-permute-done((f32[4,8,1024]{2,1,0:T(8,128)S(1)}, f32[4,8,1024]{2,1,0:T(8,128)S(1)}, u32[]{:S(2)}, u32[]{:S(2)}) %collective-permute-start.1) | collective-permute-done | bytes 131104 | tf_op jit(solution)/shard_map/ppermute | solution.py:418
  12.8 1.1 %collective-permute-start.7 = (f32[16,512]{1,0:T(8,128)S(1)}, f32[16,512]{1,0:T(8,128)S(1)}, u32[]{:S(2)}, u32[]{:S(2)}) collective-permute-start(f32[16,512]{1,0:T(8,128)S(1)} %get-tuple-element.124), channel_id=1, source_target_pairs={{0,4},{4,0},{8,12},{12,8},{16,20},{20,16},{24,28},{28,24},{32,36},... | collective-permute-start | bytes 98312 | tf_op jit(solution)/shard_map/ppermute | solution.py:408
  14.7 2.0 %shard_map.59 = (f32[3,32,1024]{2,1,0:T(8,128)S(1)}, f32[2,32,128]{2,1,0:T(8,128)S(1)}, f32[72,128]{1,0:T(8,128)S(1)}) custom-call(s32[1]{0:T(128)} %bitcast.12.bond_ref, f32[4,32,128]{2,1,0:T(8,128)S(1)} %tile.12.leaf_ref, f32[4,8,1024]{2,1,0:T(8,128)S(1)} %constant_dynamic-update-slice_fusion.refs_0_, f32[4,8,1024]{2,1,0:T(8,128)S(1)} %collective-permute-done.refs_1_, ...), custom_call_target="tpu_custom_call" | custom-call | flops 2070000000 | bytes 1024 | tf_op jit(solution)/shard_map/pallas_call | solution.py:155
  16.6 0.7 %collective-permute-start.9 = (f32[72,128]{1,0:T(8,128)S(1)}, f32[72,128]{1,0:T(8,128)S(1)}, u32[]{:S(2)}, u32[]{:S(2)}) collective-permute-start(f32[72,128]{1,0:T(8,128)S(1)} %get-tuple-element.60.after_ref.mine_ref), channel_id=1, source_target_pairs={{0,4},{4,0},{8,12},{12,8},{16,20},{20,16},{24,28},{28,24},{32,36},... | collective-permute-start | bytes 110600 | tf_op jit(solution)/shard_map/ppermute | solution.py:408
  18.2 0.9 %shard_map.63 = (f32[72,128]{1,0:T(8,128)S(1)}, bf16[64,1024]{1,0:T(8,128)(2,1)S(1)}) custom-call(s32[1]{0:T(128)} %bitcast.7.core_ref.upper_ref, bf16[64,1024]{1,0:T(8,128)(2,1)S(1)} %get-tuple-element.67.natural_ref, bf16[64,1024]{1,0:T(8,128)(2,1)S(1)} %get-tuple-element.68.moved_ref, bf16[64,1024]{1,0:T(8,128)(2,1)S(1)} %get-tuple-element.69.other_ref, ...), custom_call_target="tpu_custom_call" | custom-call | flops 1035000000 | bytes 1024 | tf_op jit(solution)/shard_map/pallas_call | solution.py:155
  19.1 0.9 %collective-permute-start.10 = (f32[72,128]{1,0:T(8,128)S(1)}, f32[72,128]{1,0:T(8,128)S(1)}, u32[]{:S(2)}, u32[]{:S(2)}) collective-permute-start(f32[72,128]{1,0:T(8,128)S(1)} %get-tuple-element.70.mine_ref), channel_id=1, source_target_pairs={{0,8},{4,12},{8,0},{12,4},{16,24},{20,28},{24,16},{28,20},{32,40},... | collective-permute-start | bytes 110600 | tf_op jit(solution)/shard_map/ppermute | solution.py:408
  20.7 3.0 %collective-permute-start.4 = (f32[32,512]{1,0:T(8,128)S(1)}, f32[32,512]{1,0:T(8,128)S(1)}, u32[]{:S(2)}, u32[]{:S(2)}) collective-permute-start(f32[32,512]{1,0:T(8,128)S(1)} %get-tuple-element.61.mine_ref), channel_id=1, source_target_pairs={{0,16},{4,20},{8,24},{12,28},{16,0},{20,4},{24,8},{28,12},{32,48},... | collective-permute-start | bytes 196616 | tf_op jit(solution)/shard_map/ppermute | solution.py:408
  24.2 0.9 %shard_map.64 = (f32[72,128]{1,0:T(8,128)S(1)}, bf16[64,1024]{1,0:T(8,128)(2,1)S(1)}) custom-call(s32[1]{0:T(128)} %bitcast.11.upper_ref, bf16[64,1024]{1,0:T(8,128)(2,1)S(1)} %get-tuple-element.63.natural_ref, bf16[64,1024]{1,0:T(8,128)(2,1)S(1)} %get-tuple-element.64.moved_ref, bf16[64,1024]{1,0:T(8,128)(2,1)S(1)} %get-tuple-element.65.other_ref, ...), custom_call_target="tpu_custom_call" | custom-call | flops 1035000000 | bytes 1024 | tf_op jit(solution)/shard_map/pallas_call | solution.py:155
  25.1 1.2 %collective-permute-start.14 = (f32[72,128]{1,0:T(8,128)S(1)}, f32[72,128]{1,0:T(8,128)S(1)}, u32[]{:S(2)}, u32[]{:S(2)}) collective-permute-start(f32[72,128]{1,0:T(8,128)S(1)} %get-tuple-element.71.after_ref.mine_ref), channel_id=1, source_target_pairs={{0,16},{4,20},{8,24},{12,28},{16,0},{20,4},{24,8},{28,12},{32,48},... | collective-permute-start | bytes 110600 | tf_op jit(solution)/shard_map/ppermute | solution.py:408
  26.3 1.0 %collective-permute-done.4.theirs_ref = f32[32,512]{1,0:T(8,128)S(1)} collective-permute-done((f32[32,512]{1,0:T(8,128)S(1)}, f32[32,512]{1,0:T(8,128)S(1)}, u32[]{:S(2)}, u32[]{:S(2)}) %collective-permute-start.4) | collective-permute-done | bytes 65568 | tf_op jit(solution)/shard_map/ppermute | solution.py:408
  27.4 0.9 %collective-permute-start.12 = (f32[16,512]{1,0:T(8,128)S(1)}, f32[16,512]{1,0:T(8,128)S(1)}, u32[]{:S(2)}, u32[]{:S(2)}) collective-permute-start(f32[16,512]{1,0:T(8,128)S(1)} %get-tuple-element.122), channel_id=1, source_target_pairs={{0,4},{4,0},{8,12},{12,8},{16,20},{20,16},{24,28},{28,24},{32,36},... | collective-permute-start | bytes 98312 | tf_op jit(solution)/shard_map/ppermute | solution.py:408
  28.4 3.3 %collective-permute-start.11 = (f32[32,512]{1,0:T(8,128)S(1)}, f32[32,512]{1,0:T(8,128)S(1)}, u32[]{:S(2)}, u32[]{:S(2)}) collective-permute-start(f32[32,512]{1,0:T(8,128)S(1)} %get-tuple-element.72.mine_ref), channel_id=1, source_target_pairs={{0,48},{4,52},{8,56},{12,60},{16,32},{20,36},{24,40},{28,44},{32,1... | collective-permute-start | bytes 196616 | tf_op jit(solution)/shard_map/ppermute | solution.py:408
  32.2 0.9 %shard_map.67 = (f32[72,128]{1,0:T(8,128)S(1)}, bf16[64,1024]{1,0:T(8,128)(2,1)S(1)}) custom-call(s32[1]{0:T(128)} %bitcast.10.upper_ref, bf16[64,1024]{1,0:T(8,128)(2,1)S(1)} %get-tuple-element.74.natural_ref, bf16[64,1024]{1,0:T(8,128)(2,1)S(1)} %get-tuple-element.75.moved_ref, bf16[64,1024]{1,0:T(8,128)(2,1)S(1)} %get-tuple-element.76.other_ref, ...), custom_call_target="tpu_custom_call" | custom-call | flops 1035000000 | bytes 1024 | tf_op jit(solution)/shard_map/pallas_call | solution.py:155
  33.0 1.2 %collective-permute-start.18 = (f32[72,128]{1,0:T(8,128)S(1)}, f32[72,128]{1,0:T(8,128)S(1)}, u32[]{:S(2)}, u32[]{:S(2)}) collective-permute-start(f32[72,128]{1,0:T(8,128)S(1)} %get-tuple-element.77.after_ref.mine_ref), channel_id=1, source_target_pairs={{0,48},{4,52},{8,56},{12,60},{16,32},{20,36},{24,40},{28,44},{32,1... | collective-permute-start | bytes 110600 | tf_op jit(solution)/shard_map/ppermute | solution.py:408
  34.4 1.6 %collective-permute-start.16 = (f32[16,512]{1,0:T(8,128)S(1)}, f32[16,512]{1,0:T(8,128)S(1)}, u32[]{:S(2)}, u32[]{:S(2)}) collective-permute-start(f32[16,512]{1,0:T(8,128)S(1)} %get-tuple-element.120), channel_id=1, source_target_pairs={{0,4},{4,0},{8,12},{12,8},{16,20},{20,16},{24,28},{28,24},{32,36},... | collective-permute-start | bytes 98312 | tf_op jit(solution)/shard_map/ppermute | solution.py:408
  36.0 0.8 %shard_map.70 = (bf16[2,256,256]{2,1,0:T(8,128)(2,1)S(1)}, bf16[2,64,1024]{2,1,0:T(8,128)(2,1)S(1)}) custom-call(f32[4,32,128]{2,1,0:T(8,128)S(1)} %tile.12.leaf_ref, f32[2,32,128]{2,1,0:T(8,128)S(1)} %get-tuple-element.83.env_ref, f32[3,32,1024]{2,1,0:T(8,128)S(1)} %get-tuple-element.84.iso_ref, f32[72,128]{1,0:T(8,128)S(1)} %get-tuple-element.77.after_ref.mine_ref), custom_call_target="tpu_custom_call" | custom-call | flops 920000000 | bytes 1024 | tf_op jit(solution)/shard_map/pallas_call | solution.py:155
  36.9 1.4 %collective-permute-start.15 = (f32[32,512]{1,0:T(8,128)S(1)}, f32[32,512]{1,0:T(8,128)S(1)}, u32[]{:S(2)}, u32[]{:S(2)}) collective-permute-start(f32[32,512]{1,0:T(8,128)S(1)} %get-tuple-element.78.mine_ref), channel_id=1, source_target_pairs={{0,64},{4,68},{8,72},{12,76},{16,80},{20,84},{24,88},{28,92},{32,9... | collective-permute-start | bytes 196616 | tf_op jit(solution)/shard_map/ppermute | solution.py:408
  38.9 0.9 %shard_map.71 = (f32[72,128]{1,0:T(8,128)S(1)}, bf16[64,1024]{1,0:T(8,128)(2,1)S(1)}) custom-call(s32[1]{0:T(128)} %bitcast.9.upper_ref, bf16[64,1024]{1,0:T(8,128)(2,1)S(1)} %get-tuple-element.80.natural_ref, bf16[64,1024]{1,0:T(8,128)(2,1)S(1)} %get-tuple-element.81.moved_ref, bf16[64,1024]{1,0:T(8,128)(2,1)S(1)} %get-tuple-element.82.other_ref, ...), custom_call_target="tpu_custom_call" | custom-call | flops 1035000000 | bytes 1024 | tf_op jit(solution)/shard_map/pallas_call | solution.py:155
  40.5 2.3 %collective-permute-start.20 = (f32[16,512]{1,0:T(8,128)S(1)}, f32[16,512]{1,0:T(8,128)S(1)}, u32[]{:S(2)}, u32[]{:S(2)}) collective-permute-start(f32[16,512]{1,0:T(8,128)S(1)} %get-tuple-element.118), channel_id=1, source_target_pairs={{0,4},{4,0},{8,12},{12,8},{16,20},{20,16},{24,28},{28,24},{32,36},... | collective-permute-start | bytes 98312 | tf_op jit(solution)/shard_map/ppermute | solution.py:408
  43.0 2.0 %collective-permute-start.19 = (f32[32,512]{1,0:T(8,128)S(1)}, f32[32,512]{1,0:T(8,128)S(1)}, u32[]{:S(2)}, u32[]{:S(2)}) collective-permute-start(f32[32,512]{1,0:T(8,128)S(1)} %get-tuple-element.87.mine_ref), channel_id=1, source_target_pairs={{0,192},{4,196},{8,200},{12,204},{16,208},{20,212},{24,216},{28,22... | collective-permute-start | bytes 196616 | tf_op jit(solution)/shard_map/ppermute | solution.py:408
  44.9 0.7 %shard_map.73 = (bf16[64,1024]{1,0:T(8,128)(2,1)S(1)}, bf16[64,1024]{1,0:T(8,128)(2,1)S(1)}, bf16[256,256]{1,0:T(8,128)(2,1)S(1)}, bf16[64,1024]{1,0:T(8,128)(2,1)S(1)}) custom-call(s32[1]{0:T(128)} %bitcast.7.core_ref.upper_ref, s32[1]{0:T(128)} %bitcast.8.upper_ref, f32[32,512]{1,0:T(8,128)S(1)} %get-tuple-element.88.mine_ref, ...), custom_call_target="tpu_custom_call" | custom-call | flops 1150000 | bytes 1024 | tf_op jit(solution)/shard_map/pallas_call | solution.py:155
  45.7 0.9 %shard_map.74 = (f32[72,128]{1,0:T(8,128)S(1)}, bf16[64,1024]{1,0:T(8,128)(2,1)S(1)}) custom-call(s32[1]{0:T(128)} %bitcast.8.upper_ref, bf16[64,1024]{1,0:T(8,128)(2,1)S(1)} %get-tuple-element.89.natural_ref, bf16[64,1024]{1,0:T(8,128)(2,1)S(1)} %get-tuple-element.90.moved_ref, bf16[64,1024]{1,0:T(8,128)(2,1)S(1)} %get-tuple-element.91.other_ref, ...), custom_call_target="tpu_custom_call" | custom-call | flops 1035000000 | bytes 1024 | tf_op jit(solution)/shard_map/pallas_call | solution.py:155
  46.6 1.0 %collective-permute-start.25 = (f32[72,128]{1,0:T(8,128)S(1)}, f32[72,128]{1,0:T(8,128)S(1)}, u32[]{:S(2)}, u32[]{:S(2)}) collective-permute-start(f32[72,128]{1,0:T(8,128)S(1)} %get-tuple-element.92.after_ref.mine_ref), channel_id=1, source_target_pairs={{0,192},{4,196},{8,200},{12,204},{16,208},{20,212},{24,216},{28,22... | collective-permute-start | bytes 110600 | tf_op jit(solution)/shard_map/ppermute | solution.py:408
  47.6 0.8 %shard_map.78 = (bf16[2,256,256]{2,1,0:T(8,128)(2,1)S(1)}, bf16[2,64,1024]{2,1,0:T(8,128)(2,1)S(1)}) custom-call(f32[4,32,128]{2,1,0:T(8,128)S(1)} %tile.12.leaf_ref, f32[2,32,128]{2,1,0:T(8,128)S(1)} %get-tuple-element.83.env_ref, f32[3,32,1024]{2,1,0:T(8,128)S(1)} %get-tuple-element.84.iso_ref, f32[72,128]{1,0:T(8,128)S(1)} %get-tuple-element.92.after_ref.mine_ref), custom_call_target="tpu_custom_call" | custom-call | flops 920000000 | bytes 1024 | tf_op jit(solution)/shard_map/pallas_call | solution.py:155
  48.6 1.4 %collective-permute-start.23 = (f32[16,512]{1,0:T(8,128)S(1)}, f32[16,512]{1,0:T(8,128)S(1)}, u32[]{:S(2)}, u32[]{:S(2)}) collective-permute-start(f32[16,512]{1,0:T(8,128)S(1)} %get-tuple-element.116), channel_id=1, source_target_pairs={{0,4},{4,0},{8,12},{12,8},{16,20},{20,16},{24,28},{28,24},{32,36},... | collective-permute-start | bytes 98312 | tf_op jit(solution)/shard_map/ppermute | solution.py:408
  50.3 0.8 %shard_map.77 = (bf16[2,256,256]{2,1,0:T(8,128)(2,1)S(1)}, bf16[2,64,1024]{2,1,0:T(8,128)(2,1)S(1)}) custom-call(f32[4,32,128]{2,1,0:T(8,128)S(1)} %tile.12.leaf_ref, f32[2,32,128]{2,1,0:T(8,128)S(1)} %get-tuple-element.83.env_ref, f32[3,32,1024]{2,1,0:T(8,128)S(1)} %get-tuple-element.84.iso_ref, f32[72,128]{1,0:T(8,128)S(1)} %get-tuple-element.92.after_ref.mine_ref), custom_call_target="tpu_custom_call" | custom-call | flops 920000000 | bytes 1024 | tf_op jit(solution)/shard_map/pallas_call | solution.py:155
  51.2 0.9 %shard_map.76 = (bf16[64,1024]{1,0:T(8,128)(2,1)S(1)}, bf16[64,1024]{1,0:T(8,128)(2,1)S(1)}, bf16[256,256]{1,0:T(8,128)(2,1)S(1)}, bf16[64,1024]{1,0:T(8,128)(2,1)S(1)}) custom-call(s32[1]{0:T(128)} %bitcast.7.core_ref.upper_ref, s32[1]{0:T(128)} %bitcast.6.upper_ref, f32[32,512]{1,0:T(8,128)S(1)} %shard_map.75.mine_ref, ...), custom_call_target="tpu_custom_call" | custom-call | flops 1150000 | bytes 1024 | tf_op jit(solution)/shard_map/pallas_call | solution.py:155
  52.1 6.4 %shard_map.79 = (f32[4,1024]{1,0:T(4,128)}, f32[3,1,1024]{2,1,0:T(1,128)}, f32[1,1,1024]{2,1,0:T(1,128)}) custom-call(s32[6]{0:T(128)S(1)} %stack.36.marked_ref, s32[1]{0:T(128)} %bitcast.6.upper_ref, bf16[64,1024]{1,0:T(8,128)(2,1)S(1)} %get-tuple-element.93.natural_ref, bf16[64,1024]{1,0:T(8,128)(2,1)S(1)} %get-tuple-element.94.moved_ref, ...), custom_call_target="tpu_custom_call" | custom-call | flops 8049999872 | bytes 1024 | tf_op jit(solution)/shard_map/pallas_call | solution.py:155
  (59 shorter events, 6.1 us)
Async XLA Ops:
  0.6 0.9 %copy-start = (f32[1,8,1024]{2,1,0:T(8,128)S(1)}, f32[1,8,1024]{2,1,0:T(8,128)}, u32[]{:S(2)}) copy-start(f32[1,8,1024]{2,1,0:T(8,128)} %param.5) | copy-start | bytes 98308
  1.6 4.6 %copy-start.1 = (f32[1,4,1024]{2,1,0:T(4,128)S(1)}, f32[1,4,1024]{2,1,0:T(4,128)}, u32[]{:S(2)}) copy-start(f32[1,4,1024]{2,1,0:T(4,128)} %param.3) | copy-start | bytes 49156
  1.6 6.0 %collective-permute-start = (f32[4,8,1024]{2,1,0:T(8,128)S(1)}, f32[4,8,1024]{2,1,0:T(8,128)S(1)}, u32[]{:S(2)}, u32[]{:S(2)}) collective-permute-start(f32[4,8,1024]{2,1,0:T(8,128)S(1)} %constant_dynamic-update-slice_fusion.refs_0_), channel_id=1, source_target_pairs={{0,2},{1,3},{2,0},{3,1},{4,6},{5,7},{6,4},{7,5},{8,10},{9,11},{10,... | collective-permute-start | bytes 393224 | tf_op jit(solution)/shard_map/ppermute | solution.py:418
  5.2 7.5 %collective-permute-start.1 = (f32[4,8,1024]{2,1,0:T(8,128)S(1)}, f32[4,8,1024]{2,1,0:T(8,128)S(1)}, u32[]{:S(2)}, u32[]{:S(2)}) collective-permute-start(f32[4,8,1024]{2,1,0:T(8,128)S(1)} %constant_dynamic-update-slice_fusion.refs_0_), channel_id=1, source_target_pairs={{0,3},{1,2},{2,1},{3,0},{4,7},{5,6},{6,5},{7,4},{8,11},{9,10},{10,... | collective-permute-start | bytes 393224 | tf_op jit(solution)/shard_map/ppermute | solution.py:418
  6.1 6.7 %collective-permute-start.2 = (f32[4,8,1024]{2,1,0:T(8,128)S(1)}, f32[4,8,1024]{2,1,0:T(8,128)S(1)}, u32[]{:S(2)}, u32[]{:S(2)}) collective-permute-start(f32[4,8,1024]{2,1,0:T(8,128)S(1)} %constant_dynamic-update-slice_fusion.refs_0_), channel_id=1, source_target_pairs={{0,1},{1,0},{2,3},{3,2},{4,5},{5,4},{6,7},{7,6},{8,9},{9,8},{10,11... | collective-permute-start | bytes 393224 | tf_op jit(solution)/shard_map/ppermute | solution.py:418
  12.8 4.5 %collective-permute-start.7 = (f32[16,512]{1,0:T(8,128)S(1)}, f32[16,512]{1,0:T(8,128)S(1)}, u32[]{:S(2)}, u32[]{:S(2)}) collective-permute-start(f32[16,512]{1,0:T(8,128)S(1)} %get-tuple-element.124), channel_id=1, source_target_pairs={{0,4},{4,0},{8,12},{12,8},{16,20},{20,16},{24,28},{28,24},{32,36},... | collective-permute-start | bytes 98312 | tf_op jit(solution)/shard_map/ppermute | solution.py:408
  13.9 3.5 %collective-permute-start.8 = (f32[16,512]{1,0:T(8,128)S(1)}, f32[16,512]{1,0:T(8,128)S(1)}, u32[]{:S(2)}, u32[]{:S(2)}) collective-permute-start(f32[16,512]{1,0:T(8,128)S(1)} %get-tuple-element.123), channel_id=1, source_target_pairs={{0,4},{4,0},{8,12},{12,8},{16,20},{20,16},{24,28},{28,24},{32,36},... | collective-permute-start | bytes 98312 | tf_op jit(solution)/shard_map/ppermute | solution.py:408
  14.0 3.9 %collective-permute-start.3 = (f32[32,512]{1,0:T(8,128)S(1)}, f32[32,512]{1,0:T(8,128)S(1)}, u32[]{:S(2)}, u32[]{:S(2)}) collective-permute-start(f32[32,512]{1,0:T(8,128)S(1)} %get-tuple-element.59.mine_ref), channel_id=1, source_target_pairs={{0,8},{4,12},{8,0},{12,4},{16,24},{20,28},{24,16},{28,20},{32,40},... | collective-permute-start | bytes 196616 | tf_op jit(solution)/shard_map/ppermute | solution.py:408
  16.6 1.6 %collective-permute-start.9 = (f32[72,128]{1,0:T(8,128)S(1)}, f32[72,128]{1,0:T(8,128)S(1)}, u32[]{:S(2)}, u32[]{:S(2)}) collective-permute-start(f32[72,128]{1,0:T(8,128)S(1)} %get-tuple-element.60.after_ref.mine_ref), channel_id=1, source_target_pairs={{0,4},{4,0},{8,12},{12,8},{16,20},{20,16},{24,28},{28,24},{32,36},... | collective-permute-start | bytes 110600 | tf_op jit(solution)/shard_map/ppermute | solution.py:408
  19.1 5.2 %collective-permute-start.10 = (f32[72,128]{1,0:T(8,128)S(1)}, f32[72,128]{1,0:T(8,128)S(1)}, u32[]{:S(2)}, u32[]{:S(2)}) collective-permute-start(f32[72,128]{1,0:T(8,128)S(1)} %get-tuple-element.70.mine_ref), channel_id=1, source_target_pairs={{0,8},{4,12},{8,0},{12,4},{16,24},{20,28},{24,16},{28,20},{32,40},... | collective-permute-start | bytes 110600 | tf_op jit(solution)/shard_map/ppermute | solution.py:408
  20.0 3.7 %collective-permute-start.5 = (f32[16,512]{1,0:T(8,128)S(1)}, f32[16,512]{1,0:T(8,128)S(1)}, u32[]{:S(2)}, u32[]{:S(2)}) collective-permute-start(f32[16,512]{1,0:T(8,128)S(1)} %get-tuple-element.126), channel_id=1, source_target_pairs={{0,4},{4,0},{8,12},{12,8},{16,20},{20,16},{24,28},{28,24},{32,36},... | collective-permute-start | bytes 98312 | tf_op jit(solution)/shard_map/ppermute | solution.py:408
  20.6 3.1 %collective-permute-start.6 = (f32[16,512]{1,0:T(8,128)S(1)}, f32[16,512]{1,0:T(8,128)S(1)}, u32[]{:S(2)}, u32[]{:S(2)}) collective-permute-start(f32[16,512]{1,0:T(8,128)S(1)} %get-tuple-element.125), channel_id=1, source_target_pairs={{0,4},{4,0},{8,12},{12,8},{16,20},{20,16},{24,28},{28,24},{32,36},... | collective-permute-start | bytes 98312 | tf_op jit(solution)/shard_map/ppermute | solution.py:408
  20.7 6.6 %collective-permute-start.4 = (f32[32,512]{1,0:T(8,128)S(1)}, f32[32,512]{1,0:T(8,128)S(1)}, u32[]{:S(2)}, u32[]{:S(2)}) collective-permute-start(f32[32,512]{1,0:T(8,128)S(1)} %get-tuple-element.61.mine_ref), channel_id=1, source_target_pairs={{0,16},{4,20},{8,24},{12,28},{16,0},{20,4},{24,8},{28,12},{32,48},... | collective-permute-start | bytes 196616 | tf_op jit(solution)/shard_map/ppermute | solution.py:408
  25.1 7.1 %collective-permute-start.14 = (f32[72,128]{1,0:T(8,128)S(1)}, f32[72,128]{1,0:T(8,128)S(1)}, u32[]{:S(2)}, u32[]{:S(2)}) collective-permute-start(f32[72,128]{1,0:T(8,128)S(1)} %get-tuple-element.71.after_ref.mine_ref), channel_id=1, source_target_pairs={{0,16},{4,20},{8,24},{12,28},{16,0},{20,4},{24,8},{28,12},{32,48},... | collective-permute-start | bytes 110600 | tf_op jit(solution)/shard_map/ppermute | solution.py:408
  27.4 4.3 %collective-permute-start.12 = (f32[16,512]{1,0:T(8,128)S(1)}, f32[16,512]{1,0:T(8,128)S(1)}, u32[]{:S(2)}, u32[]{:S(2)}) collective-permute-start(f32[16,512]{1,0:T(8,128)S(1)} %get-tuple-element.122), channel_id=1, source_target_pairs={{0,4},{4,0},{8,12},{12,8},{16,20},{20,16},{24,28},{28,24},{32,36},... | collective-permute-start | bytes 98312 | tf_op jit(solution)/shard_map/ppermute | solution.py:408
  28.3 3.4 %collective-permute-start.13 = (f32[16,512]{1,0:T(8,128)S(1)}, f32[16,512]{1,0:T(8,128)S(1)}, u32[]{:S(2)}, u32[]{:S(2)}) collective-permute-start(f32[16,512]{1,0:T(8,128)S(1)} %get-tuple-element.121), channel_id=1, source_target_pairs={{0,4},{4,0},{8,12},{12,8},{16,20},{20,16},{24,28},{28,24},{32,36},... | collective-permute-start | bytes 98312 | tf_op jit(solution)/shard_map/ppermute | solution.py:408
  28.4 5.9 %collective-permute-start.11 = (f32[32,512]{1,0:T(8,128)S(1)}, f32[32,512]{1,0:T(8,128)S(1)}, u32[]{:S(2)}, u32[]{:S(2)}) collective-permute-start(f32[32,512]{1,0:T(8,128)S(1)} %get-tuple-element.72.mine_ref), channel_id=1, source_target_pairs={{0,48},{4,52},{8,56},{12,60},{16,32},{20,36},{24,40},{28,44},{32,1... | collective-permute-start | bytes 196616 | tf_op jit(solution)/shard_map/ppermute | solution.py:408
  33.0 5.8 %collective-permute-start.18 = (f32[72,128]{1,0:T(8,128)S(1)}, f32[72,128]{1,0:T(8,128)S(1)}, u32[]{:S(2)}, u32[]{:S(2)}) collective-permute-start(f32[72,128]{1,0:T(8,128)S(1)} %get-tuple-element.77.after_ref.mine_ref), channel_id=1, source_target_pairs={{0,48},{4,52},{8,56},{12,60},{16,32},{20,36},{24,40},{28,44},{32,1... | collective-permute-start | bytes 110600 | tf_op jit(solution)/shard_map/ppermute | solution.py:408
  34.4 3.9 %collective-permute-start.16 = (f32[16,512]{1,0:T(8,128)S(1)}, f32[16,512]{1,0:T(8,128)S(1)}, u32[]{:S(2)}, u32[]{:S(2)}) collective-permute-start(f32[16,512]{1,0:T(8,128)S(1)} %get-tuple-element.120), channel_id=1, source_target_pairs={{0,4},{4,0},{8,12},{12,8},{16,20},{20,16},{24,28},{28,24},{32,36},... | collective-permute-start | bytes 98312 | tf_op jit(solution)/shard_map/ppermute | solution.py:408
  35.9 2.3 %collective-permute-start.17 = (f32[16,512]{1,0:T(8,128)S(1)}, f32[16,512]{1,0:T(8,128)S(1)}, u32[]{:S(2)}, u32[]{:S(2)}) collective-permute-start(f32[16,512]{1,0:T(8,128)S(1)} %get-tuple-element.119), channel_id=1, source_target_pairs={{0,4},{4,0},{8,12},{12,8},{16,20},{20,16},{24,28},{28,24},{32,36},... | collective-permute-start | bytes 98312 | tf_op jit(solution)/shard_map/ppermute | solution.py:408
  36.9 3.4 %collective-permute-start.15 = (f32[32,512]{1,0:T(8,128)S(1)}, f32[32,512]{1,0:T(8,128)S(1)}, u32[]{:S(2)}, u32[]{:S(2)}) collective-permute-start(f32[32,512]{1,0:T(8,128)S(1)} %get-tuple-element.78.mine_ref), channel_id=1, source_target_pairs={{0,64},{4,68},{8,72},{12,76},{16,80},{20,84},{24,88},{28,92},{32,9... | collective-permute-start | bytes 196616 | tf_op jit(solution)/shard_map/ppermute | solution.py:408
  39.7 5.9 %collective-permute-start.22 = (f32[72,128]{1,0:T(8,128)S(1)}, f32[72,128]{1,0:T(8,128)S(1)}, u32[]{:S(2)}, u32[]{:S(2)}) collective-permute-start(f32[72,128]{1,0:T(8,128)S(1)} %get-tuple-element.86.after_ref.mine_ref), channel_id=1, source_target_pairs={{0,64},{4,68},{8,72},{12,76},{16,80},{20,84},{24,88},{28,92},{32,9... | collective-permute-start | bytes 110600 | tf_op jit(solution)/shard_map/ppermute | solution.py:408
  40.5 4.5 %collective-permute-start.20 = (f32[16,512]{1,0:T(8,128)S(1)}, f32[16,512]{1,0:T(8,128)S(1)}, u32[]{:S(2)}, u32[]{:S(2)}) collective-permute-start(f32[16,512]{1,0:T(8,128)S(1)} %get-tuple-element.118), channel_id=1, source_target_pairs={{0,4},{4,0},{8,12},{12,8},{16,20},{20,16},{24,28},{28,24},{32,36},... | collective-permute-start | bytes 98312 | tf_op jit(solution)/shard_map/ppermute | solution.py:408
  42.7 2.2 %collective-permute-start.21 = (f32[16,512]{1,0:T(8,128)S(1)}, f32[16,512]{1,0:T(8,128)S(1)}, u32[]{:S(2)}, u32[]{:S(2)}) collective-permute-start(f32[16,512]{1,0:T(8,128)S(1)} %get-tuple-element.117), channel_id=1, source_target_pairs={{0,4},{4,0},{8,12},{12,8},{16,20},{20,16},{24,28},{28,24},{32,36},... | collective-permute-start | bytes 98312 | tf_op jit(solution)/shard_map/ppermute | solution.py:408
  43.0 5.4 %collective-permute-start.19 = (f32[32,512]{1,0:T(8,128)S(1)}, f32[32,512]{1,0:T(8,128)S(1)}, u32[]{:S(2)}, u32[]{:S(2)}) collective-permute-start(f32[32,512]{1,0:T(8,128)S(1)} %get-tuple-element.87.mine_ref), channel_id=1, source_target_pairs={{0,192},{4,196},{8,200},{12,204},{16,208},{20,212},{24,216},{28,22... | collective-permute-start | bytes 196616 | tf_op jit(solution)/shard_map/ppermute | solution.py:408
  46.6 5.5 %collective-permute-start.25 = (f32[72,128]{1,0:T(8,128)S(1)}, f32[72,128]{1,0:T(8,128)S(1)}, u32[]{:S(2)}, u32[]{:S(2)}) collective-permute-start(f32[72,128]{1,0:T(8,128)S(1)} %get-tuple-element.92.after_ref.mine_ref), channel_id=1, source_target_pairs={{0,192},{4,196},{8,200},{12,204},{16,208},{20,212},{24,216},{28,22... | collective-permute-start | bytes 110600 | tf_op jit(solution)/shard_map/ppermute | solution.py:408
  48.6 2.5 %collective-permute-start.23 = (f32[16,512]{1,0:T(8,128)S(1)}, f32[16,512]{1,0:T(8,128)S(1)}, u32[]{:S(2)}, u32[]{:S(2)}) collective-permute-start(f32[16,512]{1,0:T(8,128)S(1)} %get-tuple-element.116), channel_id=1, source_target_pairs={{0,4},{4,0},{8,12},{12,8},{16,20},{20,16},{24,28},{28,24},{32,36},... | collective-permute-start | bytes 98312 | tf_op jit(solution)/shard_map/ppermute | solution.py:408
  50.0 1.2 %collective-permute-start.24 = (f32[16,512]{1,0:T(8,128)S(1)}, f32[16,512]{1,0:T(8,128)S(1)}, u32[]{:S(2)}, u32[]{:S(2)}) collective-permute-start(f32[16,512]{1,0:T(8,128)S(1)} %get-tuple-element.115), channel_id=1, source_target_pairs={{0,4},{4,0},{8,12},{12,8},{16,20},{20,16},{24,28},{28,24},{32,36},... | collective-permute-start | bytes 98312 | tf_op jit(solution)/shard_map/ppermute | solution.py:408

commit v3 on v2

--- a/solution.py
+++ b/solution.py
@@ -380,15 +380,28 @@
     own_refs, partner_refs, refs = refs[:levels], refs[levels : 2 * levels - 1], refs[2 * levels - 1 :]
     local_own, local_partner, (leaf_out, inner_out, top_out) = refs[:3], refs[3:6], refs[6:9]
     first, *rooms = refs[9:-4]
-    root_env, partner = grow_and_partner(
-        upper_ref[0] == 1, natural_ref[...], moved_ref[...], other_ref[...], mine_ref, theirs_ref, in_pairs(refs[-4:])
-    )
+    pairs = in_pairs(refs[-4:])
+    upper = upper_ref[0] == 1
+    mine, theirs = mine_ref[:CHI, :], theirs_ref[:CHI, :]
+    partner = split_rows(swap(left_multiply(theirs, other_ref[...]), *pairs[1]))
     state = normalize(unflat(mine_ref[GRAM, :] + theirs_ref[GRAM, :], first))
-    top = root_env
+    steps = [
+        lambda _: left_multiply(jnp.where(upper, theirs, mine), moved_ref[...]),
+        lambda turned: swap(turned, *pairs[0]),
+        lambda turned: right_multiply(split_lanes(turned), jnp.where(upper, mine, theirs)),
+        lambda both: normalize(contract(split_rows(both), natural_ref[...])),
+    ]
+    root_env = None
+    states = []
     for level in range(levels - 1, -1, -1):
-        top = jnp.where(marked_ref[level] == 1, state, top)
+        states.append(state)
+        if steps:
+            root_env = steps.pop(0)(root_env)
         split = partner if level == levels - 1 else partner_refs[level][...]
         state = descend([(own_refs[level][...], split, state)])[0]
+    top = root_env
+    for level in range(levels):
+        top = jnp.where(marked_ref[level] == 1, states[levels - 1 - level], top)
     inner = descend([(local_own[2][side], local_partner[2][side], state) for side in range(2)])
     leaves = descend(
         [(local_own[leaf // 2][leaf % 2], local_partner[leaf // 2][leaf % 2], inner[leaf // 2]) for leaf in range(LEAVES_DEV)]

time: 58.6 us -> 58.5 us (level)
  no operation moved by 1% of the time
where the time goes in v3:
time: 58.5 us; the launch traced here: 58.4 us
  starting transfers between devices  29 us (50%)
  Pallas kernels  19.2 us (33%)
  waiting for transfers between devices  7.79 us (13%)
  local copies, waits for them, and re-layouts  1.36 us (2%)
  between operations  0.94 us (2%)
    ppermute x23, starting transfers between devices, exchange(): return lax.ppermute(value, 'leaf', pairs)  24.5 us
    pallas_call x22, Pallas kernels, kernel_call(): pl.pallas_call(kernel, out_shape=outs, in_specs=[scalar_spec()] * len(sca...  19.2 us
    ppermute x3, waiting for transfers between devices, bond_pieces(): lax.ppermute(value, 'bond', [(source, source ^ mask) for source in range(...  6.36 us
    ppermute x3, starting transfers between devices, bond_pieces(): lax.ppermute(value, 'bond', [(source, source ^ mask) for source in range(...  4.52 us
    ppermute x23, waiting for transfers between devices, exchange(): return lax.ppermute(value, 'leaf', pairs)  1.43 us
  transfers between devices with their start and end apart: 26, of which 4 were waited for; matrix products, arithmetic and copies ran while one was open for 1% of the time, Pallas kernels for 21%

profile of v3, /device:TPU:1, one launch (start us, length us, event | category | flops | bytes accessed | tf_op | source)
XLA Modules:
  0.0 58.4 jit_solution(17567720877555174931)
XLA Ops:
  0.6 0.9 %constant_dynamic-update-slice_fusion.1 = f32[4,8,1024]{2,1,0:T(8,128)S(1)} fusion(f32[3,8,1024]{2,1,0:T(8,128)} %param.4), kind=kLoop, calls=%fused_computation.1 | loop fusion | bytes 196608
  1.6 3.7 %collective-permute-start = (f32[4,8,1024]{2,1,0:T(8,128)S(1)}, f32[4,8,1024]{2,1,0:T(8,128)S(1)}, u32[]{:S(2)}, u32[]{:S(2)}) collective-permute-start(f32[4,8,1024]{2,1,0:T(8,128)S(1)} %constant_dynamic-update-slice_fusion.refs_0_), channel_id=1, source_target_pairs={{0,2},{1,3},{2,0},{3,1},{4,6},{5,7},{6,4},{7,5},{8,10},{9,11},{10,... | collective-permute-start | bytes 393224 | tf_op jit(solution)/shard_map/ppermute | solution.py:431
  5.2 0.9 %collective-permute-start.1 = (f32[4,8,1024]{2,1,0:T(8,128)S(1)}, f32[4,8,1024]{2,1,0:T(8,128)S(1)}, u32[]{:S(2)}, u32[]{:S(2)}) collective-permute-start(f32[4,8,1024]{2,1,0:T(8,128)S(1)} %constant_dynamic-update-slice_fusion.refs_0_), channel_id=1, source_target_pairs={{0,3},{1,2},{2,1},{3,0},{4,7},{5,6},{6,5},{7,4},{8,11},{9,10},{10,... | collective-permute-start | bytes 393224 | tf_op jit(solution)/shard_map/ppermute | solution.py:431
  6.4 1.2 %collective-permute-done.refs_1_ = f32[4,8,1024]{2,1,0:T(8,128)S(1)} collective-permute-done((f32[4,8,1024]{2,1,0:T(8,128)S(1)}, f32[4,8,1024]{2,1,0:T(8,128)S(1)}, u32[]{:S(2)}, u32[]{:S(2)}) %collective-permute-start) | collective-permute-done | bytes 131104 | tf_op jit(solution)/shard_map/ppermute | solution.py:431
  7.6 5.2 %collective-permute-done.1.refs_2_ = f32[4,8,1024]{2,1,0:T(8,128)S(1)} collective-permute-done((f32[4,8,1024]{2,1,0:T(8,128)S(1)}, f32[4,8,1024]{2,1,0:T(8,128)S(1)}, u32[]{:S(2)}, u32[]{:S(2)}) %collective-permute-start.1) | collective-permute-done | bytes 131104 | tf_op jit(solution)/shard_map/ppermute | solution.py:431
  12.8 1.1 %collective-permute-start.7 = (f32[16,512]{1,0:T(8,128)S(1)}, f32[16,512]{1,0:T(8,128)S(1)}, u32[]{:S(2)}, u32[]{:S(2)}) collective-permute-start(f32[16,512]{1,0:T(8,128)S(1)} %get-tuple-element.124), channel_id=1, source_target_pairs={{0,4},{4,0},{8,12},{12,8},{16,20},{20,16},{24,28},{28,24},{32,36},... | collective-permute-start | bytes 98312 | tf_op jit(solution)/shard_map/ppermute | solution.py:421
  14.7 2.0 %shard_map.59 = (f32[3,32,1024]{2,1,0:T(8,128)S(1)}, f32[2,32,128]{2,1,0:T(8,128)S(1)}, f32[72,128]{1,0:T(8,128)S(1)}) custom-call(s32[1]{0:T(128)} %bitcast.12.bond_ref, f32[4,32,128]{2,1,0:T(8,128)S(1)} %tile.12.leaf_ref, f32[4,8,1024]{2,1,0:T(8,128)S(1)} %constant_dynamic-update-slice_fusion.refs_0_, f32[4,8,1024]{2,1,0:T(8,128)S(1)} %collective-permute-done.refs_1_, ...), custom_call_target="tpu_custom_call" | custom-call | flops 2070000000 | bytes 1024 | tf_op jit(solution)/shard_map/pallas_call | solution.py:155
  16.6 0.7 %collective-permute-start.9 = (f32[72,128]{1,0:T(8,128)S(1)}, f32[72,128]{1,0:T(8,128)S(1)}, u32[]{:S(2)}, u32[]{:S(2)}) collective-permute-start(f32[72,128]{1,0:T(8,128)S(1)} %get-tuple-element.60.after_ref.mine_ref), channel_id=1, source_target_pairs={{0,4},{4,0},{8,12},{12,8},{16,20},{20,16},{24,28},{28,24},{32,36},... | collective-permute-start | bytes 110600 | tf_op jit(solution)/shard_map/ppermute | solution.py:421
  18.2 0.9 %shard_map.63 = (f32[72,128]{1,0:T(8,128)S(1)}, bf16[64,1024]{1,0:T(8,128)(2,1)S(1)}) custom-call(s32[1]{0:T(128)} %bitcast.7.core_ref.upper_ref, bf16[64,1024]{1,0:T(8,128)(2,1)S(1)} %get-tuple-element.67.natural_ref, bf16[64,1024]{1,0:T(8,128)(2,1)S(1)} %get-tuple-element.68.moved_ref, bf16[64,1024]{1,0:T(8,128)(2,1)S(1)} %get-tuple-element.69.other_ref, ...), custom_call_target="tpu_custom_call" | custom-call | flops 1035000000 | bytes 1024 | tf_op jit(solution)/shard_map/pallas_call | solution.py:155
  19.1 0.9 %collective-permute-start.10 = (f32[72,128]{1,0:T(8,128)S(1)}, f32[72,128]{1,0:T(8,128)S(1)}, u32[]{:S(2)}, u32[]{:S(2)}) collective-permute-start(f32[72,128]{1,0:T(8,128)S(1)} %get-tuple-element.70.mine_ref), channel_id=1, source_target_pairs={{0,8},{4,12},{8,0},{12,4},{16,24},{20,28},{24,16},{28,20},{32,40},... | collective-permute-start | bytes 110600 | tf_op jit(solution)/shard_map/ppermute | solution.py:421
  20.7 3.0 %collective-permute-start.4 = (f32[32,512]{1,0:T(8,128)S(1)}, f32[32,512]{1,0:T(8,128)S(1)}, u32[]{:S(2)}, u32[]{:S(2)}) collective-permute-start(f32[32,512]{1,0:T(8,128)S(1)} %get-tuple-element.61.mine_ref), channel_id=1, source_target_pairs={{0,16},{4,20},{8,24},{12,28},{16,0},{20,4},{24,8},{28,12},{32,48},... | collective-permute-start | bytes 196616 | tf_op jit(solution)/shard_map/ppermute | solution.py:421
  24.2 0.9 %shard_map.64 = (f32[72,128]{1,0:T(8,128)S(1)}, bf16[64,1024]{1,0:T(8,128)(2,1)S(1)}) custom-call(s32[1]{0:T(128)} %bitcast.11.upper_ref, bf16[64,1024]{1,0:T(8,128)(2,1)S(1)} %get-tuple-element.63.natural_ref, bf16[64,1024]{1,0:T(8,128)(2,1)S(1)} %get-tuple-element.64.moved_ref, bf16[64,1024]{1,0:T(8,128)(2,1)S(1)} %get-tuple-element.65.other_ref, ...), custom_call_target="tpu_custom_call" | custom-call | flops 1035000000 | bytes 1024 | tf_op jit(solution)/shard_map/pallas_call | solution.py:155
  25.1 1.2 %collective-permute-start.14 = (f32[72,128]{1,0:T(8,128)S(1)}, f32[72,128]{1,0:T(8,128)S(1)}, u32[]{:S(2)}, u32[]{:S(2)}) collective-permute-start(f32[72,128]{1,0:T(8,128)S(1)} %get-tuple-element.71.after_ref.mine_ref), channel_id=1, source_target_pairs={{0,16},{4,20},{8,24},{12,28},{16,0},{20,4},{24,8},{28,12},{32,48},... | collective-permute-start | bytes 110600 | tf_op jit(solution)/shard_map/ppermute | solution.py:421
  26.3 1.0 %collective-permute-done.4.theirs_ref = f32[32,512]{1,0:T(8,128)S(1)} collective-permute-done((f32[32,512]{1,0:T(8,128)S(1)}, f32[32,512]{1,0:T(8,128)S(1)}, u32[]{:S(2)}, u32[]{:S(2)}) %collective-permute-start.4) | collective-permute-done | bytes 65568 | tf_op jit(solution)/shard_map/ppermute | solution.py:421
  27.4 0.9 %collective-permute-start.12 = (f32[16,512]{1,0:T(8,128)S(1)}, f32[16,512]{1,0:T(8,128)S(1)}, u32[]{:S(2)}, u32[]{:S(2)}) collective-permute-start(f32[16,512]{1,0:T(8,128)S(1)} %get-tuple-element.122), channel_id=1, source_target_pairs={{0,4},{4,0},{8,12},{12,8},{16,20},{20,16},{24,28},{28,24},{32,36},... | collective-permute-start | bytes 98312 | tf_op jit(solution)/shard_map/ppermute | solution.py:421
  28.4 3.3 %collective-permute-start.11 = (f32[32,512]{1,0:T(8,128)S(1)}, f32[32,512]{1,0:T(8,128)S(1)}, u32[]{:S(2)}, u32[]{:S(2)}) collective-permute-start(f32[32,512]{1,0:T(8,128)S(1)} %get-tuple-element.72.mine_ref), channel_id=1, source_target_pairs={{0,48},{4,52},{8,56},{12,60},{16,32},{20,36},{24,40},{28,44},{32,1... | collective-permute-start | bytes 196616 | tf_op jit(solution)/shard_map/ppermute | solution.py:421
  32.2 0.9 %shard_map.67 = (f32[72,128]{1,0:T(8,128)S(1)}, bf16[64,1024]{1,0:T(8,128)(2,1)S(1)}) custom-call(s32[1]{0:T(128)} %bitcast.10.upper_ref, bf16[64,1024]{1,0:T(8,128)(2,1)S(1)} %get-tuple-element.74.natural_ref, bf16[64,1024]{1,0:T(8,128)(2,1)S(1)} %get-tuple-element.75.moved_ref, bf16[64,1024]{1,0:T(8,128)(2,1)S(1)} %get-tuple-element.76.other_ref, ...), custom_call_target="tpu_custom_call" | custom-call | flops 1035000000 | bytes 1024 | tf_op jit(solution)/shard_map/pallas_call | solution.py:155
  33.0 1.2 %collective-permute-start.18 = (f32[72,128]{1,0:T(8,128)S(1)}, f32[72,128]{1,0:T(8,128)S(1)}, u32[]{:S(2)}, u32[]{:S(2)}) collective-permute-start(f32[72,128]{1,0:T(8,128)S(1)} %get-tuple-element.77.after_ref.mine_ref), channel_id=1, source_target_pairs={{0,48},{4,52},{8,56},{12,60},{16,32},{20,36},{24,40},{28,44},{32,1... | collective-permute-start | bytes 110600 | tf_op jit(solution)/shard_map/ppermute | solution.py:421
  34.4 1.6 %collective-permute-start.16 = (f32[16,512]{1,0:T(8,128)S(1)}, f32[16,512]{1,0:T(8,128)S(1)}, u32[]{:S(2)}, u32[]{:S(2)}) collective-permute-start(f32[16,512]{1,0:T(8,128)S(1)} %get-tuple-element.120), channel_id=1, source_target_pairs={{0,4},{4,0},{8,12},{12,8},{16,20},{20,16},{24,28},{28,24},{32,36},... | collective-permute-start | bytes 98312 | tf_op jit(solution)/shard_map/ppermute | solution.py:421
  36.0 0.8 %shard_map.70 = (bf16[2,256,256]{2,1,0:T(8,128)(2,1)S(1)}, bf16[2,64,1024]{2,1,0:T(8,128)(2,1)S(1)}) custom-call(f32[4,32,128]{2,1,0:T(8,128)S(1)} %tile.12.leaf_ref, f32[2,32,128]{2,1,0:T(8,128)S(1)} %get-tuple-element.83.env_ref, f32[3,32,1024]{2,1,0:T(8,128)S(1)} %get-tuple-element.84.iso_ref, f32[72,128]{1,0:T(8,128)S(1)} %get-tuple-element.77.after_ref.mine_ref), custom_call_target="tpu_custom_call" | custom-call | flops 920000000 | bytes 1024 | tf_op jit(solution)/shard_map/pallas_call | solution.py:155
  36.9 1.4 %collective-permute-start.15 = (f32[32,512]{1,0:T(8,128)S(1)}, f32[32,512]{1,0:T(8,128)S(1)}, u32[]{:S(2)}, u32[]{:S(2)}) collective-permute-start(f32[32,512]{1,0:T(8,128)S(1)} %get-tuple-element.78.mine_ref), channel_id=1, source_target_pairs={{0,64},{4,68},{8,72},{12,76},{16,80},{20,84},{24,88},{28,92},{32,9... | collective-permute-start | bytes 196616 | tf_op jit(solution)/shard_map/ppermute | solution.py:421
  38.9 0.9 %shard_map.71 = (f32[72,128]{1,0:T(8,128)S(1)}, bf16[64,1024]{1,0:T(8,128)(2,1)S(1)}) custom-call(s32[1]{0:T(128)} %bitcast.9.upper_ref, bf16[64,1024]{1,0:T(8,128)(2,1)S(1)} %get-tuple-element.80.natural_ref, bf16[64,1024]{1,0:T(8,128)(2,1)S(1)} %get-tuple-element.81.moved_ref, bf16[64,1024]{1,0:T(8,128)(2,1)S(1)} %get-tuple-element.82.other_ref, ...), custom_call_target="tpu_custom_call" | custom-call | flops 1035000000 | bytes 1024 | tf_op jit(solution)/shard_map/pallas_call | solution.py:155
  40.5 2.3 %collective-permute-start.20 = (f32[16,512]{1,0:T(8,128)S(1)}, f32[16,512]{1,0:T(8,128)S(1)}, u32[]{:S(2)}, u32[]{:S(2)}) collective-permute-start(f32[16,512]{1,0:T(8,128)S(1)} %get-tuple-element.118), channel_id=1, source_target_pairs={{0,4},{4,0},{8,12},{12,8},{16,20},{20,16},{24,28},{28,24},{32,36},... | collective-permute-start | bytes 98312 | tf_op jit(solution)/shard_map/ppermute | solution.py:421
  43.0 2.0 %collective-permute-start.19 = (f32[32,512]{1,0:T(8,128)S(1)}, f32[32,512]{1,0:T(8,128)S(1)}, u32[]{:S(2)}, u32[]{:S(2)}) collective-permute-start(f32[32,512]{1,0:T(8,128)S(1)} %get-tuple-element.87.mine_ref), channel_id=1, source_target_pairs={{0,192},{4,196},{8,200},{12,204},{16,208},{20,212},{24,216},{28,22... | collective-permute-start | bytes 196616 | tf_op jit(solution)/shard_map/ppermute | solution.py:421
  44.9 0.7 %shard_map.73 = (bf16[64,1024]{1,0:T(8,128)(2,1)S(1)}, bf16[64,1024]{1,0:T(8,128)(2,1)S(1)}, bf16[256,256]{1,0:T(8,128)(2,1)S(1)}, bf16[64,1024]{1,0:T(8,128)(2,1)S(1)}) custom-call(s32[1]{0:T(128)} %bitcast.7.core_ref.upper_ref, s32[1]{0:T(128)} %bitcast.8.upper_ref, f32[32,512]{1,0:T(8,128)S(1)} %get-tuple-element.88.mine_ref, ...), custom_call_target="tpu_custom_call" | custom-call | flops 1150000 | bytes 1024 | tf_op jit(solution)/shard_map/pallas_call | solution.py:155
  45.7 0.9 %shard_map.74 = (f32[72,128]{1,0:T(8,128)S(1)}, bf16[64,1024]{1,0:T(8,128)(2,1)S(1)}) custom-call(s32[1]{0:T(128)} %bitcast.8.upper_ref, bf16[64,1024]{1,0:T(8,128)(2,1)S(1)} %get-tuple-element.89.natural_ref, bf16[64,1024]{1,0:T(8,128)(2,1)S(1)} %get-tuple-element.90.moved_ref, bf16[64,1024]{1,0:T(8,128)(2,1)S(1)} %get-tuple-element.91.other_ref, ...), custom_call_target="tpu_custom_call" | custom-call | flops 1035000000 | bytes 1024 | tf_op jit(solution)/shard_map/pallas_call | solution.py:155
  46.6 1.0 %collective-permute-start.25 = (f32[72,128]{1,0:T(8,128)S(1)}, f32[72,128]{1,0:T(8,128)S(1)}, u32[]{:S(2)}, u32[]{:S(2)}) collective-permute-start(f32[72,128]{1,0:T(8,128)S(1)} %get-tuple-element.92.after_ref.mine_ref), channel_id=1, source_target_pairs={{0,192},{4,196},{8,200},{12,204},{16,208},{20,212},{24,216},{28,22... | collective-permute-start | bytes 110600 | tf_op jit(solution)/shard_map/ppermute | solution.py:421
  47.6 0.8 %shard_map.78 = (bf16[2,256,256]{2,1,0:T(8,128)(2,1)S(1)}, bf16[2,64,1024]{2,1,0:T(8,128)(2,1)S(1)}) custom-call(f32[4,32,128]{2,1,0:T(8,128)S(1)} %tile.12.leaf_ref, f32[2,32,128]{2,1,0:T(8,128)S(1)} %get-tuple-element.83.env_ref, f32[3,32,1024]{2,1,0:T(8,128)S(1)} %get-tuple-element.84.iso_ref, f32[72,128]{1,0:T(8,128)S(1)} %get-tuple-element.92.after_ref.mine_ref), custom_call_target="tpu_custom_call" | custom-call | flops 920000000 | bytes 1024 | tf_op jit(solution)/shard_map/pallas_call | solution.py:155
  48.6 1.4 %collective-permute-start.23 = (f32[16,512]{1,0:T(8,128)S(1)}, f32[16,512]{1,0:T(8,128)S(1)}, u32[]{:S(2)}, u32[]{:S(2)}) collective-permute-start(f32[16,512]{1,0:T(8,128)S(1)} %get-tuple-element.116), channel_id=1, source_target_pairs={{0,4},{4,0},{8,12},{12,8},{16,20},{20,16},{24,28},{28,24},{32,36},... | collective-permute-start | bytes 98312 | tf_op jit(solution)/shard_map/ppermute | solution.py:421
  50.3 0.8 %shard_map.77 = (bf16[2,256,256]{2,1,0:T(8,128)(2,1)S(1)}, bf16[2,64,1024]{2,1,0:T(8,128)(2,1)S(1)}) custom-call(f32[4,32,128]{2,1,0:T(8,128)S(1)} %tile.12.leaf_ref, f32[2,32,128]{2,1,0:T(8,128)S(1)} %get-tuple-element.83.env_ref, f32[3,32,1024]{2,1,0:T(8,128)S(1)} %get-tuple-element.84.iso_ref, f32[72,128]{1,0:T(8,128)S(1)} %get-tuple-element.92.after_ref.mine_ref), custom_call_target="tpu_custom_call" | custom-call | flops 920000000 | bytes 1024 | tf_op jit(solution)/shard_map/pallas_call | solution.py:155
  51.2 0.9 %shard_map.76 = (bf16[64,1024]{1,0:T(8,128)(2,1)S(1)}, bf16[64,1024]{1,0:T(8,128)(2,1)S(1)}, bf16[256,256]{1,0:T(8,128)(2,1)S(1)}, bf16[64,1024]{1,0:T(8,128)(2,1)S(1)}) custom-call(s32[1]{0:T(128)} %bitcast.7.core_ref.upper_ref, s32[1]{0:T(128)} %bitcast.6.upper_ref, f32[32,512]{1,0:T(8,128)S(1)} %shard_map.75.mine_ref, ...), custom_call_target="tpu_custom_call" | custom-call | flops 1150000 | bytes 1024 | tf_op jit(solution)/shard_map/pallas_call | solution.py:155
  52.1 6.3 %shard_map.79 = (f32[4,1024]{1,0:T(4,128)}, f32[3,1,1024]{2,1,0:T(1,128)}, f32[1,1,1024]{2,1,0:T(1,128)}) custom-call(s32[6]{0:T(128)S(1)} %stack.36.marked_ref, s32[1]{0:T(128)} %bitcast.6.upper_ref, bf16[64,1024]{1,0:T(8,128)(2,1)S(1)} %get-tuple-element.93.natural_ref, bf16[64,1024]{1,0:T(8,128)(2,1)S(1)} %get-tuple-element.94.moved_ref, ...), custom_call_target="tpu_custom_call" | custom-call | flops 8049999872 | bytes 1024 | tf_op jit(solution)/shard_map/pallas_call | solution.py:155
  (59 shorter events, 6.1 us)
Async XLA Ops:
  0.6 0.9 %copy-start = (f32[1,8,1024]{2,1,0:T(8,128)S(1)}, f32[1,8,1024]{2,1,0:T(8,128)}, u32[]{:S(2)}) copy-start(f32[1,8,1024]{2,1,0:T(8,128)} %param.5) | copy-start | bytes 98308
  1.6 4.6 %copy-start.1 = (f32[1,4,1024]{2,1,0:T(4,128)S(1)}, f32[1,4,1024]{2,1,0:T(4,128)}, u32[]{:S(2)}) copy-start(f32[1,4,1024]{2,1,0:T(4,128)} %param.3) | copy-start | bytes 49156
  1.6 6.0 %collective-permute-start = (f32[4,8,1024]{2,1,0:T(8,128)S(1)}, f32[4,8,1024]{2,1,0:T(8,128)S(1)}, u32[]{:S(2)}, u32[]{:S(2)}) collective-permute-start(f32[4,8,1024]{2,1,0:T(8,128)S(1)} %constant_dynamic-update-slice_fusion.refs_0_), channel_id=1, source_target_pairs={{0,2},{1,3},{2,0},{3,1},{4,6},{5,7},{6,4},{7,5},{8,10},{9,11},{10,... | collective-permute-start | bytes 393224 | tf_op jit(solution)/shard_map/ppermute | solution.py:431
  5.2 7.5 %collective-permute-start.1 = (f32[4,8,1024]{2,1,0:T(8,128)S(1)}, f32[4,8,1024]{2,1,0:T(8,128)S(1)}, u32[]{:S(2)}, u32[]{:S(2)}) collective-permute-start(f32[4,8,1024]{2,1,0:T(8,128)S(1)} %constant_dynamic-update-slice_fusion.refs_0_), channel_id=1, source_target_pairs={{0,3},{1,2},{2,1},{3,0},{4,7},{5,6},{6,5},{7,4},{8,11},{9,10},{10,... | collective-permute-start | bytes 393224 | tf_op jit(solution)/shard_map/ppermute | solution.py:431
  6.1 6.7 %collective-permute-start.2 = (f32[4,8,1024]{2,1,0:T(8,128)S(1)}, f32[4,8,1024]{2,1,0:T(8,128)S(1)}, u32[]{:S(2)}, u32[]{:S(2)}) collective-permute-start(f32[4,8,1024]{2,1,0:T(8,128)S(1)} %constant_dynamic-update-slice_fusion.refs_0_), channel_id=1, source_target_pairs={{0,1},{1,0},{2,3},{3,2},{4,5},{5,4},{6,7},{7,6},{8,9},{9,8},{10,11... | collective-permute-start | bytes 393224 | tf_op jit(solution)/shard_map/ppermute | solution.py:431
  12.8 4.5 %collective-permute-start.7 = (f32[16,512]{1,0:T(8,128)S(1)}, f32[16,512]{1,0:T(8,128)S(1)}, u32[]{:S(2)}, u32[]{:S(2)}) collective-permute-start(f32[16,512]{1,0:T(8,128)S(1)} %get-tuple-element.124), channel_id=1, source_target_pairs={{0,4},{4,0},{8,12},{12,8},{16,20},{20,16},{24,28},{28,24},{32,36},... | collective-permute-start | bytes 98312 | tf_op jit(solution)/shard_map/ppermute | solution.py:421
  13.9 3.5 %collective-permute-start.8 = (f32[16,512]{1,0:T(8,128)S(1)}, f32[16,512]{1,0:T(8,128)S(1)}, u32[]{:S(2)}, u32[]{:S(2)}) collective-permute-start(f32[16,512]{1,0:T(8,128)S(1)} %get-tuple-element.123), channel_id=1, source_target_pairs={{0,4},{4,0},{8,12},{12,8},{16,20},{20,16},{24,28},{28,24},{32,36},... | collective-permute-start | bytes 98312 | tf_op jit(solution)/shard_map/ppermute | solution.py:421
  14.0 3.9 %collective-permute-start.3 = (f32[32,512]{1,0:T(8,128)S(1)}, f32[32,512]{1,0:T(8,128)S(1)}, u32[]{:S(2)}, u32[]{:S(2)}) collective-permute-start(f32[32,512]{1,0:T(8,128)S(1)} %get-tuple-element.59.mine_ref), channel_id=1, source_target_pairs={{0,8},{4,12},{8,0},{12,4},{16,24},{20,28},{24,16},{28,20},{32,40},... | collective-permute-start | bytes 196616 | tf_op jit(solution)/shard_map/ppermute | solution.py:421
  16.6 1.6 %collective-permute-start.9 = (f32[72,128]{1,0:T(8,128)S(1)}, f32[72,128]{1,0:T(8,128)S(1)}, u32[]{:S(2)}, u32[]{:S(2)}) collective-permute-start(f32[72,128]{1,0:T(8,128)S(1)} %get-tuple-element.60.after_ref.mine_ref), channel_id=1, source_target_pairs={{0,4},{4,0},{8,12},{12,8},{16,20},{20,16},{24,28},{28,24},{32,36},... | collective-permute-start | bytes 110600 | tf_op jit(solution)/shard_map/ppermute | solution.py:421
  19.1 5.2 %collective-permute-start.10 = (f32[72,128]{1,0:T(8,128)S(1)}, f32[72,128]{1,0:T(8,128)S(1)}, u32[]{:S(2)}, u32[]{:S(2)}) collective-permute-start(f32[72,128]{1,0:T(8,128)S(1)} %get-tuple-element.70.mine_ref), channel_id=1, source_target_pairs={{0,8},{4,12},{8,0},{12,4},{16,24},{20,28},{24,16},{28,20},{32,40},... | collective-permute-start | bytes 110600 | tf_op jit(solution)/shard_map/ppermute | solution.py:421
  20.0 3.7 %collective-permute-start.5 = (f32[16,512]{1,0:T(8,128)S(1)}, f32[16,512]{1,0:T(8,128)S(1)}, u32[]{:S(2)}, u32[]{:S(2)}) collective-permute-start(f32[16,512]{1,0:T(8,128)S(1)} %get-tuple-element.126), channel_id=1, source_target_pairs={{0,4},{4,0},{8,12},{12,8},{16,20},{20,16},{24,28},{28,24},{32,36},... | collective-permute-start | bytes 98312 | tf_op jit(solution)/shard_map/ppermute | solution.py:421
  20.6 3.1 %collective-permute-start.6 = (f32[16,512]{1,0:T(8,128)S(1)}, f32[16,512]{1,0:T(8,128)S(1)}, u32[]{:S(2)}, u32[]{:S(2)}) collective-permute-start(f32[16,512]{1,0:T(8,128)S(1)} %get-tuple-element.125), channel_id=1, source_target_pairs={{0,4},{4,0},{8,12},{12,8},{16,20},{20,16},{24,28},{28,24},{32,36},... | collective-permute-start | bytes 98312 | tf_op jit(solution)/shard_map/ppermute | solution.py:421
  20.7 6.6 %collective-permute-start.4 = (f32[32,512]{1,0:T(8,128)S(1)}, f32[32,512]{1,0:T(8,128)S(1)}, u32[]{:S(2)}, u32[]{:S(2)}) collective-permute-start(f32[32,512]{1,0:T(8,128)S(1)} %get-tuple-element.61.mine_ref), channel_id=1, source_target_pairs={{0,16},{4,20},{8,24},{12,28},{16,0},{20,4},{24,8},{28,12},{32,48},... | collective-permute-start | bytes 196616 | tf_op jit(solution)/shard_map/ppermute | solution.py:421
  25.1 7.1 %collective-permute-start.14 = (f32[72,128]{1,0:T(8,128)S(1)}, f32[72,128]{1,0:T(8,128)S(1)}, u32[]{:S(2)}, u32[]{:S(2)}) collective-permute-start(f32[72,128]{1,0:T(8,128)S(1)} %get-tuple-element.71.after_ref.mine_ref), channel_id=1, source_target_pairs={{0,16},{4,20},{8,24},{12,28},{16,0},{20,4},{24,8},{28,12},{32,48},... | collective-permute-start | bytes 110600 | tf_op jit(solution)/shard_map/ppermute | solution.py:421
  27.4 4.3 %collective-permute-start.12 = (f32[16,512]{1,0:T(8,128)S(1)}, f32[16,512]{1,0:T(8,128)S(1)}, u32[]{:S(2)}, u32[]{:S(2)}) collective-permute-start(f32[16,512]{1,0:T(8,128)S(1)} %get-tuple-element.122), channel_id=1, source_target_pairs={{0,4},{4,0},{8,12},{12,8},{16,20},{20,16},{24,28},{28,24},{32,36},... | collective-permute-start | bytes 98312 | tf_op jit(solution)/shard_map/ppermute | solution.py:421
  28.3 3.4 %collective-permute-start.13 = (f32[16,512]{1,0:T(8,128)S(1)}, f32[16,512]{1,0:T(8,128)S(1)}, u32[]{:S(2)}, u32[]{:S(2)}) collective-permute-start(f32[16,512]{1,0:T(8,128)S(1)} %get-tuple-element.121), channel_id=1, source_target_pairs={{0,4},{4,0},{8,12},{12,8},{16,20},{20,16},{24,28},{28,24},{32,36},... | collective-permute-start | bytes 98312 | tf_op jit(solution)/shard_map/ppermute | solution.py:421
  28.4 5.9 %collective-permute-start.11 = (f32[32,512]{1,0:T(8,128)S(1)}, f32[32,512]{1,0:T(8,128)S(1)}, u32[]{:S(2)}, u32[]{:S(2)}) collective-permute-start(f32[32,512]{1,0:T(8,128)S(1)} %get-tuple-element.72.mine_ref), channel_id=1, source_target_pairs={{0,48},{4,52},{8,56},{12,60},{16,32},{20,36},{24,40},{28,44},{32,1... | collective-permute-start | bytes 196616 | tf_op jit(solution)/shard_map/ppermute | solution.py:421
  33.0 5.8 %collective-permute-start.18 = (f32[72,128]{1,0:T(8,128)S(1)}, f32[72,128]{1,0:T(8,128)S(1)}, u32[]{:S(2)}, u32[]{:S(2)}) collective-permute-start(f32[72,128]{1,0:T(8,128)S(1)} %get-tuple-element.77.after_ref.mine_ref), channel_id=1, source_target_pairs={{0,48},{4,52},{8,56},{12,60},{16,32},{20,36},{24,40},{28,44},{32,1... | collective-permute-start | bytes 110600 | tf_op jit(solution)/shard_map/ppermute | solution.py:421
  34.4 3.9 %collective-permute-start.16 = (f32[16,512]{1,0:T(8,128)S(1)}, f32[16,512]{1,0:T(8,128)S(1)}, u32[]{:S(2)}, u32[]{:S(2)}) collective-permute-start(f32[16,512]{1,0:T(8,128)S(1)} %get-tuple-element.120), channel_id=1, source_target_pairs={{0,4},{4,0},{8,12},{12,8},{16,20},{20,16},{24,28},{28,24},{32,36},... | collective-permute-start | bytes 98312 | tf_op jit(solution)/shard_map/ppermute | solution.py:421
  35.9 2.3 %collective-permute-start.17 = (f32[16,512]{1,0:T(8,128)S(1)}, f32[16,512]{1,0:T(8,128)S(1)}, u32[]{:S(2)}, u32[]{:S(2)}) collective-permute-start(f32[16,512]{1,0:T(8,128)S(1)} %get-tuple-element.119), channel_id=1, source_target_pairs={{0,4},{4,0},{8,12},{12,8},{16,20},{20,16},{24,28},{28,24},{32,36},... | collective-permute-start | bytes 98312 | tf_op jit(solution)/shard_map/ppermute | solution.py:421
  36.9 3.4 %collective-permute-start.15 = (f32[32,512]{1,0:T(8,128)S(1)}, f32[32,512]{1,0:T(8,128)S(1)}, u32[]{:S(2)}, u32[]{:S(2)}) collective-permute-start(f32[32,512]{1,0:T(8,128)S(1)} %get-tuple-element.78.mine_ref), channel_id=1, source_target_pairs={{0,64},{4,68},{8,72},{12,76},{16,80},{20,84},{24,88},{28,92},{32,9... | collective-permute-start | bytes 196616 | tf_op jit(solution)/shard_map/ppermute | solution.py:421
  39.7 5.9 %collective-permute-start.22 = (f32[72,128]{1,0:T(8,128)S(1)}, f32[72,128]{1,0:T(8,128)S(1)}, u32[]{:S(2)}, u32[]{:S(2)}) collective-permute-start(f32[72,128]{1,0:T(8,128)S(1)} %get-tuple-element.86.after_ref.mine_ref), channel_id=1, source_target_pairs={{0,64},{4,68},{8,72},{12,76},{16,80},{20,84},{24,88},{28,92},{32,9... | collective-permute-start | bytes 110600 | tf_op jit(solution)/shard_map/ppermute | solution.py:421
  40.5 4.5 %collective-permute-start.20 = (f32[16,512]{1,0:T(8,128)S(1)}, f32[16,512]{1,0:T(8,128)S(1)}, u32[]{:S(2)}, u32[]{:S(2)}) collective-permute-start(f32[16,512]{1,0:T(8,128)S(1)} %get-tuple-element.118), channel_id=1, source_target_pairs={{0,4},{4,0},{8,12},{12,8},{16,20},{20,16},{24,28},{28,24},{32,36},... | collective-permute-start | bytes 98312 | tf_op jit(solution)/shard_map/ppermute | solution.py:421
  42.7 2.2 %collective-permute-start.21 = (f32[16,512]{1,0:T(8,128)S(1)}, f32[16,512]{1,0:T(8,128)S(1)}, u32[]{:S(2)}, u32[]{:S(2)}) collective-permute-start(f32[16,512]{1,0:T(8,128)S(1)} %get-tuple-element.117), channel_id=1, source_target_pairs={{0,4},{4,0},{8,12},{12,8},{16,20},{20,16},{24,28},{28,24},{32,36},... | collective-permute-start | bytes 98312 | tf_op jit(solution)/shard_map/ppermute | solution.py:421
  43.0 5.4 %collective-permute-start.19 = (f32[32,512]{1,0:T(8,128)S(1)}, f32[32,512]{1,0:T(8,128)S(1)}, u32[]{:S(2)}, u32[]{:S(2)}) collective-permute-start(f32[32,512]{1,0:T(8,128)S(1)} %get-tuple-element.87.mine_ref), channel_id=1, source_target_pairs={{0,192},{4,196},{8,200},{12,204},{16,208},{20,212},{24,216},{28,22... | collective-permute-start | bytes 196616 | tf_op jit(solution)/shard_map/ppermute | solution.py:421
  46.6 5.5 %collective-permute-start.25 = (f32[72,128]{1,0:T(8,128)S(1)}, f32[72,128]{1,0:T(8,128)S(1)}, u32[]{:S(2)}, u32[]{:S(2)}) collective-permute-start(f32[72,128]{1,0:T(8,128)S(1)} %get-tuple-element.92.after_ref.mine_ref), channel_id=1, source_target_pairs={{0,192},{4,196},{8,200},{12,204},{16,208},{20,212},{24,216},{28,22... | collective-permute-start | bytes 110600 | tf_op jit(solution)/shard_map/ppermute | solution.py:421
  48.6 2.5 %collective-permute-start.23 = (f32[16,512]{1,0:T(8,128)S(1)}, f32[16,512]{1,0:T(8,128)S(1)}, u32[]{:S(2)}, u32[]{:S(2)}) collective-permute-start(f32[16,512]{1,0:T(8,128)S(1)} %get-tuple-element.116), channel_id=1, source_target_pairs={{0,4},{4,0},{8,12},{12,8},{16,20},{20,16},{24,28},{28,24},{32,36},... | collective-permute-start | bytes 98312 | tf_op jit(solution)/shard_map/ppermute | solution.py:421
  50.0 1.2 %collective-permute-start.24 = (f32[16,512]{1,0:T(8,128)S(1)}, f32[16,512]{1,0:T(8,128)S(1)}, u32[]{:S(2)}, u32[]{:S(2)}) collective-permute-start(f32[16,512]{1,0:T(8,128)S(1)} %get-tuple-element.115), channel_id=1, source_target_pairs={{0,4},{4,0},{8,12},{12,8},{16,20},{20,16},{24,28},{28,24},{32,36},... | collective-permute-start | bytes 98312 | tf_op jit(solution)/shard_map/ppermute | solution.py:421

commit v4 on v3

--- a/solution.py
+++ b/solution.py
@@ -217,18 +217,24 @@
 
 def merge_kernel(width, upper_ref, mine_ref, theirs_ref, after_ref, now_ref, *later_refs):
     upper = upper_ref[0] == 1
-    mine = [mine_ref[:, LANES * c : LANES * (c + 1)] for c in range(CHUNKS // 2)]
-    theirs = [theirs_ref[:, LANES * c : LANES * (c + 1)] for c in range(CHUNKS // 2)]
+    parts = mine_ref.shape[1] // LANES
+    mine = [mine_ref[:, LANES * c : LANES * (c + 1)] for c in range(parts)]
+    theirs = [theirs_ref[:, LANES * c : LANES * (c + 1)] for c in range(parts)]
     low = [jnp.where(upper, t, m) for m, t in zip(mine, theirs)]
     high = [jnp.where(upper, m, t) for m, t in zip(mine, theirs)]
     for parity, out_ref in enumerate((now_ref, *later_refs)):
-        out = every_other(low, width, parity) + every_other(high, width, parity)
+        if later_refs:
+            out = every_other(low, width, parity) + every_other(high, width, parity)
+        else:
+            out = low + high
+        if out_ref.shape[1] == CHI2 // 4:
+            out = every_other(out, width // 2, 0)
         for c, chunk in enumerate(out):
             out_ref[:, LANES * c : LANES * (c + 1)] = chunk
 
 
-def merge(width, upper, mine, theirs, after, last):
-    outs = [shape_of(*HALF)] * (1 if last else 2)
+def merge(width, upper, mine, theirs, after, later_columns):
+    outs = [shape_of(*HALF)] + [shape_of(CHI, later_columns)] * (later_columns > 0)
     return kernel_call(
         functools.partial(merge_kernel, width), outs, (upper,), (mine, theirs, after), [], 300
     )
@@ -466,7 +472,7 @@
             owns.append(own)
             break
         if level == 0:
-            early = merge(CHI2 >> 2, bits[1], later, incoming, message, False)
+            early = merge(CHI2 >> 2, bits[1], later, incoming, message, CHI2 // 2)
             before = early[:1]
         elif level == 3:
             local_edges_2 = local_edges(2, leaves, local_envs, local_whole, message)
@@ -479,7 +485,8 @@
             if level == 0:
                 now, *rest = early
             else:
-                now, *rest = merge(CHI2 >> level + 2, bits[level + 1], later, incoming, message, last)
+                columns = 0 if last else CHI2 // 4 if level + 3 == top_levels else CHI2 // 2
+                now, *rest = merge(CHI2 >> level + 2, bits[level + 1], later, incoming, message, columns)
             later = None if last else rest[0]
         owns.append(own)
         partners.append(partner)

time: 58.5 us -> 58.6 us (level)
  no operation moved by 1% of the time
where the time goes in v4:
time: 58.6 us; the launch traced here: 58.2 us
  starting transfers between devices  28.9 us (49%)
  Pallas kernels  19.1 us (33%)
  waiting for transfers between devices  7.79 us (13%)
  local copies, waits for them, and re-layouts  1.36 us (2%)
  between operations  0.93 us (2%)
    ppermute x23, starting transfers between devices, exchange(): return lax.ppermute(value, 'leaf', pairs)  24.4 us
    pallas_call x22, Pallas kernels, kernel_call(): pl.pallas_call(kernel, out_shape=outs, in_specs=[scalar_spec()] * len(sca...  19.1 us
    ppermute x3, waiting for transfers between devices, bond_pieces(): lax.ppermute(value, 'bond', [(source, source ^ mask) for source in range(...  6.36 us
    ppermute x3, starting transfers between devices, bond_pieces(): lax.ppermute(value, 'bond', [(source, source ^ mask) for source in range(...  4.52 us
    ppermute x23, waiting for transfers between devices, exchange(): return lax.ppermute(value, 'leaf', pairs)  1.44 us
  transfers between devices with their start and end apart: 26, of which 4 were waited for; matrix products, arithmetic and copies ran while one was open for 1% of the time, Pallas kernels for 21%

profile of v4, /device:TPU:1, one launch (start us, length us, event | category | flops | bytes accessed | tf_op | source)
XLA Modules:
  0.0 58.2 jit_solution(15116860566145473050)
XLA Ops:
  0.6 0.9 %constant_dynamic-update-slice_fusion.1 = f32[4,8,1024]{2,1,0:T(8,128)S(1)} fusion(f32[3,8,1024]{2,1,0:T(8,128)} %param.4), kind=kLoop, calls=%fused_computation.1 | loop fusion | bytes 196608
  1.6 3.7 %collective-permute-start = (f32[4,8,1024]{2,1,0:T(8,128)S(1)}, f32[4,8,1024]{2,1,0:T(8,128)S(1)}, u32[]{:S(2)}, u32[]{:S(2)}) collective-permute-start(f32[4,8,1024]{2,1,0:T(8,128)S(1)} %constant_dynamic-update-slice_fusion.refs_0_), channel_id=1, source_target_pairs={{0,2},{1,3},{2,0},{3,1},{4,6},{5,7},{6,4},{7,5},{8,10},{9,11},{10,... | collective-permute-start | bytes 393224 | tf_op jit(solution)/shard_map/ppermute | solution.py:437
  5.2 0.9 %collective-permute-start.1 = (f32[4,8,1024]{2,1,0:T(8,128)S(1)}, f32[4,8,1024]{2,1,0:T(8,128)S(1)}, u32[]{:S(2)}, u32[]{:S(2)}) collective-permute-start(f32[4,8,1024]{2,1,0:T(8,128)S(1)} %constant_dynamic-update-slice_fusion.refs_0_), channel_id=1, source_target_pairs={{0,3},{1,2},{2,1},{3,0},{4,7},{5,6},{6,5},{7,4},{8,11},{9,10},{10,... | collective-permute-start | bytes 393224 | tf_op jit(solution)/shard_map/ppermute | solution.py:437
  6.4 1.2 %collective-permute-done.refs_1_ = f32[4,8,1024]{2,1,0:T(8,128)S(1)} collective-permute-done((f32[4,8,1024]{2,1,0:T(8,128)S(1)}, f32[4,8,1024]{2,1,0:T(8,128)S(1)}, u32[]{:S(2)}, u32[]{:S(2)}) %collective-permute-start) | collective-permute-done | bytes 131104 | tf_op jit(solution)/shard_map/ppermute | solution.py:437
  7.6 5.2 %collective-permute-done.1.refs_2_ = f32[4,8,1024]{2,1,0:T(8,128)S(1)} collective-permute-done((f32[4,8,1024]{2,1,0:T(8,128)S(1)}, f32[4,8,1024]{2,1,0:T(8,128)S(1)}, u32[]{:S(2)}, u32[]{:S(2)}) %collective-permute-start.1) | collective-permute-done | bytes 131104 | tf_op jit(solution)/shard_map/ppermute | solution.py:437
  12.8 1.1 %collective-permute-start.7 = (f32[16,512]{1,0:T(8,128)S(1)}, f32[16,512]{1,0:T(8,128)S(1)}, u32[]{:S(2)}, u32[]{:S(2)}) collective-permute-start(f32[16,512]{1,0:T(8,128)S(1)} %get-tuple-element.124), channel_id=1, source_target_pairs={{0,4},{4,0},{8,12},{12,8},{16,20},{20,16},{24,28},{28,24},{32,36},... | collective-permute-start | bytes 98312 | tf_op jit(solution)/shard_map/ppermute | solution.py:427
  14.7 2.0 %shard_map.59 = (f32[3,32,1024]{2,1,0:T(8,128)S(1)}, f32[2,32,128]{2,1,0:T(8,128)S(1)}, f32[72,128]{1,0:T(8,128)S(1)}) custom-call(s32[1]{0:T(128)} %bitcast.12.bond_ref, f32[4,32,128]{2,1,0:T(8,128)S(1)} %tile.12.leaf_ref, f32[4,8,1024]{2,1,0:T(8,128)S(1)} %constant_dynamic-update-slice_fusion.refs_0_, f32[4,8,1024]{2,1,0:T(8,128)S(1)} %collective-permute-done.refs_1_, ...), custom_call_target="tpu_custom_call" | custom-call | flops 2070000000 | bytes 1024 | tf_op jit(solution)/shard_map/pallas_call | solution.py:155
  16.6 0.7 %collective-permute-start.9 = (f32[72,128]{1,0:T(8,128)S(1)}, f32[72,128]{1,0:T(8,128)S(1)}, u32[]{:S(2)}, u32[]{:S(2)}) collective-permute-start(f32[72,128]{1,0:T(8,128)S(1)} %get-tuple-element.60.after_ref.mine_ref), channel_id=1, source_target_pairs={{0,4},{4,0},{8,12},{12,8},{16,20},{20,16},{24,28},{28,24},{32,36},... | collective-permute-start | bytes 110600 | tf_op jit(solution)/shard_map/ppermute | solution.py:427
  18.2 0.9 %shard_map.63 = (f32[72,128]{1,0:T(8,128)S(1)}, bf16[64,1024]{1,0:T(8,128)(2,1)S(1)}) custom-call(s32[1]{0:T(128)} %bitcast.7.core_ref.upper_ref, bf16[64,1024]{1,0:T(8,128)(2,1)S(1)} %get-tuple-element.67.natural_ref, bf16[64,1024]{1,0:T(8,128)(2,1)S(1)} %get-tuple-element.68.moved_ref, bf16[64,1024]{1,0:T(8,128)(2,1)S(1)} %get-tuple-element.69.other_ref, ...), custom_call_target="tpu_custom_call" | custom-call | flops 1035000000 | bytes 1024 | tf_op jit(solution)/shard_map/pallas_call | solution.py:155
  19.1 0.9 %collective-permute-start.10 = (f32[72,128]{1,0:T(8,128)S(1)}, f32[72,128]{1,0:T(8,128)S(1)}, u32[]{:S(2)}, u32[]{:S(2)}) collective-permute-start(f32[72,128]{1,0:T(8,128)S(1)} %get-tuple-element.70.mine_ref), channel_id=1, source_target_pairs={{0,8},{4,12},{8,0},{12,4},{16,24},{20,28},{24,16},{28,20},{32,40},... | collective-permute-start | bytes 110600 | tf_op jit(solution)/shard_map/ppermute | solution.py:427
  20.7 3.0 %collective-permute-start.4 = (f32[32,512]{1,0:T(8,128)S(1)}, f32[32,512]{1,0:T(8,128)S(1)}, u32[]{:S(2)}, u32[]{:S(2)}) collective-permute-start(f32[32,512]{1,0:T(8,128)S(1)} %get-tuple-element.61.mine_ref), channel_id=1, source_target_pairs={{0,16},{4,20},{8,24},{12,28},{16,0},{20,4},{24,8},{28,12},{32,48},... | collective-permute-start | bytes 196616 | tf_op jit(solution)/shard_map/ppermute | solution.py:427
  24.2 0.9 %shard_map.64 = (f32[72,128]{1,0:T(8,128)S(1)}, bf16[64,1024]{1,0:T(8,128)(2,1)S(1)}) custom-call(s32[1]{0:T(128)} %bitcast.11.upper_ref, bf16[64,1024]{1,0:T(8,128)(2,1)S(1)} %get-tuple-element.63.natural_ref, bf16[64,1024]{1,0:T(8,128)(2,1)S(1)} %get-tuple-element.64.moved_ref, bf16[64,1024]{1,0:T(8,128)(2,1)S(1)} %get-tuple-element.65.other_ref, ...), custom_call_target="tpu_custom_call" | custom-call | flops 1035000000 | bytes 1024 | tf_op jit(solution)/shard_map/pallas_call | solution.py:155
  25.1 1.2 %collective-permute-start.14 = (f32[72,128]{1,0:T(8,128)S(1)}, f32[72,128]{1,0:T(8,128)S(1)}, u32[]{:S(2)}, u32[]{:S(2)}) collective-permute-start(f32[72,128]{1,0:T(8,128)S(1)} %get-tuple-element.71.after_ref.mine_ref), channel_id=1, source_target_pairs={{0,16},{4,20},{8,24},{12,28},{16,0},{20,4},{24,8},{28,12},{32,48},... | collective-permute-start | bytes 110600 | tf_op jit(solution)/shard_map/ppermute | solution.py:427
  26.3 1.0 %collective-permute-done.4.theirs_ref = f32[32,512]{1,0:T(8,128)S(1)} collective-permute-done((f32[32,512]{1,0:T(8,128)S(1)}, f32[32,512]{1,0:T(8,128)S(1)}, u32[]{:S(2)}, u32[]{:S(2)}) %collective-permute-start.4) | collective-permute-done | bytes 65568 | tf_op jit(solution)/shard_map/ppermute | solution.py:427
  27.4 0.9 %collective-permute-start.12 = (f32[16,512]{1,0:T(8,128)S(1)}, f32[16,512]{1,0:T(8,128)S(1)}, u32[]{:S(2)}, u32[]{:S(2)}) collective-permute-start(f32[16,512]{1,0:T(8,128)S(1)} %get-tuple-element.122), channel_id=1, source_target_pairs={{0,4},{4,0},{8,12},{12,8},{16,20},{20,16},{24,28},{28,24},{32,36},... | collective-permute-start | bytes 98312 | tf_op jit(solution)/shard_map/ppermute | solution.py:427
  28.4 3.3 %collective-permute-start.11 = (f32[32,512]{1,0:T(8,128)S(1)}, f32[32,512]{1,0:T(8,128)S(1)}, u32[]{:S(2)}, u32[]{:S(2)}) collective-permute-start(f32[32,512]{1,0:T(8,128)S(1)} %get-tuple-element.72.mine_ref), channel_id=1, source_target_pairs={{0,48},{4,52},{8,56},{12,60},{16,32},{20,36},{24,40},{28,44},{32,1... | collective-permute-start | bytes 196616 | tf_op jit(solution)/shard_map/ppermute | solution.py:427
  32.2 0.9 %shard_map.67 = (f32[72,128]{1,0:T(8,128)S(1)}, bf16[64,1024]{1,0:T(8,128)(2,1)S(1)}) custom-call(s32[1]{0:T(128)} %bitcast.10.upper_ref, bf16[64,1024]{1,0:T(8,128)(2,1)S(1)} %get-tuple-element.74.natural_ref, bf16[64,1024]{1,0:T(8,128)(2,1)S(1)} %get-tuple-element.75.moved_ref, bf16[64,1024]{1,0:T(8,128)(2,1)S(1)} %get-tuple-element.76.other_ref, ...), custom_call_target="tpu_custom_call" | custom-call | flops 1035000000 | bytes 1024 | tf_op jit(solution)/shard_map/pallas_call | solution.py:155
  33.0 1.2 %collective-permute-start.18 = (f32[72,128]{1,0:T(8,128)S(1)}, f32[72,128]{1,0:T(8,128)S(1)}, u32[]{:S(2)}, u32[]{:S(2)}) collective-permute-start(f32[72,128]{1,0:T(8,128)S(1)} %get-tuple-element.77.after_ref.mine_ref), channel_id=1, source_target_pairs={{0,48},{4,52},{8,56},{12,60},{16,32},{20,36},{24,40},{28,44},{32,1... | collective-permute-start | bytes 110600 | tf_op jit(solution)/shard_map/ppermute | solution.py:427
  34.4 1.6 %collective-permute-start.16 = (f32[16,512]{1,0:T(8,128)S(1)}, f32[16,512]{1,0:T(8,128)S(1)}, u32[]{:S(2)}, u32[]{:S(2)}) collective-permute-start(f32[16,512]{1,0:T(8,128)S(1)} %get-tuple-element.120), channel_id=1, source_target_pairs={{0,4},{4,0},{8,12},{12,8},{16,20},{20,16},{24,28},{28,24},{32,36},... | collective-permute-start | bytes 98312 | tf_op jit(solution)/shard_map/ppermute | solution.py:427
  36.0 0.8 %shard_map.70 = (bf16[2,256,256]{2,1,0:T(8,128)(2,1)S(1)}, bf16[2,64,1024]{2,1,0:T(8,128)(2,1)S(1)}) custom-call(f32[4,32,128]{2,1,0:T(8,128)S(1)} %tile.12.leaf_ref, f32[2,32,128]{2,1,0:T(8,128)S(1)} %get-tuple-element.83.env_ref, f32[3,32,1024]{2,1,0:T(8,128)S(1)} %get-tuple-element.84.iso_ref, f32[72,128]{1,0:T(8,128)S(1)} %get-tuple-element.77.after_ref.mine_ref), custom_call_target="tpu_custom_call" | custom-call | flops 920000000 | bytes 1024 | tf_op jit(solution)/shard_map/pallas_call | solution.py:155
  36.9 1.4 %collective-permute-start.15 = (f32[32,512]{1,0:T(8,128)S(1)}, f32[32,512]{1,0:T(8,128)S(1)}, u32[]{:S(2)}, u32[]{:S(2)}) collective-permute-start(f32[32,512]{1,0:T(8,128)S(1)} %get-tuple-element.78.mine_ref), channel_id=1, source_target_pairs={{0,64},{4,68},{8,72},{12,76},{16,80},{20,84},{24,88},{28,92},{32,9... | collective-permute-start | bytes 196616 | tf_op jit(solution)/shard_map/ppermute | solution.py:427
  38.9 0.9 %shard_map.71 = (f32[72,128]{1,0:T(8,128)S(1)}, bf16[64,1024]{1,0:T(8,128)(2,1)S(1)}) custom-call(s32[1]{0:T(128)} %bitcast.9.upper_ref, bf16[64,1024]{1,0:T(8,128)(2,1)S(1)} %get-tuple-element.80.natural_ref, bf16[64,1024]{1,0:T(8,128)(2,1)S(1)} %get-tuple-element.81.moved_ref, bf16[64,1024]{1,0:T(8,128)(2,1)S(1)} %get-tuple-element.82.other_ref, ...), custom_call_target="tpu_custom_call" | custom-call | flops 1035000000 | bytes 1024 | tf_op jit(solution)/shard_map/pallas_call | solution.py:155
  40.6 2.3 %collective-permute-start.20 = (f32[16,512]{1,0:T(8,128)S(1)}, f32[16,512]{1,0:T(8,128)S(1)}, u32[]{:S(2)}, u32[]{:S(2)}) collective-permute-start(f32[16,512]{1,0:T(8,128)S(1)} %get-tuple-element.118), channel_id=1, source_target_pairs={{0,4},{4,0},{8,12},{12,8},{16,20},{20,16},{24,28},{28,24},{32,36},... | collective-permute-start | bytes 98312 | tf_op jit(solution)/shard_map/ppermute | solution.py:427
  43.1 2.0 %collective-permute-start.19 = (f32[32,256]{1,0:T(8,128)S(1)}, f32[32,256]{1,0:T(8,128)S(1)}, u32[]{:S(2)}, u32[]{:S(2)}) collective-permute-start(f32[32,256]{1,0:T(8,128)S(1)} %get-tuple-element.87.mine_ref), channel_id=1, source_target_pairs={{0,192},{4,196},{8,200},{12,204},{16,208},{20,212},{24,216},{28,22... | collective-permute-start | bytes 98312 | tf_op jit(solution)/shard_map/ppermute | solution.py:427
  45.0 0.7 %shard_map.73 = (bf16[64,1024]{1,0:T(8,128)(2,1)S(1)}, bf16[64,1024]{1,0:T(8,128)(2,1)S(1)}, bf16[256,256]{1,0:T(8,128)(2,1)S(1)}, bf16[64,1024]{1,0:T(8,128)(2,1)S(1)}) custom-call(s32[1]{0:T(128)} %bitcast.7.core_ref.upper_ref, s32[1]{0:T(128)} %bitcast.8.upper_ref, f32[32,512]{1,0:T(8,128)S(1)} %get-tuple-element.88.mine_ref, ...), custom_call_target="tpu_custom_call" | custom-call | flops 1150000 | bytes 1024 | tf_op jit(solution)/shard_map/pallas_call | solution.py:155
  45.8 0.9 %shard_map.74 = (f32[72,128]{1,0:T(8,128)S(1)}, bf16[64,1024]{1,0:T(8,128)(2,1)S(1)}) custom-call(s32[1]{0:T(128)} %bitcast.8.upper_ref, bf16[64,1024]{1,0:T(8,128)(2,1)S(1)} %get-tuple-element.89.natural_ref, bf16[64,1024]{1,0:T(8,128)(2,1)S(1)} %get-tuple-element.90.moved_ref, bf16[64,1024]{1,0:T(8,128)(2,1)S(1)} %get-tuple-element.91.other_ref, ...), custom_call_target="tpu_custom_call" | custom-call | flops 1035000000 | bytes 1024 | tf_op jit(solution)/shard_map/pallas_call | solution.py:155
  46.7 0.8 %shard_map.78 = (bf16[2,256,256]{2,1,0:T(8,128)(2,1)S(1)}, bf16[2,64,1024]{2,1,0:T(8,128)(2,1)S(1)}) custom-call(f32[4,32,128]{2,1,0:T(8,128)S(1)} %tile.12.leaf_ref, f32[2,32,128]{2,1,0:T(8,128)S(1)} %get-tuple-element.83.env_ref, f32[3,32,1024]{2,1,0:T(8,128)S(1)} %get-tuple-element.84.iso_ref, f32[72,128]{1,0:T(8,128)S(1)} %get-tuple-element.92.after_ref.mine_ref), custom_call_target="tpu_custom_call" | custom-call | flops 920000000 | bytes 1024 | tf_op jit(solution)/shard_map/pallas_call | solution.py:155
  47.5 1.0 %collective-permute-start.25 = (f32[72,128]{1,0:T(8,128)S(1)}, f32[72,128]{1,0:T(8,128)S(1)}, u32[]{:S(2)}, u32[]{:S(2)}) collective-permute-start(f32[72,128]{1,0:T(8,128)S(1)} %get-tuple-element.92.after_ref.mine_ref), channel_id=1, source_target_pairs={{0,192},{4,196},{8,200},{12,204},{16,208},{20,212},{24,216},{28,22... | collective-permute-start | bytes 110600 | tf_op jit(solution)/shard_map/ppermute | solution.py:427
  48.5 1.3 %collective-permute-start.23 = (f32[16,512]{1,0:T(8,128)S(1)}, f32[16,512]{1,0:T(8,128)S(1)}, u32[]{:S(2)}, u32[]{:S(2)}) collective-permute-start(f32[16,512]{1,0:T(8,128)S(1)} %get-tuple-element.116), channel_id=1, source_target_pairs={{0,4},{4,0},{8,12},{12,8},{16,20},{20,16},{24,28},{28,24},{32,36},... | collective-permute-start | bytes 98312 | tf_op jit(solution)/shard_map/ppermute | solution.py:427
  50.1 0.8 %shard_map.77 = (bf16[2,256,256]{2,1,0:T(8,128)(2,1)S(1)}, bf16[2,64,1024]{2,1,0:T(8,128)(2,1)S(1)}) custom-call(f32[4,32,128]{2,1,0:T(8,128)S(1)} %tile.12.leaf_ref, f32[2,32,128]{2,1,0:T(8,128)S(1)} %get-tuple-element.83.env_ref, f32[3,32,1024]{2,1,0:T(8,128)S(1)} %get-tuple-element.84.iso_ref, f32[72,128]{1,0:T(8,128)S(1)} %get-tuple-element.92.after_ref.mine_ref), custom_call_target="tpu_custom_call" | custom-call | flops 920000000 | bytes 1024 | tf_op jit(solution)/shard_map/pallas_call | solution.py:155
  51.0 0.9 %shard_map.76 = (bf16[64,1024]{1,0:T(8,128)(2,1)S(1)}, bf16[64,1024]{1,0:T(8,128)(2,1)S(1)}, bf16[256,256]{1,0:T(8,128)(2,1)S(1)}, bf16[64,1024]{1,0:T(8,128)(2,1)S(1)}) custom-call(s32[1]{0:T(128)} %bitcast.7.core_ref.upper_ref, s32[1]{0:T(128)} %bitcast.6.upper_ref, f32[32,512]{1,0:T(8,128)S(1)} %shard_map.75.mine_ref, ...), custom_call_target="tpu_custom_call" | custom-call | flops 1150000 | bytes 1024 | tf_op jit(solution)/shard_map/pallas_call | solution.py:155
  51.9 6.3 %shard_map.79 = (f32[4,1024]{1,0:T(4,128)}, f32[3,1,1024]{2,1,0:T(1,128)}, f32[1,1,1024]{2,1,0:T(1,128)}) custom-call(s32[6]{0:T(128)S(1)} %stack.36.marked_ref, s32[1]{0:T(128)} %bitcast.6.upper_ref, bf16[64,1024]{1,0:T(8,128)(2,1)S(1)} %get-tuple-element.93.natural_ref, bf16[64,1024]{1,0:T(8,128)(2,1)S(1)} %get-tuple-element.94.moved_ref, ...), custom_call_target="tpu_custom_call" | custom-call | flops 8049999872 | bytes 1024 | tf_op jit(solution)/shard_map/pallas_call | solution.py:155
  (59 shorter events, 6.1 us)
Async XLA Ops:
  0.6 0.9 %copy-start = (f32[1,8,1024]{2,1,0:T(8,128)S(1)}, f32[1,8,1024]{2,1,0:T(8,128)}, u32[]{:S(2)}) copy-start(f32[1,8,1024]{2,1,0:T(8,128)} %param.5) | copy-start | bytes 98308
  1.6 4.6 %copy-start.1 = (f32[1,4,1024]{2,1,0:T(4,128)S(1)}, f32[1,4,1024]{2,1,0:T(4,128)}, u32[]{:S(2)}) copy-start(f32[1,4,1024]{2,1,0:T(4,128)} %param.3) | copy-start | bytes 49156
  1.6 6.0 %collective-permute-start = (f32[4,8,1024]{2,1,0:T(8,128)S(1)}, f32[4,8,1024]{2,1,0:T(8,128)S(1)}, u32[]{:S(2)}, u32[]{:S(2)}) collective-permute-start(f32[4,8,1024]{2,1,0:T(8,128)S(1)} %constant_dynamic-update-slice_fusion.refs_0_), channel_id=1, source_target_pairs={{0,2},{1,3},{2,0},{3,1},{4,6},{5,7},{6,4},{7,5},{8,10},{9,11},{10,... | collective-permute-start | bytes 393224 | tf_op jit(solution)/shard_map/ppermute | solution.py:437
  5.2 7.5 %collective-permute-start.1 = (f32[4,8,1024]{2,1,0:T(8,128)S(1)}, f32[4,8,1024]{2,1,0:T(8,128)S(1)}, u32[]{:S(2)}, u32[]{:S(2)}) collective-permute-start(f32[4,8,1024]{2,1,0:T(8,128)S(1)} %constant_dynamic-update-slice_fusion.refs_0_), channel_id=1, source_target_pairs={{0,3},{1,2},{2,1},{3,0},{4,7},{5,6},{6,5},{7,4},{8,11},{9,10},{10,... | collective-permute-start | bytes 393224 | tf_op jit(solution)/shard_map/ppermute | solution.py:437
  6.1 6.7 %collective-permute-start.2 = (f32[4,8,1024]{2,1,0:T(8,128)S(1)}, f32[4,8,1024]{2,1,0:T(8,128)S(1)}, u32[]{:S(2)}, u32[]{:S(2)}) collective-permute-start(f32[4,8,1024]{2,1,0:T(8,128)S(1)} %constant_dynamic-update-slice_fusion.refs_0_), channel_id=1, source_target_pairs={{0,1},{1,0},{2,3},{3,2},{4,5},{5,4},{6,7},{7,6},{8,9},{9,8},{10,11... | collective-permute-start | bytes 393224 | tf_op jit(solution)/shard_map/ppermute | solution.py:437
  12.8 4.5 %collective-permute-start.7 = (f32[16,512]{1,0:T(8,128)S(1)}, f32[16,512]{1,0:T(8,128)S(1)}, u32[]{:S(2)}, u32[]{:S(2)}) collective-permute-start(f32[16,512]{1,0:T(8,128)S(1)} %get-tuple-element.124), channel_id=1, source_target_pairs={{0,4},{4,0},{8,12},{12,8},{16,20},{20,16},{24,28},{28,24},{32,36},... | collective-permute-start | bytes 98312 | tf_op jit(solution)/shard_map/ppermute | solution.py:427
  13.9 3.5 %collective-permute-start.8 = (f32[16,512]{1,0:T(8,128)S(1)}, f32[16,512]{1,0:T(8,128)S(1)}, u32[]{:S(2)}, u32[]{:S(2)}) collective-permute-start(f32[16,512]{1,0:T(8,128)S(1)} %get-tuple-element.123), channel_id=1, source_target_pairs={{0,4},{4,0},{8,12},{12,8},{16,20},{20,16},{24,28},{28,24},{32,36},... | collective-permute-start | bytes 98312 | tf_op jit(solution)/shard_map/ppermute | solution.py:427
  14.0 3.9 %collective-permute-start.3 = (f32[32,512]{1,0:T(8,128)S(1)}, f32[32,512]{1,0:T(8,128)S(1)}, u32[]{:S(2)}, u32[]{:S(2)}) collective-permute-start(f32[32,512]{1,0:T(8,128)S(1)} %get-tuple-element.59.mine_ref), channel_id=1, source_target_pairs={{0,8},{4,12},{8,0},{12,4},{16,24},{20,28},{24,16},{28,20},{32,40},... | collective-permute-start | bytes 196616 | tf_op jit(solution)/shard_map/ppermute | solution.py:427
  16.6 1.6 %collective-permute-start.9 = (f32[72,128]{1,0:T(8,128)S(1)}, f32[72,128]{1,0:T(8,128)S(1)}, u32[]{:S(2)}, u32[]{:S(2)}) collective-permute-start(f32[72,128]{1,0:T(8,128)S(1)} %get-tuple-element.60.after_ref.mine_ref), channel_id=1, source_target_pairs={{0,4},{4,0},{8,12},{12,8},{16,20},{20,16},{24,28},{28,24},{32,36},... | collective-permute-start | bytes 110600 | tf_op jit(solution)/shard_map/ppermute | solution.py:427
  19.1 5.2 %collective-permute-start.10 = (f32[72,128]{1,0:T(8,128)S(1)}, f32[72,128]{1,0:T(8,128)S(1)}, u32[]{:S(2)}, u32[]{:S(2)}) collective-permute-start(f32[72,128]{1,0:T(8,128)S(1)} %get-tuple-element.70.mine_ref), channel_id=1, source_target_pairs={{0,8},{4,12},{8,0},{12,4},{16,24},{20,28},{24,16},{28,20},{32,40},... | collective-permute-start | bytes 110600 | tf_op jit(solution)/shard_map/ppermute | solution.py:427
  20.0 3.7 %collective-permute-start.5 = (f32[16,512]{1,0:T(8,128)S(1)}, f32[16,512]{1,0:T(8,128)S(1)}, u32[]{:S(2)}, u32[]{:S(2)}) collective-permute-start(f32[16,512]{1,0:T(8,128)S(1)} %get-tuple-element.126), channel_id=1, source_target_pairs={{0,4},{4,0},{8,12},{12,8},{16,20},{20,16},{24,28},{28,24},{32,36},... | collective-permute-start | bytes 98312 | tf_op jit(solution)/shard_map/ppermute | solution.py:427
  20.6 3.1 %collective-permute-start.6 = (f32[16,512]{1,0:T(8,128)S(1)}, f32[16,512]{1,0:T(8,128)S(1)}, u32[]{:S(2)}, u32[]{:S(2)}) collective-permute-start(f32[16,512]{1,0:T(8,128)S(1)} %get-tuple-element.125), channel_id=1, source_target_pairs={{0,4},{4,0},{8,12},{12,8},{16,20},{20,16},{24,28},{28,24},{32,36},... | collective-permute-start | bytes 98312 | tf_op jit(solution)/shard_map/ppermute | solution.py:427
  20.7 6.6 %collective-permute-start.4 = (f32[32,512]{1,0:T(8,128)S(1)}, f32[32,512]{1,0:T(8,128)S(1)}, u32[]{:S(2)}, u32[]{:S(2)}) collective-permute-start(f32[32,512]{1,0:T(8,128)S(1)} %get-tuple-element.61.mine_ref), channel_id=1, source_target_pairs={{0,16},{4,20},{8,24},{12,28},{16,0},{20,4},{24,8},{28,12},{32,48},... | collective-permute-start | bytes 196616 | tf_op jit(solution)/shard_map/ppermute | solution.py:427
  25.1 7.1 %collective-permute-start.14 = (f32[72,128]{1,0:T(8,128)S(1)}, f32[72,128]{1,0:T(8,128)S(1)}, u32[]{:S(2)}, u32[]{:S(2)}) collective-permute-start(f32[72,128]{1,0:T(8,128)S(1)} %get-tuple-element.71.after_ref.mine_ref), channel_id=1, source_target_pairs={{0,16},{4,20},{8,24},{12,28},{16,0},{20,4},{24,8},{28,12},{32,48},... | collective-permute-start | bytes 110600 | tf_op jit(solution)/shard_map/ppermute | solution.py:427
  27.4 4.3 %collective-permute-start.12 = (f32[16,512]{1,0:T(8,128)S(1)}, f32[16,512]{1,0:T(8,128)S(1)}, u32[]{:S(2)}, u32[]{:S(2)}) collective-permute-start(f32[16,512]{1,0:T(8,128)S(1)} %get-tuple-element.122), channel_id=1, source_target_pairs={{0,4},{4,0},{8,12},{12,8},{16,20},{20,16},{24,28},{28,24},{32,36},... | collective-permute-start | bytes 98312 | tf_op jit(solution)/shard_map/ppermute | solution.py:427
  28.3 3.4 %collective-permute-start.13 = (f32[16,512]{1,0:T(8,128)S(1)}, f32[16,512]{1,0:T(8,128)S(1)}, u32[]{:S(2)}, u32[]{:S(2)}) collective-permute-start(f32[16,512]{1,0:T(8,128)S(1)} %get-tuple-element.121), channel_id=1, source_target_pairs={{0,4},{4,0},{8,12},{12,8},{16,20},{20,16},{24,28},{28,24},{32,36},... | collective-permute-start | bytes 98312 | tf_op jit(solution)/shard_map/ppermute | solution.py:427
  28.4 5.9 %collective-permute-start.11 = (f32[32,512]{1,0:T(8,128)S(1)}, f32[32,512]{1,0:T(8,128)S(1)}, u32[]{:S(2)}, u32[]{:S(2)}) collective-permute-start(f32[32,512]{1,0:T(8,128)S(1)} %get-tuple-element.72.mine_ref), channel_id=1, source_target_pairs={{0,48},{4,52},{8,56},{12,60},{16,32},{20,36},{24,40},{28,44},{32,1... | collective-permute-start | bytes 196616 | tf_op jit(solution)/shard_map/ppermute | solution.py:427
  33.0 5.8 %collective-permute-start.18 = (f32[72,128]{1,0:T(8,128)S(1)}, f32[72,128]{1,0:T(8,128)S(1)}, u32[]{:S(2)}, u32[]{:S(2)}) collective-permute-start(f32[72,128]{1,0:T(8,128)S(1)} %get-tuple-element.77.after_ref.mine_ref), channel_id=1, source_target_pairs={{0,48},{4,52},{8,56},{12,60},{16,32},{20,36},{24,40},{28,44},{32,1... | collective-permute-start | bytes 110600 | tf_op jit(solution)/shard_map/ppermute | solution.py:427
  34.4 3.9 %collective-permute-start.16 = (f32[16,512]{1,0:T(8,128)S(1)}, f32[16,512]{1,0:T(8,128)S(1)}, u32[]{:S(2)}, u32[]{:S(2)}) collective-permute-start(f32[16,512]{1,0:T(8,128)S(1)} %get-tuple-element.120), channel_id=1, source_target_pairs={{0,4},{4,0},{8,12},{12,8},{16,20},{20,16},{24,28},{28,24},{32,36},... | collective-permute-start | bytes 98312 | tf_op jit(solution)/shard_map/ppermute | solution.py:427
  35.9 2.3 %collective-permute-start.17 = (f32[16,512]{1,0:T(8,128)S(1)}, f32[16,512]{1,0:T(8,128)S(1)}, u32[]{:S(2)}, u32[]{:S(2)}) collective-permute-start(f32[16,512]{1,0:T(8,128)S(1)} %get-tuple-element.119), channel_id=1, source_target_pairs={{0,4},{4,0},{8,12},{12,8},{16,20},{20,16},{24,28},{28,24},{32,36},... | collective-permute-start | bytes 98312 | tf_op jit(solution)/shard_map/ppermute | solution.py:427
  36.9 3.4 %collective-permute-start.15 = (f32[32,512]{1,0:T(8,128)S(1)}, f32[32,512]{1,0:T(8,128)S(1)}, u32[]{:S(2)}, u32[]{:S(2)}) collective-permute-start(f32[32,512]{1,0:T(8,128)S(1)} %get-tuple-element.78.mine_ref), channel_id=1, source_target_pairs={{0,64},{4,68},{8,72},{12,76},{16,80},{20,84},{24,88},{28,92},{32,9... | collective-permute-start | bytes 196616 | tf_op jit(solution)/shard_map/ppermute | solution.py:427
  39.7 6.0 %collective-permute-start.22 = (f32[72,128]{1,0:T(8,128)S(1)}, f32[72,128]{1,0:T(8,128)S(1)}, u32[]{:S(2)}, u32[]{:S(2)}) collective-permute-start(f32[72,128]{1,0:T(8,128)S(1)} %get-tuple-element.86.after_ref.mine_ref), channel_id=1, source_target_pairs={{0,64},{4,68},{8,72},{12,76},{16,80},{20,84},{24,88},{28,92},{32,9... | collective-permute-start | bytes 110600 | tf_op jit(solution)/shard_map/ppermute | solution.py:427
  40.6 4.5 %collective-permute-start.20 = (f32[16,512]{1,0:T(8,128)S(1)}, f32[16,512]{1,0:T(8,128)S(1)}, u32[]{:S(2)}, u32[]{:S(2)}) collective-permute-start(f32[16,512]{1,0:T(8,128)S(1)} %get-tuple-element.118), channel_id=1, source_target_pairs={{0,4},{4,0},{8,12},{12,8},{16,20},{20,16},{24,28},{28,24},{32,36},... | collective-permute-start | bytes 98312 | tf_op jit(solution)/shard_map/ppermute | solution.py:427
  42.9 2.2 %collective-permute-start.21 = (f32[16,512]{1,0:T(8,128)S(1)}, f32[16,512]{1,0:T(8,128)S(1)}, u32[]{:S(2)}, u32[]{:S(2)}) collective-permute-start(f32[16,512]{1,0:T(8,128)S(1)} %get-tuple-element.117), channel_id=1, source_target_pairs={{0,4},{4,0},{8,12},{12,8},{16,20},{20,16},{24,28},{28,24},{32,36},... | collective-permute-start | bytes 98312 | tf_op jit(solution)/shard_map/ppermute | solution.py:427
  43.1 5.4 %collective-permute-start.19 = (f32[32,256]{1,0:T(8,128)S(1)}, f32[32,256]{1,0:T(8,128)S(1)}, u32[]{:S(2)}, u32[]{:S(2)}) collective-permute-start(f32[32,256]{1,0:T(8,128)S(1)} %get-tuple-element.87.mine_ref), channel_id=1, source_target_pairs={{0,192},{4,196},{8,200},{12,204},{16,208},{20,212},{24,216},{28,22... | collective-permute-start | bytes 98312 | tf_op jit(solution)/shard_map/ppermute | solution.py:427
  47.5 4.4 %collective-permute-start.25 = (f32[72,128]{1,0:T(8,128)S(1)}, f32[72,128]{1,0:T(8,128)S(1)}, u32[]{:S(2)}, u32[]{:S(2)}) collective-permute-start(f32[72,128]{1,0:T(8,128)S(1)} %get-tuple-element.92.after_ref.mine_ref), channel_id=1, source_target_pairs={{0,192},{4,196},{8,200},{12,204},{16,208},{20,212},{24,216},{28,22... | collective-permute-start | bytes 110600 | tf_op jit(solution)/shard_map/ppermute | solution.py:427
  48.5 2.4 %collective-permute-start.23 = (f32[16,512]{1,0:T(8,128)S(1)}, f32[16,512]{1,0:T(8,128)S(1)}, u32[]{:S(2)}, u32[]{:S(2)}) collective-permute-start(f32[16,512]{1,0:T(8,128)S(1)} %get-tuple-element.116), channel_id=1, source_target_pairs={{0,4},{4,0},{8,12},{12,8},{16,20},{20,16},{24,28},{28,24},{32,36},... | collective-permute-start | bytes 98312 | tf_op jit(solution)/shard_map/ppermute | solution.py:427
  49.8 1.2 %collective-permute-start.24 = (f32[16,512]{1,0:T(8,128)S(1)}, f32[16,512]{1,0:T(8,128)S(1)}, u32[]{:S(2)}, u32[]{:S(2)}) collective-permute-start(f32[16,512]{1,0:T(8,128)S(1)} %get-tuple-element.115), channel_id=1, source_target_pairs={{0,4},{4,0},{8,12},{12,8},{16,20},{20,16},{24,28},{28,24},{32,36},... | collective-permute-start | bytes 98312 | tf_op jit(solution)/shard_map/ppermute | solution.py:427
